TPU v7x, 128 devices: a whole 4x4x4 slice. The times are simulated.
128 devices in a mesh: section: 4 (over x), dp: 16 (over z, y), tensor: 2 (over core).
Axes of the slice: x: 4, y: 4, z: 4, core: 2. Of those that a mesh axis runs over, the one named last changes fastest.
Arguments:
- carried: bfloat16 [4, 4096, 8192], P('section', 'dp', 'tensor'), may hold values from -448 to 448
- norm_gain: float32 [4, 8192], P('section'), may hold values from 0.5 to 1.5
- frozen_key_matrix: bfloat16 [4, 8192, 1024], P('section', None, 'tensor'), may hold values from -0.044194174 to 0.044194174
- frozen_value_matrix: bfloat16 [4, 8192, 1024], P('section', None, 'tensor'), may hold values from -0.044194174 to 0.044194174
- adapter_params: float32 [4, 2, 8192, 256], P('section', None, ('dp', 'tensor')), may hold values from -0.08 to 0.08
- adapter_second: float32 [4, 8192, 256], P('section', ('dp', 'tensor')), may hold values from 0.003 to 0.03
- right_params: float32 [4, 2, 128, 2, 1024], P('section', None, 'dp', None, 'tensor'), may hold values from -0.2 to 0.2
- right_second: float32 [4, 128, 2, 1024], P('section', 'dp', None, 'tensor'), may hold values from 0.003 to 0.03
- row_jobs: int32 [4, 4096], P('section', 'dp'), may hold values from 0 to 7
- job_tokens: int32 [8], replicated, may hold values from 512 to 1023
- finishing: int32 [4], P('section'), may hold values from 0 to 7
- cotangent: bfloat16 [4, 4096, 2, 1024], P('section', 'dp', None, 'tensor'), may hold values from -6 to 6
Outputs:
- kv_out: bfloat16 [4, 4096, 2, 1024], P('section', 'dp', None, 'tensor')
- input_grad: bfloat16 [4, 4096, 8192], P('section', 'dp', 'tensor')
- new_adapter: float32 [4, 3, 8192, 256], P('section', None, ('dp', 'tensor'))
- new_right: float32 [4, 3, 128, 2, 1024], P('section', None, 'dp', None, 'tensor')
- checkpoint: float32 [4, 3, 32, 8192], P('section', None, None, 'dp')
All inputs are finite; a program needn't handle non-finite values.
Results may differ from a plain program's by a relative error of at most 0.011.
Values may be sent and summed in bfloat16 or wider, within the bound.
No kernel may reach another device: no remote copies, remote signals or barrier semaphores. Data moves between devices by JAX's collectives and lax.ppermute only.
A program may use at most 192 MiB of HBM per device.

v0:
```python
import jax
import jax.numpy as jnp
from jax import lax
from jax.experimental import pallas as pl
from jax.experimental.pallas import tpu as pltpu
from jax.sharding import PartitionSpec as P

JOBS = 8
RANK = 16
ADAM_STEP = 10
ADAPTER_SCALING = 2.0
BETA_ONE = 0.9
BETA_TWO = 0.999
ADAM_EPS = 1e-08
LEARN_RATE = 0.01

FEATURE_WIDTH = JOBS * RANK
COLUMNS = 2 * FEATURE_WIDTH
STEP = 1024
SIDE = 4
VMEM_LIMIT = 54 * 1024 * 1024
HINT = 16

F32 = jnp.float32
BF16 = jnp.bfloat16


def shifted(value, axis, steps):
    count = lax.axis_size(axis)
    pairs = [(source, (source + steps) % count) for source in range(count)]
    return lax.ppermute(value, axis, pairs)


def swapped(value):
    return shifted(value, "tensor", 1)


def after(value, *others):
    return lax.optimization_barrier((value,) + others)[0]


def shifted_y(value, steps):
    pairs = [
        (z * SIDE + y, z * SIDE + (y + steps) % SIDE) for z in range(SIDE) for y in range(SIDE)
    ]
    return lax.ppermute(value, "dp", pairs)


def shifted_z(value, steps):
    pairs = [
        (z * SIDE + y, (z + steps) % SIDE * SIDE + y) for z in range(SIDE) for y in range(SIDE)
    ]
    return lax.ppermute(value, "dp", pairs)


def adam_update(param, first, second, grad):
    first = BETA_ONE * first + (1.0 - BETA_ONE) * grad
    second = BETA_TWO * second + (1.0 - BETA_TWO) * grad * grad
    first_fix = 1.0 - BETA_ONE**ADAM_STEP
    second_fix = 1.0 - BETA_TWO**ADAM_STEP
    param = param - LEARN_RATE * (first / first_fix) / (jnp.sqrt(second / second_fix) + ADAM_EPS)
    return param, first, second


def rows_dot(left, right):
    return lax.dot_general(left, right, (((0,), (0,)), ((), ())), preferred_element_type=F32)


def columns_dot(left, right):
    return lax.dot_general(left, right, (((1,), (1,)), ((), ())), preferred_element_type=F32)


def dot(left, right):
    return jnp.dot(left, right, preferred_element_type=F32)


def whole(shape):
    return pl.BlockSpec(shape, lambda i, core: (0,) * len(shape))


HBM = pl.BlockSpec(memory_space=pl.ANY)


def call(body, core, args, streamed, out_shape, flops, scratch=(), streamed_outs=()):
    outs = jax.tree.leaves(out_shape)
    moved = sum(a.size * a.dtype.itemsize for a in outs + list(args))
    out_specs = [
        HBM if index in streamed_outs else whole(out.shape) for index, out in enumerate(outs)
    ]
    single = not isinstance(out_shape, list)
    return pl.pallas_call(
        body,
        out_shape=out_shape,
        grid_spec=pltpu.PrefetchScalarGridSpec(
            num_scalar_prefetch=1,
            grid=(1,),
            in_specs=[
                HBM if index in streamed else whole(arg.shape) for index, arg in enumerate(args)
            ],
            out_specs=out_specs[0] if single else out_specs,
            scratch_shapes=list(scratch),
        ),
        compiler_params=pltpu.CompilerParams(vmem_limit_bytes=VMEM_LIMIT),
        cost_estimate=pl.CostEstimate(
            flops=flops // HINT, bytes_accessed=moved // HINT, transcendentals=0
        ),
    )(core, *args)


def started(pairs, sems):
    copies = [
        pltpu.make_async_copy(source, target, sems.at[index])
        for index, (source, target) in enumerate(pairs)
    ]
    for copy in copies:
        copy.start()
    return copies


def lanes_of(index, size=STEP):
    return pl.ds(index * size, size)


def frozen_back(core, cot, key_matrix, value_matrix, half, received=None, gain=None):
    tokens, kv = cot.shape[0], cot.shape[1] // 2
    steps = half // STEP
    own = received is not None

    def body(core_ref, cot_ref, key_ref, value_ref, *rest):
        if own:
            received_ref, gain_ref, *rest = rest
        out_ref, keys, values, out, key_sems, value_sems, out_sems, *rest = rest
        side = core_ref[0] if own else 1 - core_ref[0]
        base = pl.multiple_of(side * half, half)
        rows = [pl.ds(base + i * STEP, STEP) for i in range(steps)]
        copies = []
        for i in range(steps):
            pairs = [
                (key_ref.at[rows[i]], keys.at[lanes_of(i)], key_sems.at[i]),
                (value_ref.at[rows[i]], values.at[lanes_of(i)], value_sems.at[i]),
            ]
            if own:
                arrived, arrived_sems = rest
                pairs.append(
                    (
                        received_ref.at[:, lanes_of(i)],
                        arrived.at[:, lanes_of(i)],
                        arrived_sems.at[i],
                    )
                )
            copies.append([pltpu.make_async_copy(*pair) for pair in pairs])
            for copy in copies[i]:
                copy.start()
        leaving = []
        for i in range(steps):
            for copy in copies[i]:
                copy.wait()
            total = columns_dot(cot_ref[:, :kv], keys[lanes_of(i)])
            total += columns_dot(cot_ref[:, kv:], values[lanes_of(i)])
            if own:
                total = (total + arrived[:, lanes_of(i)].astype(F32)) * gain_ref[:, rows[i]]
            out[:, lanes_of(i)] = total.astype(BF16)
            leaving.append(
                pltpu.make_async_copy(
                    out.at[:, lanes_of(i)], out_ref.at[:, lanes_of(i)], out_sems.at[i]
                )
            )
            leaving[i].start()
        for copy in leaving:
            copy.wait()

    sems = pltpu.SemaphoreType.DMA((steps,))
    args = [cot, key_matrix, value_matrix]
    scratch = [
        pltpu.VMEM((half, kv), BF16),
        pltpu.VMEM((half, kv), BF16),
        pltpu.VMEM((tokens, half), BF16),
        sems,
        sems,
        sems,
    ]
    if own:
        args += [received, gain]
        scratch += [pltpu.VMEM((tokens, half), BF16), sems]
    return call(
        body,
        core,
        args,
        (1, 2, 3),
        jax.ShapeDtypeStruct((tokens, half), BF16),
        4 * tokens * half * kv,
        scratch,
        (0,),
    )


def normed_by_parity(core, x, rstd, gain, block):
    tokens, half = x.shape
    steps = half // STEP
    pairs = STEP // (2 * block)
    part = pairs * block

    def body(core_ref, x_ref, rstd_ref, gain_ref, kept_ref, given_ref, xs, kept, given, *sems):
        x_sems, kept_sems, given_sems = sems
        base = pl.multiple_of(core_ref[0] * half, half)
        copies = started(
            [(x_ref.at[:, lanes_of(i)], xs.at[:, lanes_of(i)]) for i in range(steps)], x_sems
        )
        rstd = rstd_ref[...]
        leaving = []
        for i in range(steps):
            copies[i].wait()
            for pair in range(pairs):
                for side in range(2):
                    start = i * STEP + (2 * pair + side) * block
                    normed = xs[:, start : start + block].astype(F32) * rstd
                    normed = (normed * gain_ref[:, pl.ds(base + start, block)]).astype(BF16)
                    out = lanes_of(i * pairs + pair, block)

                    @pl.when(core_ref[0] == side)
                    def _():
                        kept[:, out] = normed

                    @pl.when(core_ref[0] != side)
                    def _():
                        given[:, out] = normed

            for buffer, ref, out_sems in (
                (given, given_ref, given_sems),
                (kept, kept_ref, kept_sems),
            ):
                leaving.append(
                    pltpu.make_async_copy(
                        buffer.at[:, lanes_of(i, part)],
                        ref.at[:, lanes_of(i, part)],
                        out_sems.at[i],
                    )
                )
                leaving[-1].start()
        for copy in leaving:
            copy.wait()

    shape = jax.ShapeDtypeStruct((tokens, half // 2), BF16)
    sems = pltpu.SemaphoreType.DMA((steps,))
    return call(
        body,
        core,
        [x, rstd, gain],
        (0,),
        [shape, shape],
        tokens * half,
        [
            pltpu.VMEM((tokens, half), BF16),
            pltpu.VMEM((tokens, half // 2), BF16),
            pltpu.VMEM((tokens, half // 2), BF16),
            sems,
            sems,
            sems,
        ],
        (0, 1),
    )


def down_gradient(core, kept, taken, back, block):
    tokens, width = kept.shape
    count = width // block
    group = 4
    steps = count // group

    def body(core_ref, kept_ref, taken_ref, back_ref, out_ref, normed, out, in_sems, out_sems):
        copies = started(
            [(kept_ref, normed.at[0]), (taken_ref, normed.at[1])],
            in_sems,
        )
        turned = (ADAPTER_SCALING * back_ref[...].astype(F32)).T.astype(BF16)
        leaving = []
        for side in range(2):
            copies[side].wait()
            owner = core_ref[0] if side == 0 else 1 - core_ref[0]
            for step in range(steps):
                for index in range(step * group, (step + 1) * group):
                    piece = dot(turned, normed[side, :, index * block : (index + 1) * block])
                    out[side * count + index] = piece.astype(BF16)
                copy = pltpu.make_async_copy(
                    out.at[pl.ds(side * count + step * group, group)],
                    out_ref.at[pl.ds(owner * count + step * group, group)],
                    out_sems.at[side * steps + step],
                )
                copy.start()
                leaving.append(copy)
        for copy in leaving:
            copy.wait()

    return call(
        body,
        core,
        [kept, taken, back],
        (0, 1),
        jax.ShapeDtypeStruct((2 * count, COLUMNS, block), BF16),
        4 * tokens * width * COLUMNS,
        [
            pltpu.VMEM((2, tokens, width), BF16),
            pltpu.VMEM((2 * count, COLUMNS, block), BF16),
            pltpu.SemaphoreType.DMA((2,)),
            pltpu.SemaphoreType.DMA((2 * steps,)),
        ],
        (0,),
    )


def projected(core, x, x_other, rstd, gain, key_matrix, value_matrix, cot):
    tokens, half = x.shape
    kv = key_matrix.shape[1]
    steps = half // STEP

    def body(core_ref, x_ref, other_ref, rstd_ref, gain_ref, key_ref, value_ref, cot_ref, *rest):
        out_ref, sum_ref, xs, keys, values, x_sems, key_sems, value_sems = rest
        rows, copies = [], []
        for side, ref in enumerate((x_ref, other_ref)):
            base = core_ref[0] if side == 0 else 1 - core_ref[0]
            for i in range(steps):
                at = side * steps + i
                rows.append(pl.ds(pl.multiple_of(base * half + i * STEP, STEP), STEP))
                sources = [
                    (ref.at[:, lanes_of(i)], xs.at[:, lanes_of(at)], x_sems),
                    (key_ref.at[rows[at]], keys.at[lanes_of(at)], key_sems),
                    (value_ref.at[rows[at]], values.at[lanes_of(at)], value_sems),
                ]
                copies.append(
                    [pltpu.make_async_copy(a, b, sems.at[at]) for a, b, sems in sources]
                )
                for copy in copies[at]:
                    copy.start()
        rstd = rstd_ref[...]
        for at in range(2 * steps):
            for copy in copies[at]:
                copy.wait()
            normed = xs[:, lanes_of(at)].astype(F32) * rstd * gain_ref[:, rows[at]]
            normed = normed.astype(BF16)
            for lanes, matrix in ((slice(0, kv), keys), (slice(kv, 2 * kv), values)):
                product = dot(normed, matrix[lanes_of(at)])
                if at == 0:
                    out_ref[:, lanes] = product
                else:
                    out_ref[:, lanes] += product
        sum_ref[...] = jnp.sum(out_ref[...] * cot_ref[...].astype(F32), axis=1, keepdims=True)

    sems = pltpu.SemaphoreType.DMA((2 * steps,))
    return call(
        body,
        core,
        [x, x_other, rstd, gain, key_matrix, value_matrix, cot],
        (0, 1, 4, 5),
        [
            jax.ShapeDtypeStruct((tokens, 2 * kv), F32),
            jax.ShapeDtypeStruct((tokens, 1), F32),
        ],
        8 * tokens * half * kv,
        [
            pltpu.VMEM((tokens, 2 * half), BF16),
            pltpu.VMEM((2 * half, kv), BF16),
            pltpu.VMEM((2 * half, kv), BF16),
            sems,
            sems,
            sems,
        ],
    )


def low_rank_down(core, x, rstd, gain, factors):
    tokens, half = x.shape
    steps = half // STEP

    def body(core_ref, x_ref, rstd_ref, gain_ref, factors_ref, out_ref, xs, ours, x_sems, sems):
        base = pl.multiple_of(core_ref[0] * half, half)
        copies = []
        for i in range(steps):
            copies.append(
                [
                    pltpu.make_async_copy(
                        x_ref.at[:, lanes_of(i)], xs.at[:, lanes_of(i)], x_sems.at[i]
                    ),
                    pltpu.make_async_copy(
                        factors_ref.at[pl.ds(base + i * STEP, STEP), :COLUMNS],
                        ours.at[lanes_of(i)],
                        sems.at[i],
                    ),
                ]
            )
            for copy in copies[i]:
                copy.start()
        rstd = rstd_ref[...]
        for i in range(steps):
            for copy in copies[i]:
                copy.wait()
            normed = xs[:, lanes_of(i)].astype(F32) * rstd
            normed = (normed * gain_ref[:, pl.ds(base + i * STEP, STEP)]).astype(BF16)
            product = dot(normed, ours[lanes_of(i)])
            if i == 0:
                out_ref[...] = product
            else:
                out_ref[...] += product

    sems = pltpu.SemaphoreType.DMA((steps,))
    return call(
        body,
        core,
        [x, rstd, gain, factors],
        (0, 3),
        jax.ShapeDtypeStruct((tokens, COLUMNS), F32),
        2 * tokens * half * COLUMNS,
        [
            pltpu.VMEM((tokens, half), BF16),
            pltpu.VMEM((half, COLUMNS), BF16),
            sems,
            sems,
        ],
    )


def masked(value, jobs):
    column = lax.broadcasted_iota(jnp.int32, value.shape, 1)
    return jnp.where(jobs == (column & (FEATURE_WIDTH - 1)) // RANK, value, 0.0)


def back_product(scalars, cot, ups):
    tokens, kv = cot.shape[0], cot.shape[1] // 2
    rows = ups[0].shape[1]

    def body(scalars_ref, cot_ref, *rest):
        up_refs, (out_ref, up_ref, ordered) = rest[:SIDE], rest[SIDE:]
        for down, ref in enumerate(up_refs):
            z = lax.rem(scalars_ref[1] + SIDE - down, SIDE)
            for left in range(SIDE):
                y = lax.rem(scalars_ref[2] + SIDE - left, SIDE)
                start = pl.multiple_of((z * SIDE + y) * rows, rows)
                ordered[pl.ds(start, rows), :] = ref[left].astype(F32)
        up_ref[...] = ordered[...].astype(BF16)
        for side in range(2):
            lanes = pl.ds(side * kv, kv)
            picked = columns_dot(cot_ref[:, lanes], up_ref[:, lanes])
            out_ref[:, side * FEATURE_WIDTH : (side + 1) * FEATURE_WIDTH] = picked

    return call(
        body,
        scalars,
        [cot, *ups],
        (),
        [
            jax.ShapeDtypeStruct((tokens, COLUMNS), F32),
            jax.ShapeDtypeStruct((FEATURE_WIDTH, 2 * kv), BF16),
        ],
        4 * tokens * kv * FEATURE_WIDTH,
        [pltpu.VMEM((FEATURE_WIDTH, 2 * kv), F32)],
    )


def up_gradient(core, mine, other, jobs, cot, back):
    tokens, kv = cot.shape[0], cot.shape[1] // 2

    def body(core_ref, mine_ref, other_ref, jobs_ref, cot_ref, back_ref, *outs):
        low_ref, out_ref, sum_ref = outs
        total = masked(mine_ref[...] + other_ref[...], jobs_ref[...])
        sum_ref[...] = ADAPTER_SCALING * jnp.sum(
            total * back_ref[...].astype(F32), axis=1, keepdims=True
        )
        low = total.astype(BF16)
        low_ref[...] = low
        for side in range(2):
            lanes = lanes_of(side, kv)
            picked = low[:, side * FEATURE_WIDTH : (side + 1) * FEATURE_WIDTH]
            out_ref[:, lanes] = (ADAPTER_SCALING * rows_dot(picked, cot_ref[:, lanes])).astype(BF16)

    return call(
        body,
        core,
        [mine, other, jobs, cot, back],
        (),
        [
            jax.ShapeDtypeStruct((tokens, COLUMNS), BF16),
            jax.ShapeDtypeStruct((FEATURE_WIDTH, 2 * kv), BF16),
            jax.ShapeDtypeStruct((tokens, 1), F32),
        ],
        4 * tokens * kv * FEATURE_WIDTH,
    )


def with_low_rank(core, frozen, low, up):
    tokens, kv = frozen.shape[0], frozen.shape[1] // 2

    def body(core_ref, frozen_ref, low_ref, up_ref, out_ref):
        for side in range(2):
            lanes = lanes_of(side, kv)
            picked = low_ref[:, side * FEATURE_WIDTH : (side + 1) * FEATURE_WIDTH]
            total = frozen_ref[:, lanes] + ADAPTER_SCALING * dot(picked, up_ref[:, lanes])
            out_ref[:, lanes] = total.astype(BF16)

    return call(
        body,
        core,
        [frozen, low, up],
        (),
        jax.ShapeDtypeStruct(frozen.shape, BF16),
        4 * tokens * kv * FEATURE_WIDTH,
    )


def norm_backward(core, scaled, back, factors, gain, x, rstd, mean):
    tokens, half = x.shape
    steps = half // STEP

    def body(core_ref, scaled_ref, back_ref, factors_ref, gain_ref, x_ref, *rest):
        rstd_ref, mean_ref, out_ref, ins, ours, xs, out, in_sems, sems, x_sems, out_sems = rest
        base = pl.multiple_of(core_ref[0] * half, half)
        rows = [pl.ds(base + i * STEP, STEP) for i in range(steps)]
        copies = []
        for i in range(steps):
            lanes = lanes_of(i)
            sources = [
                (factors_ref.at[rows[i], COLUMNS:], ours.at[lanes], sems),
                (x_ref.at[:, lanes], xs.at[:, lanes], x_sems),
                (scaled_ref.at[:, lanes], ins.at[:, lanes], in_sems),
            ]
            copies.append([pltpu.make_async_copy(a, b, c.at[i]) for a, b, c in sources])
            for copy in copies[i]:
                copy.start()
        back = back_ref[...]
        rstd = rstd_ref[...]
        shift = rstd * rstd * mean_ref[...]
        leaving = []
        for i in range(steps):
            lanes = lanes_of(i)
            for copy in copies[i]:
                copy.wait()
            low = columns_dot(back, ours[lanes])
            total = ins[:, lanes].astype(F32) + (ADAPTER_SCALING * gain_ref[:, rows[i]]) * low
            out[:, lanes] = (rstd * total - xs[:, lanes].astype(F32) * shift).astype(BF16)
            leaving.append(
                pltpu.make_async_copy(out.at[:, lanes], out_ref.at[:, lanes], out_sems.at[i])
            )
            leaving[i].start()
        for copy in leaving:
            copy.wait()

    sems = pltpu.SemaphoreType.DMA((steps,))
    strip = pltpu.VMEM((tokens, half), BF16)
    return call(
        body,
        core,
        [scaled, back, factors, gain, x, rstd, mean],
        (0, 2, 4),
        jax.ShapeDtypeStruct((tokens, half), BF16),
        2 * tokens * half * COLUMNS,
        [strip, pltpu.VMEM((half, COLUMNS), BF16), strip, strip, sems, sems, sems, sems],
        (0,),
    )


def summed(core, pieces):
    count, rows, columns = pieces.shape
    steps = 4
    part = rows // steps

    def body(core_ref, pieces_ref, out_ref, held, sems):
        copies = started(
            [
                (pieces_ref.at[:, lanes_of(i, part)], held.at[:, lanes_of(i, part)])
                for i in range(steps)
            ],
            sems,
        )
        for i in range(steps):
            copies[i].wait()
            total = jnp.sum(held[:, lanes_of(i, part)].astype(F32), axis=0)
            out_ref[lanes_of(i, part)] = total.astype(BF16)

    return call(
        body,
        core,
        [pieces],
        (0,),
        jax.ShapeDtypeStruct((rows, columns), BF16),
        pieces.size,
        [pltpu.VMEM(pieces.shape, BF16), pltpu.SemaphoreType.DMA((steps,))],
    )


def down_optimizer(scalars, params, second, grad, totals):
    rows, columns = grad.shape

    def body(scalars_ref, params_ref, second_ref, grad_ref, totals_ref, new_ref, chosen_ref, turned):
        grad = grad_ref[...].astype(F32).T / totals_ref[...]
        new = adam_update(params_ref[0], params_ref[1], second_ref[...], grad)
        job = pl.multiple_of(scalars_ref[1] * RANK, RANK)
        for index, value in enumerate(new):
            new_ref[index] = value
            turned[...] = value.T
            for side in range(2):
                picked = turned[pl.ds(side * FEATURE_WIDTH + job, RANK), :]
                chosen_ref[index, side * RANK : (side + 1) * RANK] = picked

    return call(
        body,
        scalars,
        [params, second, grad, totals],
        (),
        [
            jax.ShapeDtypeStruct((3, rows, columns), F32),
            jax.ShapeDtypeStruct((3, 2 * RANK, rows), F32),
        ],
        20 * rows * columns,
        [pltpu.VMEM((columns, rows), F32)],
    )


def local(
    carried,
    norm_gain,
    frozen_key_matrix,
    frozen_value_matrix,
    adapter_params,
    adapter_second,
    right_params,
    right_second,
    row_jobs,
    job_tokens,
    finishing,
    cotangent,
):
    n_data = lax.axis_size("dp")
    core_index = lax.axis_index("tensor")
    core = core_index[None].astype(jnp.int32)
    place = lax.axis_index("dp")
    x_here = carried[0]
    tokens, half = x_here.shape
    width = 2 * half
    block = adapter_params.shape[2]
    kv = frozen_key_matrix.shape[2]
    gain = norm_gain
    key_matrix, value_matrix = frozen_key_matrix[0], frozen_value_matrix[0]
    cot = cotangent[0].reshape(tokens, 2 * kv)
    jobs = row_jobs[0][:, None]

    factors = adapter_params[0, 0].astype(BF16)
    factors_next = shifted(factors, "section", -1)
    x_in = shifted(x_here, "section", 1)
    gain_next = shifted(gain, "section", -1)
    both = lax.all_gather(
        jnp.concatenate([factors, factors_next], axis=1), ("dp", "tensor"), axis=0, tiled=True
    )

    up_here = right_params[0, 0].astype(BF16).reshape(-1, 2 * kv)
    rows_local = up_here.shape[0]
    up_row = jnp.stack([up_here] + [shifted_y(up_here, step) for step in range(1, SIDE)])
    ups = [up_row] + [shifted_z(up_row, step) for step in range(1, SIDE)]
    spot = jnp.stack([core_index, place // SIDE, place % SIDE]).astype(jnp.int32)

    leaving = frozen_back(after(core, up_row), cot, key_matrix, value_matrix, half)
    received = swapped(leaving)

    back_part, up = back_product(after(spot, leaving), cot, ups)
    back = masked(back_part + swapped(back_part), jobs).astype(BF16)
    back_next = shifted(back, "section", -1)

    scaled = frozen_back(
        after(core, back), cot, key_matrix, value_matrix, half, received, gain
    )
    scaled_next = shifted(scaled, "section", -1)

    x_wide = x_here.astype(F32)
    squares = jnp.sum(x_wide * x_wide, axis=1, keepdims=True)
    rstd = lax.rsqrt((squares + swapped(squares)) / width + 1e-05)
    rstd_in = shifted(rstd, "section", 1)
    kept, given = normed_by_parity(after(core, scaled), x_here, rstd, gain_next, block)
    down_piece = down_gradient(core, kept, swapped(given), back_next, block)
    down_pieces = lax.all_to_all(down_piece, "dp", 0, 0, tiled=True)

    x_in = after(x_in, down_piece)
    frozen, products = projected(
        core, x_in, swapped(x_in), rstd_in, gain, key_matrix, value_matrix, cot
    )
    low_part = low_rank_down(after(core, frozen), x_in, rstd_in, gain, both)
    low, up_piece, low_products = up_gradient(
        core, low_part, swapped(low_part), jobs, cot, back
    )
    up_pieces = up_piece.reshape(n_data, rows_local, 2 * kv)
    up_pieces = lax.all_to_all(up_pieces, "dp", 0, 0, tiled=True)
    mean = shifted((products + swapped(products) + low_products) / width, "section", -1)
    down_sum = summed(after(core, up_piece), down_pieces)
    kv_out = with_low_rank(after(core, down_sum), frozen, low, up)
    down_sum = shifted(down_sum, "section", 1)

    input_grad = norm_backward(
        after(core, kv_out), scaled_next, back_next, both, gain_next, x_here, rstd, mean
    )
    kv_out = kv_out.reshape(1, tokens, 2, kv)
    up_sum = jnp.sum(up_pieces.astype(F32), axis=0).reshape(rows_local, 2, kv)

    job_ids = jnp.arange(JOBS, dtype=jnp.int32)
    counts = job_tokens.astype(F32)
    col_job = jnp.arange(COLUMNS, dtype=jnp.int32) % FEATURE_WIDTH // RANK
    column_total = jnp.sum(
        jnp.where(col_job[:, None] == job_ids[None, :], counts[None, :], 0.0), axis=1
    )
    row_job = (place * rows_local + jnp.arange(rows_local, dtype=jnp.int32)) // RANK
    row_count = jnp.sum(
        jnp.where(row_job[:, None] == job_ids[None, :], counts[None, :], 0.0), axis=1
    )
    scalars = jnp.concatenate([after(core, input_grad), finishing.astype(jnp.int32)])
    new_a, chosen = down_optimizer(
        scalars, adapter_params[0], adapter_second[0], down_sum, column_total[None, :]
    )
    new_b = jnp.stack(
        adam_update(
            right_params[0, 0],
            right_params[0, 1],
            right_second[0],
            up_sum / row_count[:, None, None],
        )
    )
    other = swapped(chosen)
    own = core_index == 0
    checkpoint = jnp.concatenate(
        [jnp.where(own, chosen, other), jnp.where(own, other, chosen)], axis=2
    )[None]
    return (kv_out, input_grad[None], new_a[None], new_b[None], checkpoint)


def solution(mesh):
    return jax.shard_map(
        local,
        mesh=mesh,
        in_specs=(
            P("section", "dp", "tensor"),
            P("section", None),
            P("section", None, "tensor"),
            P("section", None, "tensor"),
            P("section", None, ("dp", "tensor"), None),
            P("section", ("dp", "tensor"), None),
            P("section", None, "dp", None, "tensor"),
            P("section", "dp", None, "tensor"),
            P("section", "dp"),
            P(),
            P("section"),
            P("section", "dp", None, "tensor"),
        ),
        out_specs=(
            P("section", "dp", None, "tensor"),
            P("section", "dp", "tensor"),
            P("section", None, ("dp", "tensor"), None),
            P("section", None, "dp", None, "tensor"),
            P("section", None, None, "dp"),
        ),
        check_vma=False,
    )
```

profile of v0, /device:TPU:1, one launch (start us, length us, event | category | flops | bytes accessed | tf_op | source)
XLA Modules:
  0.0 168.3 jit_solution(8748883158373333195)
XLA Ops:
  7.2 1.0 fusion
  8.2 3.4 %collective-permute-start.15 = (bf16[256,256]{1,0:T(8,128)(2,1)S(1)}, bf16[256,256]{1,0:T(8,128)(2,1)S(1)}, u32[]{:S(2)}, u32[]{:S(2)}) collective-permute-start(bf16[256,256]{1,0:T(8,128)(2,1)S(1)} %fusion), channel_id=1, source_target_pairs={{0,96},{32,0},{64,32},{96,64},{1,97},{33,1},{65,33},{97,65},{2,98}... | collective-permute-start | bytes 393224 | tf_op jit(solution)/shard_map/ppermute | solution.py:31
  11.6 2.2 %collective-permute-done.15 = bf16[256,256]{1,0:T(8,128)(2,1)S(1)} collective-permute-done((bf16[256,256]{1,0:T(8,128)(2,1)S(1)}, bf16[256,256]{1,0:T(8,128)(2,1)S(1)}, u32[]{:S(2)}, u32[]{:S(2)}) %collective-permute-start.15) | collective-permute-done | bytes 131104 | tf_op jit(solution)/shard_map/ppermute | solution.py:31
  13.7 0.7 pad_maximum_fusion
  14.5 0.8 slice_bitcast_fusion
  15.3 1.4 collective-permute-start.1
  16.6 2.6 %collective-permute-start.2 = (bf16[8,1024]{1,0:T(8,128)(2,1)S(1)}, bf16[8,1024]{1,0:T(8,128)(2,1)S(1)}, u32[]{:S(2)}, u32[]{:S(2)}) collective-permute-start(bf16[8,1024]{1,0:T(8,128)(2,1)S(1)} %bitcast.56), channel_id=1, source_target_pairs={{0,4},{2,6},{4,0},{6,2},{8,12},{10,14},{12,8},{14,10},{16,20},{18,... | collective-permute-start | bytes 49160 | tf_op jit(solution)/shard_map/ppermute | solution.py:46
  19.2 1.1 collective-permute-start.3
  20.3 0.8 slice.21
  21.1 1.9 %copy.28 = bf16[32,8,2,512]{3,1,2,0:T(8,128)(2,1)} copy(bf16[32,8,2,512]{3,2,1,0:T(2,128)(2,1)} %bitcast.53) | data formatting | bytes 1048576
  23.1 6.6 %shard_map.155 = bf16[256,4096]{1,0:T(8,128)(2,1)} custom-call(s32[1]{0:T(128)} %bitcast.core_ref, bf16[256,1024]{1,0:T(8,128)(2,1)} %bitcast.43, bf16[8192,512]{1,0:T(8,128)(2,1)} %bitcast.37, bf16[8192,512]{1,0:T(8,128)(2,1)} %bitcast.40), custom_call_target="tpu_custom_call" | custom-call | flops 134217728 | bytes 1212416 | tf_op jit(solution)/shard_map/pallas_call | solution.py:91
  29.7 2.5 %collective-permute-start.8 = (bf16[256,4096]{1,0:T(8,128)(2,1)}, bf16[256,4096]{1,0:T(8,128)(2,1)}, u32[]{:S(2)}, u32[]{:S(2)}) collective-permute-start(bf16[256,4096]{1,0:T(8,128)(2,1)} %shard_map.155), channel_id=1, source_target_pairs={{0,1},{1,0},{2,3},{3,2},{4,5},{5,4},{6,7},{7,6},{8,9},{9,8},{10,11... | collective-permute-start | bytes 6291464 | tf_op jit(solution)/shard_map/ppermute | solution.py:31
  32.2 0.9 collective-permute-start
  33.6 1.7 %collective-permute-start.4 = (bf16[4,8,1024]{2,1,0:T(8,128)(2,1)S(1)}, bf16[4,8,1024]{2,1,0:T(8,128)(2,1)S(1)}, u32[]{:S(2)}, u32[]{:S(2)}) collective-permute-start(bf16[4,8,1024]{2,1,0:T(8,128)(2,1)S(1)} %pad_maximum_fusion.1.rest_0_), channel_id=1, source_target_pairs={{0,8},{2,10},{4,12},{6,14},{8,16},{10,18},{12,20},{14,22},{16,24},... | collective-permute-start | bytes 196616 | tf_op jit(solution)/shard_map/ppermute | solution.py:53
  35.4 3.4 %collective-permute-start.5 = (bf16[4,8,1024]{2,1,0:T(8,128)(2,1)S(1)}, bf16[4,8,1024]{2,1,0:T(8,128)(2,1)S(1)}, u32[]{:S(2)}, u32[]{:S(2)}) collective-permute-start(bf16[4,8,1024]{2,1,0:T(8,128)(2,1)S(1)} %pad_maximum_fusion.1.rest_0_), channel_id=1, source_target_pairs={{0,16},{2,18},{4,20},{6,22},{8,24},{10,26},{12,28},{14,30},{16,0},... | collective-permute-start | bytes 196616 | tf_op jit(solution)/shard_map/ppermute | solution.py:53
  40.0 0.8 collective-permute-done.4.rest_1_
  41.4 1.9 %collective-permute-done.5.rest_2_ = bf16[4,8,1024]{2,1,0:T(8,128)(2,1)S(1)} collective-permute-done((bf16[4,8,1024]{2,1,0:T(8,128)(2,1)S(1)}, bf16[4,8,1024]{2,1,0:T(8,128)(2,1)S(1)}, u32[]{:S(2)}, u32[]{:S(2)}) %collective-permute-start.5) | collective-permute-done | bytes 65568 | tf_op jit(solution)/shard_map/ppermute | solution.py:53
  43.3 2.7 %collective-permute-start.10 = (f32[1,8192]{1,0:T(1,128)S(1)}, f32[1,8192]{1,0:T(1,128)S(1)}, u32[]{:S(2)}, u32[]{:S(2)}) collective-permute-start(f32[1,8192]{1,0:T(1,128)S(1)} %copy-done.8), channel_id=1, source_target_pairs={{0,96},{32,0},{64,32},{96,64},{1,97},{33,1},{65,33},{97,65},{2,98}... | collective-permute-start | bytes 98312 | tf_op jit(solution)/shard_map/ppermute | solution.py:31
  46.7 2.8 %shard_map.156 = (f32[256,256]{1,0:T(8,128)}, bf16[128,1024]{1,0:T(8,128)(2,1)}) custom-call(s32[3]{0:T(128)} %pad_add_fusion.scalars_ref, bf16[256,1024]{1,0:T(8,128)(2,1)} %bitcast.44, bf16[4,8,1024]{2,1,0:T(8,128)(2,1)} %copy-done.10, bf16[4,8,1024]{2,1,0:T(8,128)(2,1)} %copy-done.16, bf16[4,8,1024]{2,1,0:T(8,128)(2,1)} %copy-done.17, ...), custom_call_target="tpu_custom_call" | custom-call | flops 4194304 | bytes 81920 | tf_op jit(solution)/shard_map/pallas_call | solution.py:91
  49.5 1.1 collective-permute-start.7
  51.4 0.9 collective-permute-done.7
  52.3 1.0 select_convert_fusion.back_ref
  53.4 7.4 %shard_map.157 = bf16[256,4096]{1,0:T(8,128)(2,1)} custom-call(s32[1]{0:T(128)} %bitcast.core_ref, bf16[256,1024]{1,0:T(8,128)(2,1)} %bitcast.45, bf16[8192,512]{1,0:T(8,128)(2,1)} %bitcast.38, bf16[8192,512]{1,0:T(8,128)(2,1)} %bitcast.41, bf16[256,4096]{1,0:T(8,128)(2,1)} %collective-permute-done.8.rest_0_, f32[1,8192]{1,0:T(1,128)} %gain_ref.3), custom_call_target="tpu_custom_call" | custom-call | flops 134217728 | bytes 1345536 | tf_op jit(solution)/shard_map/pallas_call | solution.py:91
  61.5 3.8 %shard_map.158 = (bf16[256,2048]{1,0:T(8,128)(2,1)}, bf16[256,2048]{1,0:T(8,128)(2,1)}) custom-call(s32[1]{0:T(128)} %bitcast.core_ref, bf16[256,4096]{1,0:T(8,128)(2,1)} %bitcast.48, f32[256,1]{1,0:T(8,128)} %rsqrt.3.rstd_ref.rest_0_, f32[1,8192]{1,0:T(1,128)} %copy-done.13), custom_call_target="tpu_custom_call" | custom-call | flops 65536 | bytes 264256 | tf_op jit(solution)/shard_map/pallas_call | solution.py:91
  66.3 4.4 %collective-permute-done.12.back_ref = bf16[256,256]{1,0:T(8,128)(2,1)S(1)} collective-permute-done((bf16[256,256]{1,0:T(8,128)(2,1)S(1)}, bf16[256,256]{1,0:T(8,128)(2,1)S(1)}, u32[]{:S(2)}, u32[]{:S(2)}) %collective-permute-start.12) | collective-permute-done | bytes 131104 | tf_op jit(solution)/shard_map/ppermute | solution.py:31
  71.8 3.9 %shard_map.159 = bf16[16,256,256]{2,1,0:T(8,128)(2,1)} custom-call(s32[1]{0:T(128)} %bitcast.core_ref, bf16[256,2048]{1,0:T(8,128)(2,1)} %get-tuple-element.31.kept_ref, bf16[256,2048]{1,0:T(8,128)(2,1)} %copy-done.4, bf16[256,256]{1,0:T(8,128)(2,1)} %copy-done.6), custom_call_target="tpu_custom_call" | custom-call | flops 33554432 | bytes 270336 | tf_op jit(solution)/shard_map/pallas_call | solution.py:91
  75.7 6.0 %collective-permute-done.x_ref = bf16[256,4096]{1,0:T(8,128)(2,1)} collective-permute-done((bf16[256,4096]{1,0:T(8,128)(2,1)S(1)}, bf16[256,4096]{1,0:T(8,128)(2,1)}, u32[]{:S(2)}, u32[]{:S(2)}) %collective-permute-start) | collective-permute-done | bytes 2097184 | tf_op jit(solution)/shard_map/ppermute | solution.py:31
  82.4 1.5 collective-permute-start.17
  83.8 6.8 %all-to-all-start = ((bf16[16,256,256]{2,1,0:T(8,128)(2,1)}), bf16[16,256,256]{2,1,0:T(8,128)(2,1)S(1)}, u32[]{:S(2)}, u32[]{:S(2)}) async-start(bf16[16,256,256]{2,1,0:T(8,128)(2,1)} %shard_map.159), calls=%async_computation | async-start | bytes 4194304 | tf_op jit(solution)/shard_map/all_to_all | solution.py:676
  90.7 5.7 %collective-permute-done.14.rstd_ref = f32[256,1]{1,0:T(8,128)S(1)} collective-permute-done((f32[256,1]{1,0:T(8,128)S(1)}, f32[256,1]{1,0:T(8,128)S(1)}, u32[]{:S(2)}, u32[]{:S(2)}) %collective-permute-start.14) | collective-permute-done | bytes 1056 | tf_op jit(solution)/shard_map/ppermute | solution.py:31
  97.1 10.1 %shard_map.160 = (f32[256,1024]{1,0:T(8,128)}, f32[256,1]{1,0:T(8,128)}) custom-call(s32[1]{0:T(128)} %bitcast.core_ref, bf16[256,4096]{1,0:T(8,128)(2,1)} %collective-permute-done.x_ref, bf16[256,4096]{1,0:T(8,128)(2,1)} %collective-permute-done.13.other_ref, f32[256,1]{1,0:T(8,128)} %copy-done.5, f32[1,8192]{1,0:T(1,128)} %gain_ref.3, ...), custom_call_target="tpu_custom_call" | custom-call | flops 268435456 | bytes 1411200 | tf_op jit(solution)/shard_map/pallas_call | solution.py:91
  107.3 4.4 %shard_map.161.mine_ref = f32[256,256]{1,0:T(8,128)} custom-call(s32[1]{0:T(128)} %bitcast.core_ref, bf16[256,4096]{1,0:T(8,128)(2,1)} %collective-permute-done.x_ref, f32[256,1]{1,0:T(8,128)} %copy-done.5, f32[1,8192]{1,0:T(1,128)} %gain_ref.3, bf16[8192,512]{1,0:T(8,128)(2,1)} %all-gather.2.cloned.1.call-done.factors_ref), custom_call_target="tpu_custom_call" | custom-call | flops 33554432 | bytes 673856 | tf_op jit(solution)/shard_map/pallas_call | solution.py:91
  111.7 1.5 collective-permute-start.16
  114.0 0.8 copy.26.jobs_ref
  115.5 2.4 %shard_map.162 = (bf16[256,256]{1,0:T(8,128)(2,1)}, bf16[128,1024]{1,0:T(8,128)(2,1)}, f32[256,1]{1,0:T(8,128)}) custom-call(s32[1]{0:T(128)} %bitcast.core_ref, f32[256,256]{1,0:T(8,128)} %shard_map.161.mine_ref, f32[256,256]{1,0:T(8,128)} %copy-done.9, s32[256,1]{1,0:T(8,128)} %copy.26.jobs_ref, bf16[256,1024]{1,0:T(8,128)(2,1)} %bitcast.47, ...), custom_call_target="tpu_custom_call" | custom-call | flops 4194304 | bytes 98432 | tf_op jit(solution)/shard_map/pallas_call | solution.py:91
  117.8 0.9 add_multiply_fusion
  118.8 4.4 %all-to-all-done.pieces_ref = bf16[16,256,256]{2,1,0:T(8,128)(2,1)S(1)} async-done(((bf16[16,256,256]{2,1,0:T(8,128)(2,1)}), bf16[16,256,256]{2,1,0:T(8,128)(2,1)S(1)}, u32[]{:S(2)}, u32[]{:S(2)}) %all-to-all-start) | async-done | bytes 2097184 | tf_op jit(solution)/shard_map/all_to_all | solution.py:676
  123.2 1.3 copy-done.1
  124.5 2.3 %shard_map.163 = bf16[256,256]{1,0:T(8,128)(2,1)} custom-call(s32[1]{0:T(128)} %bitcast.core_ref, bf16[16,256,256]{2,1,0:T(8,128)(2,1)} %copy-done.1), custom_call_target="tpu_custom_call" | custom-call | flops 65536 | bytes 139264 | tf_op jit(solution)/shard_map/pallas_call | solution.py:91
  127.6 2.4 %shard_map.164 = bf16[256,1024]{1,0:T(8,128)(2,1)} custom-call(s32[1]{0:T(128)} %bitcast.core_ref, f32[256,1024]{1,0:T(8,128)} %get-tuple-element.34.frozen_ref, bf16[256,256]{1,0:T(8,128)(2,1)} %get-tuple-element.39.low_ref, bf16[128,1024]{1,0:T(8,128)(2,1)} %get-tuple-element.40.up_ref), custom_call_target="tpu_custom_call" | custom-call | flops 4194304 | bytes 122880 | tf_op jit(solution)/shard_map/pallas_call | solution.py:91
  130.0 2.7 %collective-permute-done.19.rest_1_ = f32[256,1]{1,0:T(8,128)S(1)} collective-permute-done((f32[256,1]{1,0:T(8,128)S(1)}, f32[256,1]{1,0:T(8,128)S(1)}, u32[]{:S(2)}, u32[]{:S(2)}) %collective-permute-start.19) | collective-permute-done | bytes 1056 | tf_op jit(solution)/shard_map/ppermute | solution.py:31
  133.3 5.4 %shard_map.165 = bf16[256,4096]{1,0:T(8,128)(2,1)} custom-call(s32[1]{0:T(128)} %bitcast.core_ref, bf16[256,4096]{1,0:T(8,128)(2,1)} %collective-permute-done.17.scaled_ref, bf16[256,256]{1,0:T(8,128)(2,1)} %copy-done.6, bf16[8192,512]{1,0:T(8,128)(2,1)} %all-gather.2.cloned.1.call-done.factors_ref, f32[1,8192]{1,0:T(1,128)} %copy-done.13, ...), custom_call_target="tpu_custom_call" | custom-call | flops 33554432 | bytes 927872 | tf_op jit(solution)/shard_map/pallas_call | solution.py:91
  140.0 3.0 %shard_map.166 = (f32[3,256,256]{2,1,0:T(8,128)}, f32[3,32,256]{2,1,0:T(8,128)}) custom-call(s32[2]{0:T(128)} %pad_add_fusion.1.scalars_ref, f32[2,256,256]{2,1,0:T(8,128)} %bitcast.52, f32[256,256]{1,0:T(8,128)} %bitcast.54, bf16[256,256]{1,0:T(8,128)(2,1)} %copy-done.15, f32[1,256]{1,0:T(1,128)} %bitcast.65), custom_call_target="tpu_custom_call" | custom-call | flops 81920 | bytes 112704 | tf_op jit(solution)/shard_map/pallas_call | solution.py:91
  143.0 0.8 collective-permute-start.21
  144.0 1.2 reshape.130
  145.1 6.8 %all-to-all-start.1 = ((bf16[16,8,1024]{2,1,0:T(8,128)(2,1)}), bf16[16,8,1024]{2,1,0:T(8,128)(2,1)S(1)}, u32[]{:S(2)}, u32[]{:S(2)}) async-start(bf16[16,8,1024]{2,1,0:T(8,128)(2,1)} %bitcast.20), calls=%async_computation.1 | async-start | bytes 524288 | tf_op jit(solution)/shard_map/all_to_all | solution.py:687
  152.0 0.9 broadcast_select_fusion.1
  153.6 6.9 %all-to-all-done.1 = bf16[16,8,1024]{2,1,0:T(8,128)(2,1)S(1)} async-done(((bf16[16,8,1024]{2,1,0:T(8,128)(2,1)}), bf16[16,8,1024]{2,1,0:T(8,128)(2,1)S(1)}, u32[]{:S(2)}, u32[]{:S(2)}) %all-to-all-start.1) | async-done | bytes 262176 | tf_op jit(solution)/shard_map/all_to_all | solution.py:687
  (90 shorter events, 13.5 us)
Async XLA Ops:
  7.2 100.1 %all-gather.2.cloned.1.call-start = ((), (), s32[]{:S(2)}) async-start(), calls=%async_computation.2 | async-start | bytes 8650752 | tf_op jit(solution)/shard_map/all_gather | solution.py:648
  8.2 5.5 %collective-permute-start.15 = (bf16[256,256]{1,0:T(8,128)(2,1)S(1)}, bf16[256,256]{1,0:T(8,128)(2,1)S(1)}, u32[]{:S(2)}, u32[]{:S(2)}) collective-permute-start(bf16[256,256]{1,0:T(8,128)(2,1)S(1)} %fusion), channel_id=1, source_target_pairs={{0,96},{32,0},{64,32},{96,64},{1,97},{33,1},{65,33},{97,65},{2,98}... | collective-permute-start | bytes 393224 | tf_op jit(solution)/shard_map/ppermute | solution.py:31
  15.3 7.8 %collective-permute-start.1 = (bf16[8,1024]{1,0:T(8,128)(2,1)S(1)}, bf16[8,1024]{1,0:T(8,128)(2,1)S(1)}, u32[]{:S(2)}, u32[]{:S(2)}) collective-permute-start(bf16[8,1024]{1,0:T(8,128)(2,1)S(1)} %bitcast.55), channel_id=1, source_target_pairs={{0,2},{2,4},{4,6},{6,0},{8,10},{10,12},{12,14},{14,8},{16,18},{18,... | collective-permute-start | bytes 49160 | tf_op jit(solution)/shard_map/ppermute | solution.py:46
  16.6 6.4 %collective-permute-start.2 = (bf16[8,1024]{1,0:T(8,128)(2,1)S(1)}, bf16[8,1024]{1,0:T(8,128)(2,1)S(1)}, u32[]{:S(2)}, u32[]{:S(2)}) collective-permute-start(bf16[8,1024]{1,0:T(8,128)(2,1)S(1)} %bitcast.56), channel_id=1, source_target_pairs={{0,4},{2,6},{4,0},{6,2},{8,12},{10,14},{12,8},{14,10},{16,20},{18,... | collective-permute-start | bytes 49160 | tf_op jit(solution)/shard_map/ppermute | solution.py:46
  19.2 3.8 %collective-permute-start.3 = (bf16[8,1024]{1,0:T(8,128)(2,1)S(1)}, bf16[8,1024]{1,0:T(8,128)(2,1)S(1)}, u32[]{:S(2)}, u32[]{:S(2)}) collective-permute-start(bf16[8,1024]{1,0:T(8,128)(2,1)S(1)} %bitcast.57), channel_id=1, source_target_pairs={{0,6},{2,0},{4,2},{6,4},{8,14},{10,8},{12,10},{14,12},{16,22},{18,... | collective-permute-start | bytes 49160 | tf_op jit(solution)/shard_map/ppermute | solution.py:46
  23.1 15.7 %copy-start.10 = (bf16[4,8,1024]{2,1,0:T(8,128)(2,1)}, bf16[4,8,1024]{2,1,0:T(8,128)(2,1)S(1)}, u32[]{:S(2)}) copy-start(bf16[4,8,1024]{2,1,0:T(8,128)(2,1)S(1)} %pad_maximum_fusion.1.rest_0_) | copy-start | bytes 196612
  23.1 9.1 %copy-start = (bf16[1,256,4096]{2,1,0:T(8,128)(2,1)S(1)}, bf16[1,256,4096]{2,1,0:T(8,128)(2,1)}, u32[]{:S(2)}) copy-start(bf16[1,256,4096]{2,1,0:T(8,128)(2,1)} %param.12) | copy-start | bytes 6291460
  29.7 13.6 %copy-start.8 = (f32[1,8192]{1,0:T(1,128)S(1)}, f32[1,8192]{1,0:T(1,128)}, u32[]{:S(2)}) copy-start(f32[1,8192]{1,0:T(1,128)} %gain_ref.3) | copy-start | bytes 98308
  29.7 22.6 %copy-start.20 = (s32[1,256]{1,0:T(1,128)S(1)}, s32[1,256]{1,0:T(1,128)}, u32[]{:S(2)}) copy-start(s32[1,256]{1,0:T(1,128)} %param.20) | copy-start | bytes 3076
  29.7 23.7 %collective-permute-start.8 = (bf16[256,4096]{1,0:T(8,128)(2,1)}, bf16[256,4096]{1,0:T(8,128)(2,1)}, u32[]{:S(2)}, u32[]{:S(2)}) collective-permute-start(bf16[256,4096]{1,0:T(8,128)(2,1)} %shard_map.155), channel_id=1, source_target_pairs={{0,1},{1,0},{2,3},{3,2},{4,5},{5,4},{6,7},{7,6},{8,9},{9,8},{10,11... | collective-permute-start | bytes 6291464 | tf_op jit(solution)/shard_map/ppermute | solution.py:31
  32.2 49.5 %collective-permute-start = (bf16[256,4096]{1,0:T(8,128)(2,1)S(1)}, bf16[256,4096]{1,0:T(8,128)(2,1)}, u32[]{:S(2)}, u32[]{:S(2)}) collective-permute-start(bf16[256,4096]{1,0:T(8,128)(2,1)S(1)} %bitcast.50), channel_id=1, source_target_pairs={{0,32},{32,64},{64,96},{96,0},{1,33},{33,65},{65,97},{97,1},{2,34}... | collective-permute-start | bytes 6291464 | tf_op jit(solution)/shard_map/ppermute | solution.py:31
  33.6 7.2 %collective-permute-start.4 = (bf16[4,8,1024]{2,1,0:T(8,128)(2,1)S(1)}, bf16[4,8,1024]{2,1,0:T(8,128)(2,1)S(1)}, u32[]{:S(2)}, u32[]{:S(2)}) collective-permute-start(bf16[4,8,1024]{2,1,0:T(8,128)(2,1)S(1)} %pad_maximum_fusion.1.rest_0_), channel_id=1, source_target_pairs={{0,8},{2,10},{4,12},{6,14},{8,16},{10,18},{12,20},{14,22},{16,24},... | collective-permute-start | bytes 196616 | tf_op jit(solution)/shard_map/ppermute | solution.py:53
  35.4 8.0 %collective-permute-start.5 = (bf16[4,8,1024]{2,1,0:T(8,128)(2,1)S(1)}, bf16[4,8,1024]{2,1,0:T(8,128)(2,1)S(1)}, u32[]{:S(2)}, u32[]{:S(2)}) collective-permute-start(bf16[4,8,1024]{2,1,0:T(8,128)(2,1)S(1)} %pad_maximum_fusion.1.rest_0_), channel_id=1, source_target_pairs={{0,16},{2,18},{4,20},{6,22},{8,24},{10,26},{12,28},{14,30},{16,0},... | collective-permute-start | bytes 196616 | tf_op jit(solution)/shard_map/ppermute | solution.py:53
  38.7 7.4 %collective-permute-start.6 = (bf16[4,8,1024]{2,1,0:T(8,128)(2,1)S(1)}, bf16[4,8,1024]{2,1,0:T(8,128)(2,1)S(1)}, u32[]{:S(2)}, u32[]{:S(2)}) collective-permute-start(bf16[4,8,1024]{2,1,0:T(8,128)(2,1)S(1)} %pad_maximum_fusion.1.rest_0_), channel_id=1, source_target_pairs={{0,24},{2,26},{4,28},{6,30},{8,0},{10,2},{12,4},{14,6},{16,8},{18,... | collective-permute-start | bytes 196616 | tf_op jit(solution)/shard_map/ppermute | solution.py:53
  40.8 5.2 %copy-start.16 = (bf16[4,8,1024]{2,1,0:T(8,128)(2,1)}, bf16[4,8,1024]{2,1,0:T(8,128)(2,1)S(1)}, u32[]{:S(2)}) copy-start(bf16[4,8,1024]{2,1,0:T(8,128)(2,1)S(1)} %collective-permute-done.4.rest_1_) | copy-start | bytes 196612
  40.8 9.8 %collective-permute-start.9 = (f32[256,1]{0,1:T(1,128)S(1)}, f32[256,1]{0,1:T(1,128)S(1)}, u32[]{:S(2)}, u32[]{:S(2)}) collective-permute-start(f32[256,1]{0,1:T(1,128)S(1)} %bitcast.63), channel_id=1, source_target_pairs={{0,1},{1,0},{2,3},{3,2},{4,5},{5,4},{6,7},{7,6},{8,9},{9,8},{10,11... | collective-permute-start | bytes 3080 | tf_op jit(solution)/shard_map/ppermute | solution.py:31
  43.3 2.8 %copy-start.17 = (bf16[4,8,1024]{2,1,0:T(8,128)(2,1)}, bf16[4,8,1024]{2,1,0:T(8,128)(2,1)S(1)}, u32[]{:S(2)}) copy-start(bf16[4,8,1024]{2,1,0:T(8,128)(2,1)S(1)} %collective-permute-done.5.rest_2_) | copy-start | bytes 196612
  43.3 17.5 %collective-permute-start.10 = (f32[1,8192]{1,0:T(1,128)S(1)}, f32[1,8192]{1,0:T(1,128)S(1)}, u32[]{:S(2)}, u32[]{:S(2)}) collective-permute-start(f32[1,8192]{1,0:T(1,128)S(1)} %copy-done.8), channel_id=1, source_target_pairs={{0,96},{32,0},{64,32},{96,64},{1,97},{33,1},{65,33},{97,65},{2,98}... | collective-permute-start | bytes 98312 | tf_op jit(solution)/shard_map/ppermute | solution.py:31
  46.1 0.6 copy-start.18
  49.5 2.8 %collective-permute-start.7 = (f32[256,256]{1,0:T(8,128)}, f32[256,256]{1,0:T(8,128)S(1)}, u32[]{:S(2)}, u32[]{:S(2)}) collective-permute-start(f32[256,256]{1,0:T(8,128)} %get-tuple-element.28), channel_id=1, source_target_pairs={{0,1},{1,0},{2,3},{3,2},{4,5},{5,4},{6,7},{7,6},{8,9},{9,8},{10,11... | collective-permute-start | bytes 786440 | tf_op jit(solution)/shard_map/ppermute | solution.py:31
  53.4 12.4 %copy-start.7 = (bf16[256,256]{1,0:T(8,128)(2,1)}, bf16[256,256]{1,0:T(8,128)(2,1)S(1)}, u32[]{:S(2)}) copy-start(bf16[256,256]{1,0:T(8,128)(2,1)S(1)} %select_convert_fusion.back_ref) | copy-start | bytes 393220
  60.9 0.6 copy-start.13
  65.3 5.4 %collective-permute-start.11 = (bf16[256,2048]{1,0:T(8,128)(2,1)}, bf16[256,2048]{1,0:T(8,128)(2,1)S(1)}, u32[]{:S(2)}, u32[]{:S(2)}) collective-permute-start(bf16[256,2048]{1,0:T(8,128)(2,1)} %get-tuple-element.32), channel_id=1, source_target_pairs={{0,1},{1,0},{2,3},{3,2},{4,5},{5,4},{6,7},{7,6},{8,9},{9,8},{10,11... | collective-permute-start | bytes 3145736 | tf_op jit(solution)/shard_map/ppermute | solution.py:31
  65.8 4.9 %collective-permute-start.12 = (bf16[256,256]{1,0:T(8,128)(2,1)S(1)}, bf16[256,256]{1,0:T(8,128)(2,1)S(1)}, u32[]{:S(2)}, u32[]{:S(2)}) collective-permute-start(bf16[256,256]{1,0:T(8,128)(2,1)S(1)} %select_convert_fusion.back_ref), channel_id=1, source_target_pairs={{0,96},{32,0},{64,32},{96,64},{1,97},{33,1},{65,33},{97,65},{2,98}... | collective-permute-start | bytes 393224 | tf_op jit(solution)/shard_map/ppermute | solution.py:31
  70.7 0.6 copy-start.6
  70.7 1.1 copy-start.4
  75.7 14.9 %copy-start.3 = (f32[256,1]{1,0:T(8,128)S(1)}, f32[256,1]{1,0:T(8,128)}, u32[]{:S(2)}) copy-start(f32[256,1]{1,0:T(8,128)} %rsqrt.3.rstd_ref.rest_0_) | copy-start | bytes 3076
  81.7 14.7 %collective-permute-start.13 = (bf16[256,4096]{1,0:T(8,128)(2,1)}, bf16[256,4096]{1,0:T(8,128)(2,1)}, u32[]{:S(2)}, u32[]{:S(2)}) collective-permute-start(bf16[256,4096]{1,0:T(8,128)(2,1)} %collective-permute-done.x_ref), channel_id=1, source_target_pairs={{0,1},{1,0},{2,3},{3,2},{4,5},{5,4},{6,7},{7,6},{8,9},{9,8},{10,11... | collective-permute-start | bytes 6291464 | tf_op jit(solution)/shard_map/ppermute | solution.py:31
  82.4 47.6 %collective-permute-start.17 = (bf16[256,4096]{1,0:T(8,128)(2,1)}, bf16[256,4096]{1,0:T(8,128)(2,1)}, u32[]{:S(2)}, u32[]{:S(2)}) collective-permute-start(bf16[256,4096]{1,0:T(8,128)(2,1)} %shard_map.157), channel_id=1, source_target_pairs={{0,96},{32,0},{64,32},{96,64},{1,97},{33,1},{65,33},{97,65},{2,98}... | collective-permute-start | bytes 6291464 | tf_op jit(solution)/shard_map/ppermute | solution.py:31
  83.8 39.4 %all-to-all-start = ((bf16[16,256,256]{2,1,0:T(8,128)(2,1)}), bf16[16,256,256]{2,1,0:T(8,128)(2,1)S(1)}, u32[]{:S(2)}, u32[]{:S(2)}) async-start(bf16[16,256,256]{2,1,0:T(8,128)(2,1)} %shard_map.159), calls=%async_computation | async-start | bytes 4194304 | tf_op jit(solution)/shard_map/all_to_all | solution.py:676
  90.7 5.8 %collective-permute-start.14 = (f32[256,1]{1,0:T(8,128)S(1)}, f32[256,1]{1,0:T(8,128)S(1)}, u32[]{:S(2)}, u32[]{:S(2)}) collective-permute-start(f32[256,1]{1,0:T(8,128)S(1)} %copy-done.3), channel_id=1, source_target_pairs={{0,32},{32,64},{64,96},{96,0},{1,33},{33,65},{65,97},{97,1},{2,34}... | collective-permute-start | bytes 3080 | tf_op jit(solution)/shard_map/ppermute | solution.py:31
  96.4 0.6 copy-start.5
  107.2 6.0 %copy-start.21 = (s32[8]{0:T(128)S(1)}, s32[8]{0:T(128)}, u32[]{:S(2)}) copy-start(s32[8]{0:T(128)} %param.21) | copy-start | bytes 100
  107.2 6.0 %copy-start.14 = (f32[256,1]{1,0:T(8,128)S(1)}, f32[256,1]{1,0:T(8,128)}, u32[]{:S(2)}) copy-start(f32[256,1]{1,0:T(8,128)} %get-tuple-element.42) | copy-start | bytes 3076
  111.7 3.1 %collective-permute-start.16 = (f32[256,256]{1,0:T(8,128)}, f32[256,256]{1,0:T(8,128)S(1)}, u32[]{:S(2)}, u32[]{:S(2)}) collective-permute-start(f32[256,256]{1,0:T(8,128)} %shard_map.161.mine_ref), channel_id=1, source_target_pairs={{0,1},{1,0},{2,3},{3,2},{4,5},{5,4},{6,7},{7,6},{8,9},{9,8},{10,11... | collective-permute-start | bytes 786440 | tf_op jit(solution)/shard_map/ppermute | solution.py:31
  113.2 4.6 %collective-permute-start.18 = (f32[256,1]{1,0:T(8,128)S(1)}, f32[256,1]{1,0:T(8,128)S(1)}, u32[]{:S(2)}, u32[]{:S(2)}) collective-permute-start(f32[256,1]{1,0:T(8,128)S(1)} %copy-done.14), channel_id=1, source_target_pairs={{0,1},{1,0},{2,3},{3,2},{4,5},{5,4},{6,7},{7,6},{8,9},{9,8},{10,11... | collective-permute-start | bytes 3080 | tf_op jit(solution)/shard_map/ppermute | solution.py:31
  114.8 0.7 copy-start.9
  118.8 13.9 %collective-permute-start.19 = (f32[256,1]{1,0:T(8,128)S(1)}, f32[256,1]{1,0:T(8,128)S(1)}, u32[]{:S(2)}, u32[]{:S(2)}) collective-permute-start(f32[256,1]{1,0:T(8,128)S(1)} %add_multiply_fusion), channel_id=1, source_target_pairs={{0,96},{32,0},{64,32},{96,64},{1,97},{33,1},{65,33},{97,65},{2,98}... | collective-permute-start | bytes 3080 | tf_op jit(solution)/shard_map/ppermute | solution.py:31
  123.2 1.3 copy-start.1
  126.8 12.5 %collective-permute-start.20 = (bf16[256,256]{1,0:T(8,128)(2,1)}, bf16[256,256]{1,0:T(8,128)(2,1)S(1)}, u32[]{:S(2)}, u32[]{:S(2)}) collective-permute-start(bf16[256,256]{1,0:T(8,128)(2,1)} %shard_map.163), channel_id=1, source_target_pairs={{0,32},{32,64},{64,96},{96,0},{1,33},{33,65},{65,97},{97,1},{2,34}... | collective-permute-start | bytes 393224 | tf_op jit(solution)/shard_map/ppermute | solution.py:31
  130.0 14.0 %copy-start.2 = (bf16[256,1024]{1,0:T(8,128)(2,1)S(1)}, bf16[256,1024]{1,0:T(8,128)(2,1)}, u32[]{:S(2)}) copy-start(bf16[256,1024]{1,0:T(8,128)(2,1)} %shard_map.164) | copy-start | bytes 1572868
  132.6 0.7 copy-start.12
  138.7 21.9 %copy-start.11 = (f32[1,2,8,2,512]{4,3,2,1,0:T(2,128)S(1)}, f32[1,2,8,2,512]{4,3,2,1,0:T(2,128)}, u32[]{:S(2)}) copy-start(f32[1,2,8,2,512]{4,3,2,1,0:T(2,128)} %param.18) | copy-start | bytes 196612
  138.7 21.9 %copy-start.19 = (f32[1,8,2,512]{3,2,1,0:T(2,128)S(1)}, f32[1,8,2,512]{3,2,1,0:T(2,128)}, u32[]{:S(2)}) copy-start(f32[1,8,2,512]{3,2,1,0:T(2,128)} %param.19) | copy-start | bytes 98308
  139.3 0.7 copy-start.15
  143.0 8.9 %collective-permute-start.21 = (f32[3,32,256]{2,1,0:T(8,128)}, f32[3,32,256]{2,1,0:T(8,128)S(1)}, u32[]{:S(2)}, u32[]{:S(2)}) collective-permute-start(f32[3,32,256]{2,1,0:T(8,128)} %get-tuple-element.46), channel_id=1, source_target_pairs={{0,1},{1,0},{2,3},{3,2},{4,5},{5,4},{6,7},{7,6},{8,9},{9,8},{10,11... | collective-permute-start | bytes 294920 | tf_op jit(solution)/shard_map/ppermute | solution.py:31
  145.1 15.3 %all-to-all-start.1 = ((bf16[16,8,1024]{2,1,0:T(8,128)(2,1)}), bf16[16,8,1024]{2,1,0:T(8,128)(2,1)S(1)}, u32[]{:S(2)}, u32[]{:S(2)}) async-start(bf16[16,8,1024]{2,1,0:T(8,128)(2,1)} %bitcast.20), calls=%async_computation.1 | async-start | bytes 524288 | tf_op jit(solution)/shard_map/all_to_all | solution.py:687
Sparse Core Ops, SparseCore 0:
  14.6 58.7 all-gather.1
where the time goes:
time: 169 us; the launch traced here: 168 us
  Pallas kernels  54.6 us (32%)
  starting transfers between devices  41.4 us (24%)
  waiting for transfers between devices  35.8 us (21%)
  between operations  15.1 us (9%)
  local copies, waits for them, and re-layouts  13.6 us (8%)
  other arithmetic  7.82 us (5%)
    pallas_call x12, Pallas kernels, call(): pl.pallas_call(body, out_shape=out_shape, grid_spec=pltpu.PrefetchScalarG...  54.6 us
    ppermute x16, waiting for transfers between devices, shifted(): return lax.ppermute(value, axis, pairs)  21.8 us
    ppermute x16, starting transfers between devices, shifted(): return lax.ppermute(value, axis, pairs)  16.9 us
    unnamed x47, local copies, waits for them, and re-layouts  9.02 us
    all_to_all x1, waiting for transfers between devices, local(): up_pieces = lax.all_to_all(up_pieces, 'dp', 0, 0, tiled=True)  6.91 us
    all_to_all x1, starting transfers between devices, local(): up_pieces = lax.all_to_all(up_pieces, 'dp', 0, 0, tiled=True)  6.8 us
    all_to_all x1, starting transfers between devices, local(): down_pieces = lax.all_to_all(down_piece, 'dp', 0, 0, tiled=True)  6.8 us
    ppermute x3, starting transfers between devices, shifted_z(): return lax.ppermute(value, 'dp', pairs)  5.81 us
  transfers between devices with their start and end apart: 25, of which 10 were waited for; matrix products, arithmetic and copies ran while one was open for 7% of the time, Pallas kernels for 31%

commit v1 on v0

--- a/solution.py
+++ b/solution.py
@@ -17,9 +17,12 @@
 FEATURE_WIDTH = JOBS * RANK
 COLUMNS = 2 * FEATURE_WIDTH
 STEP = 1024
-SIDE = 4
 VMEM_LIMIT = 54 * 1024 * 1024
+FULL_LIMIT = 60 * 1024 * 1024
+SMALL_LIMIT = 24 * 1024 * 1024
 HINT = 16
+CHUNKS = 2
+PARTS = 2
 
 F32 = jnp.float32
 BF16 = jnp.bfloat16
@@ -37,20 +40,6 @@
 
 def after(value, *others):
     return lax.optimization_barrier((value,) + others)[0]
-
-
-def shifted_y(value, steps):
-    pairs = [
-        (z * SIDE + y, z * SIDE + (y + steps) % SIDE) for z in range(SIDE) for y in range(SIDE)
-    ]
-    return lax.ppermute(value, "dp", pairs)
-
-
-def shifted_z(value, steps):
-    pairs = [
-        (z * SIDE + y, (z + steps) % SIDE * SIDE + y) for z in range(SIDE) for y in range(SIDE)
-    ]
-    return lax.ppermute(value, "dp", pairs)
 
 
 def adam_update(param, first, second, grad):
@@ -81,7 +70,9 @@
 HBM = pl.BlockSpec(memory_space=pl.ANY)
 
 
-def call(body, core, args, streamed, out_shape, flops, scratch=(), streamed_outs=()):
+def call(
+    body, core, args, streamed, out_shape, flops, scratch=(), streamed_outs=(), limit=SMALL_LIMIT
+):
     outs = jax.tree.leaves(out_shape)
     moved = sum(a.size * a.dtype.itemsize for a in outs + list(args))
     out_specs = [
@@ -100,7 +91,7 @@
             out_specs=out_specs[0] if single else out_specs,
             scratch_shapes=list(scratch),
         ),
-        compiler_params=pltpu.CompilerParams(vmem_limit_bytes=VMEM_LIMIT),
+        compiler_params=pltpu.CompilerParams(vmem_limit_bytes=limit),
         cost_estimate=pl.CostEstimate(
             flops=flops // HINT, bytes_accessed=moved // HINT, transcendentals=0
         ),
@@ -125,11 +116,16 @@
     tokens, kv = cot.shape[0], cot.shape[1] // 2
     steps = half // STEP
     own = received is not None
+    parts = CHUNKS
+    within = steps // parts
 
     def body(core_ref, cot_ref, key_ref, value_ref, *rest):
         if own:
-            received_ref, gain_ref, *rest = rest
-        out_ref, keys, values, out, key_sems, value_sems, out_sems, *rest = rest
+            received_refs, (gain_ref, *rest) = rest[:parts], rest[parts:]
+            out_refs, rest = rest[:1], rest[1:]
+        else:
+            out_refs, rest = rest[:parts], rest[parts:]
+        keys, values, out, key_sems, value_sems, out_sems, *rest = rest
         side = core_ref[0] if own else 1 - core_ref[0]
         base = pl.multiple_of(side * half, half)
         rows = [pl.ds(base + i * STEP, STEP) for i in range(steps)]
@@ -143,7 +139,7 @@
                 arrived, arrived_sems = rest
                 pairs.append(
                     (
-                        received_ref.at[:, lanes_of(i)],
+                        received_refs[i // within].at[:, lanes_of(i % within)],
                         arrived.at[:, lanes_of(i)],
                         arrived_sems.at[i],
                     )
@@ -160,11 +156,11 @@
             if own:
                 total = (total + arrived[:, lanes_of(i)].astype(F32)) * gain_ref[:, rows[i]]
             out[:, lanes_of(i)] = total.astype(BF16)
-            leaving.append(
-                pltpu.make_async_copy(
-                    out.at[:, lanes_of(i)], out_ref.at[:, lanes_of(i)], out_sems.at[i]
-                )
-            )
+            if own:
+                target = out_refs[0].at[:, lanes_of(i)]
+            else:
+                target = out_refs[i // within].at[:, lanes_of(i % within)]
+            leaving.append(pltpu.make_async_copy(out.at[:, lanes_of(i)], target, out_sems.at[i]))
             leaving[i].start()
         for copy in leaving:
             copy.wait()
@@ -180,17 +176,19 @@
         sems,
     ]
     if own:
-        args += [received, gain]
+        args += [*received, gain]
         scratch += [pltpu.VMEM((tokens, half), BF16), sems]
+    piece = jax.ShapeDtypeStruct((tokens, half // parts), BF16)
     return call(
         body,
         core,
         args,
-        (1, 2, 3),
-        jax.ShapeDtypeStruct((tokens, half), BF16),
+        (1, 2) + tuple(range(3, 3 + parts)) * own,
+        jax.ShapeDtypeStruct((tokens, half), BF16) if own else [piece] * parts,
         4 * tokens * half * kv,
         scratch,
-        (0,),
+        tuple(range(1 if own else parts)),
+        VMEM_LIMIT,
     )
 
 
@@ -308,77 +306,93 @@
     )
 
 
-def projected(core, x, x_other, rstd, gain, key_matrix, value_matrix, cot):
-    tokens, half = x.shape
+def projected(core, own, other, start, half, gain, key_matrix, value_matrix, cot, before=None):
+    tokens, part = own.shape
     kv = key_matrix.shape[1]
+    within = part // STEP
+    steps = 2 * within
+    last = before is not None
+
+    def body(core_ref, own_ref, other_ref, gain_ref, key_ref, value_ref, *rest):
+        if last:
+            cot_ref, before_ref, sums_before_ref, *rest = rest
+        out_ref, sums_ref, *rest = rest
+        held, keys, values, x_sems, key_sems, value_sems = rest
+        rows, copies = [], []
+        for i in range(steps):
+            ref, side = (own_ref, core_ref[0]) if i < within else (other_ref, 1 - core_ref[0])
+            first = side * half + start + i % within * STEP
+            rows.append(pl.ds(pl.multiple_of(first, STEP), STEP))
+            sources = [
+                (ref.at[:, lanes_of(i % within)], held.at[:, lanes_of(i)], x_sems),
+                (key_ref.at[rows[i]], keys.at[lanes_of(i)], key_sems),
+                (value_ref.at[rows[i]], values.at[lanes_of(i)], value_sems),
+            ]
+            copies.append([pltpu.make_async_copy(a, b, sems.at[i]) for a, b, sems in sources])
+            for copy in copies[i]:
+                copy.start()
+        for i in range(steps):
+            for copy in copies[i]:
+                copy.wait()
+            wide = held[:, lanes_of(i)].astype(F32)
+            if i < within:
+                square = jnp.sum(wide * wide, axis=1, keepdims=True)
+                squares = square if i == 0 else squares + square
+            scaled = (wide * gain_ref[:, rows[i]]).astype(BF16)
+            for lanes, matrix in ((slice(0, kv), keys), (slice(kv, 2 * kv), values)):
+                product = dot(scaled, matrix[lanes_of(i)])
+                if i > 0:
+                    out_ref[:, lanes] += product
+                elif last:
+                    out_ref[:, lanes] = before_ref[:, lanes] + product
+                else:
+                    out_ref[:, lanes] = product
+        sums_ref[...] = jnp.broadcast_to(squares, sums_ref.shape)
+        if last:
+            products = jnp.sum(out_ref[...] * cot_ref[...].astype(F32), axis=1, keepdims=True)
+            lane = lax.broadcasted_iota(jnp.int32, sums_ref.shape, 1)
+            sums_ref[...] = jnp.where(lane == 0, squares + sums_before_ref[...], products)
+
+    sems = pltpu.SemaphoreType.DMA((steps,))
+    total = jax.ShapeDtypeStruct((tokens, 2 * kv), F32)
+    return call(
+        body,
+        core,
+        [own, other, gain, key_matrix, value_matrix] + ([cot, *before] if last else []),
+        (0, 1, 3, 4),
+        [total, jax.ShapeDtypeStruct((tokens, 128), F32)],
+        8 * tokens * part * kv,
+        [
+            pltpu.VMEM((tokens, 2 * part), BF16),
+            pltpu.VMEM((2 * part, kv), BF16),
+            pltpu.VMEM((2 * part, kv), BF16),
+            sems,
+            sems,
+            sems,
+        ],
+        limit=VMEM_LIMIT,
+    )
+
+
+def low_rank_down(core, xs, gain, factors):
+    parts = len(xs)
+    tokens, part = xs[0].shape
+    half = parts * part
+    within = part // STEP
     steps = half // STEP
 
-    def body(core_ref, x_ref, other_ref, rstd_ref, gain_ref, key_ref, value_ref, cot_ref, *rest):
-        out_ref, sum_ref, xs, keys, values, x_sems, key_sems, value_sems = rest
-        rows, copies = [], []
-        for side, ref in enumerate((x_ref, other_ref)):
-            base = core_ref[0] if side == 0 else 1 - core_ref[0]
-            for i in range(steps):
-                at = side * steps + i
-                rows.append(pl.ds(pl.multiple_of(base * half + i * STEP, STEP), STEP))
-                sources = [
-                    (ref.at[:, lanes_of(i)], xs.at[:, lanes_of(at)], x_sems),
-                    (key_ref.at[rows[at]], keys.at[lanes_of(at)], key_sems),
-                    (value_ref.at[rows[at]], values.at[lanes_of(at)], value_sems),
-                ]
-                copies.append(
-                    [pltpu.make_async_copy(a, b, sems.at[at]) for a, b, sems in sources]
-                )
-                for copy in copies[at]:
-                    copy.start()
-        rstd = rstd_ref[...]
-        for at in range(2 * steps):
-            for copy in copies[at]:
-                copy.wait()
-            normed = xs[:, lanes_of(at)].astype(F32) * rstd * gain_ref[:, rows[at]]
-            normed = normed.astype(BF16)
-            for lanes, matrix in ((slice(0, kv), keys), (slice(kv, 2 * kv), values)):
-                product = dot(normed, matrix[lanes_of(at)])
-                if at == 0:
-                    out_ref[:, lanes] = product
-                else:
-                    out_ref[:, lanes] += product
-        sum_ref[...] = jnp.sum(out_ref[...] * cot_ref[...].astype(F32), axis=1, keepdims=True)
-
-    sems = pltpu.SemaphoreType.DMA((2 * steps,))
-    return call(
-        body,
-        core,
-        [x, x_other, rstd, gain, key_matrix, value_matrix, cot],
-        (0, 1, 4, 5),
-        [
-            jax.ShapeDtypeStruct((tokens, 2 * kv), F32),
-            jax.ShapeDtypeStruct((tokens, 1), F32),
-        ],
-        8 * tokens * half * kv,
-        [
-            pltpu.VMEM((tokens, 2 * half), BF16),
-            pltpu.VMEM((2 * half, kv), BF16),
-            pltpu.VMEM((2 * half, kv), BF16),
-            sems,
-            sems,
-            sems,
-        ],
-    )
-
-
-def low_rank_down(core, x, rstd, gain, factors):
-    tokens, half = x.shape
-    steps = half // STEP
-
-    def body(core_ref, x_ref, rstd_ref, gain_ref, factors_ref, out_ref, xs, ours, x_sems, sems):
+    def body(core_ref, *rest):
+        x_refs, rest = rest[:parts], rest[parts:]
+        gain_ref, factors_ref, out_ref, held, ours, x_sems, sems = rest
         base = pl.multiple_of(core_ref[0] * half, half)
         copies = []
         for i in range(steps):
             copies.append(
                 [
                     pltpu.make_async_copy(
-                        x_ref.at[:, lanes_of(i)], xs.at[:, lanes_of(i)], x_sems.at[i]
+                        x_refs[i // within].at[:, lanes_of(i % within)],
+                        held.at[:, lanes_of(i)],
+                        x_sems.at[i],
                     ),
                     pltpu.make_async_copy(
                         factors_ref.at[pl.ds(base + i * STEP, STEP), :COLUMNS],
@@ -389,13 +403,11 @@
             )
             for copy in copies[i]:
                 copy.start()
-        rstd = rstd_ref[...]
         for i in range(steps):
             for copy in copies[i]:
                 copy.wait()
-            normed = xs[:, lanes_of(i)].astype(F32) * rstd
-            normed = (normed * gain_ref[:, pl.ds(base + i * STEP, STEP)]).astype(BF16)
-            product = dot(normed, ours[lanes_of(i)])
+            scaled = held[:, lanes_of(i)].astype(F32) * gain_ref[:, pl.ds(base + i * STEP, STEP)]
+            product = dot(scaled.astype(BF16), ours[lanes_of(i)])
             if i == 0:
                 out_ref[...] = product
             else:
@@ -405,8 +417,8 @@
     return call(
         body,
         core,
-        [x, rstd, gain, factors],
-        (0, 3),
+        [*xs, gain, factors],
+        tuple(range(parts)) + (parts + 1,),
         jax.ShapeDtypeStruct((tokens, COLUMNS), F32),
         2 * tokens * half * COLUMNS,
         [
@@ -415,6 +427,7 @@
             sems,
             sems,
         ],
+        limit=VMEM_LIMIT,
     )
 
 
@@ -423,47 +436,36 @@
     return jnp.where(jobs == (column & (FEATURE_WIDTH - 1)) // RANK, value, 0.0)
 
 
-def back_product(scalars, cot, ups):
+def back_product(core, cot, up):
     tokens, kv = cot.shape[0], cot.shape[1] // 2
-    rows = ups[0].shape[1]
-
-    def body(scalars_ref, cot_ref, *rest):
-        up_refs, (out_ref, up_ref, ordered) = rest[:SIDE], rest[SIDE:]
-        for down, ref in enumerate(up_refs):
-            z = lax.rem(scalars_ref[1] + SIDE - down, SIDE)
-            for left in range(SIDE):
-                y = lax.rem(scalars_ref[2] + SIDE - left, SIDE)
-                start = pl.multiple_of((z * SIDE + y) * rows, rows)
-                ordered[pl.ds(start, rows), :] = ref[left].astype(F32)
-        up_ref[...] = ordered[...].astype(BF16)
+
+    def body(core_ref, cot_ref, up_ref, out_ref):
         for side in range(2):
-            lanes = pl.ds(side * kv, kv)
+            lanes = lanes_of(side, kv)
             picked = columns_dot(cot_ref[:, lanes], up_ref[:, lanes])
             out_ref[:, side * FEATURE_WIDTH : (side + 1) * FEATURE_WIDTH] = picked
 
     return call(
         body,
-        scalars,
-        [cot, *ups],
+        core,
+        [cot, up],
         (),
-        [
-            jax.ShapeDtypeStruct((tokens, COLUMNS), F32),
-            jax.ShapeDtypeStruct((FEATURE_WIDTH, 2 * kv), BF16),
-        ],
+        jax.ShapeDtypeStruct((tokens, COLUMNS), F32),
         4 * tokens * kv * FEATURE_WIDTH,
-        [pltpu.VMEM((FEATURE_WIDTH, 2 * kv), F32)],
-    )
-
-
-def up_gradient(core, mine, other, jobs, cot, back):
+    )
+
+
+def up_gradient(core, mine, other, jobs, cot, back, sums, other_sums, width):
     tokens, kv = cot.shape[0], cot.shape[1] // 2
 
-    def body(core_ref, mine_ref, other_ref, jobs_ref, cot_ref, back_ref, *outs):
-        low_ref, out_ref, sum_ref = outs
-        total = masked(mine_ref[...] + other_ref[...], jobs_ref[...])
-        sum_ref[...] = ADAPTER_SCALING * jnp.sum(
-            total * back_ref[...].astype(F32), axis=1, keepdims=True
-        )
+    def body(core_ref, mine_ref, other_ref, jobs_ref, cot_ref, back_ref, *rest):
+        sums_ref, other_sums_ref, low_ref, out_ref, rstd_ref, mean_ref = rest
+        sums = sums_ref[...] + other_sums_ref[...]
+        rstd = lax.rsqrt(sums[:, :1] / width + 1e-05)
+        rstd_ref[...] = rstd
+        total = masked((mine_ref[...] + other_ref[...]) * rstd, jobs_ref[...])
+        low_products = jnp.sum(total * back_ref[...].astype(F32), axis=1, keepdims=True)
+        mean_ref[...] = (sums[:, 1:2] * rstd + ADAPTER_SCALING * low_products) / width
         low = total.astype(BF16)
         low_ref[...] = low
         for side in range(2):
@@ -471,34 +473,38 @@
             picked = low[:, side * FEATURE_WIDTH : (side + 1) * FEATURE_WIDTH]
             out_ref[:, lanes] = (ADAPTER_SCALING * rows_dot(picked, cot_ref[:, lanes])).astype(BF16)
 
-    return call(
-        body,
-        core,
-        [mine, other, jobs, cot, back],
+    column = jax.ShapeDtypeStruct((tokens, 1), F32)
+    return call(
+        body,
+        core,
+        [mine, other, jobs, cot, back, sums, other_sums],
         (),
         [
             jax.ShapeDtypeStruct((tokens, COLUMNS), BF16),
             jax.ShapeDtypeStruct((FEATURE_WIDTH, 2 * kv), BF16),
-            jax.ShapeDtypeStruct((tokens, 1), F32),
+            column,
+            column,
         ],
         4 * tokens * kv * FEATURE_WIDTH,
-    )
-
-
-def with_low_rank(core, frozen, low, up):
+        limit=FULL_LIMIT,
+    )
+
+
+def with_low_rank(core, frozen, low, up, rstd):
     tokens, kv = frozen.shape[0], frozen.shape[1] // 2
 
-    def body(core_ref, frozen_ref, low_ref, up_ref, out_ref):
+    def body(core_ref, frozen_ref, low_ref, up_ref, rstd_ref, out_ref):
         for side in range(2):
             lanes = lanes_of(side, kv)
             picked = low_ref[:, side * FEATURE_WIDTH : (side + 1) * FEATURE_WIDTH]
-            total = frozen_ref[:, lanes] + ADAPTER_SCALING * dot(picked, up_ref[:, lanes])
+            total = frozen_ref[:, lanes] * rstd_ref[...]
+            total += ADAPTER_SCALING * dot(picked, up_ref[:, lanes])
             out_ref[:, lanes] = total.astype(BF16)
 
     return call(
         body,
         core,
-        [frozen, low, up],
+        [frozen, low, up, rstd],
         (),
         jax.ShapeDtypeStruct(frozen.shape, BF16),
         4 * tokens * kv * FEATURE_WIDTH,
@@ -553,6 +559,7 @@
         2 * tokens * half * COLUMNS,
         [strip, pltpu.VMEM((half, COLUMNS), BF16), strip, strip, sems, sems, sems, sems],
         (0,),
+        VMEM_LIMIT,
     )
 
 
@@ -642,52 +649,60 @@
     jobs = row_jobs[0][:, None]
 
     factors = adapter_params[0, 0].astype(BF16)
-    factors_next = shifted(factors, "section", -1)
-    x_in = shifted(x_here, "section", 1)
-    gain_next = shifted(gain, "section", -1)
+    gain_high = gain.astype(BF16)
+    gain_low = (gain - gain_high.astype(F32)).astype(BF16)
+    gain_rows = width // COLUMNS
+    sent = [factors, gain_high.reshape(gain_rows, COLUMNS), gain_low.reshape(gain_rows, COLUMNS)]
+    sent = shifted(jnp.concatenate(sent, axis=0), "section", -1)
+    factors_next = sent[:block]
+    gain_next = sent[block : block + gain_rows].astype(F32) + sent[block + gain_rows :].astype(F32)
+    gain_next = gain_next.reshape(1, width)
+    part = half // PARTS
+    x_parts = [x_here[:, index * part : (index + 1) * part] for index in range(PARTS)]
+    x_in = [shifted(value, "section", 1) for value in x_parts]
+    up = right_params[0, 0].astype(BF16).reshape(1, -1, 2 * kv)
+    rows_local = up.shape[1]
+    up = lax.all_to_all(jnp.tile(up, (n_data, 1, 1)), "dp", 0, 0, tiled=True)
+    up = up.reshape(FEATURE_WIDTH, 2 * kv)
+
     both = lax.all_gather(
-        jnp.concatenate([factors, factors_next], axis=1), ("dp", "tensor"), axis=0, tiled=True
-    )
-
-    up_here = right_params[0, 0].astype(BF16).reshape(-1, 2 * kv)
-    rows_local = up_here.shape[0]
-    up_row = jnp.stack([up_here] + [shifted_y(up_here, step) for step in range(1, SIDE)])
-    ups = [up_row] + [shifted_z(up_row, step) for step in range(1, SIDE)]
-    spot = jnp.stack([core_index, place // SIDE, place % SIDE]).astype(jnp.int32)
-
-    leaving = frozen_back(after(core, up_row), cot, key_matrix, value_matrix, half)
-    received = swapped(leaving)
-
-    back_part, up = back_product(after(spot, leaving), cot, ups)
+        jnp.concatenate([factors, after(factors_next, *x_parts)], axis=1), ("dp", "tensor"), axis=0, tiled=True
+    )
+
+    leaving = frozen_back(core, cot, key_matrix, value_matrix, half)
+    received = [swapped(part) for part in leaving]
+
+    squares = jnp.sum(jnp.square(x_here.astype(F32)), axis=1, keepdims=True)
+    rstd = lax.rsqrt((squares + swapped(squares)) / width + 1e-05)
+
+    back_part = back_product(after(core, leaving[0]), cot, up)
+    kept, given = normed_by_parity(after(core, back_part), x_here, rstd, gain_next, block)
+    taken = swapped(given)
     back = masked(back_part + swapped(back_part), jobs).astype(BF16)
     back_next = shifted(back, "section", -1)
 
     scaled = frozen_back(
-        after(core, back), cot, key_matrix, value_matrix, half, received, gain
+        after(core, back, kept, x_in[0]), cot, key_matrix, value_matrix, half, received, gain
     )
     scaled_next = shifted(scaled, "section", -1)
 
-    x_wide = x_here.astype(F32)
-    squares = jnp.sum(x_wide * x_wide, axis=1, keepdims=True)
-    rstd = lax.rsqrt((squares + swapped(squares)) / width + 1e-05)
-    rstd_in = shifted(rstd, "section", 1)
-    kept, given = normed_by_parity(after(core, scaled), x_here, rstd, gain_next, block)
-    down_piece = down_gradient(core, kept, swapped(given), back_next, block)
+    down_piece = down_gradient(after(core, scaled), kept, taken, back_next, block)
     down_pieces = lax.all_to_all(down_piece, "dp", 0, 0, tiled=True)
 
-    x_in = after(x_in, down_piece)
-    frozen, products = projected(
-        core, x_in, swapped(x_in), rstd_in, gain, key_matrix, value_matrix, cot
-    )
-    low_part = low_rank_down(after(core, frozen), x_in, rstd_in, gain, both)
-    low, up_piece, low_products = up_gradient(
-        core, low_part, swapped(low_part), jobs, cot, back
+    x_other = [swapped(value) for value in x_in]
+    sources = (gain, key_matrix, value_matrix)
+    frozen = projected(after(core, down_piece), x_in[0], x_other[0], 0, half, *sources, cot)
+    frozen, sums = projected(core, x_in[1], x_other[1], part, half, *sources, cot, frozen)
+    low_part = low_rank_down(after(core, frozen), x_in, gain, both)
+    low, up_piece, rstd_in, mean = up_gradient(
+        core, low_part, swapped(low_part), jobs, cot, back, sums, swapped(sums), width
     )
     up_pieces = up_piece.reshape(n_data, rows_local, 2 * kv)
     up_pieces = lax.all_to_all(up_pieces, "dp", 0, 0, tiled=True)
-    mean = shifted((products + swapped(products) + low_products) / width, "section", -1)
-    down_sum = summed(after(core, up_piece), down_pieces)
-    kv_out = with_low_rank(after(core, down_sum), frozen, low, up)
+    mean = shifted(mean, "section", -1)
+    kv_out = with_low_rank(after(core, up_piece, scaled_next), frozen, low, up, rstd_in)
+    turn = swapped(kv_out[:16, :128])
+    down_sum = summed(after(core, turn), down_pieces)
     down_sum = shifted(down_sum, "section", 1)
 
     input_grad = norm_backward(
@@ -706,7 +721,7 @@
     row_count = jnp.sum(
         jnp.where(row_job[:, None] == job_ids[None, :], counts[None, :], 0.0), axis=1
     )
-    scalars = jnp.concatenate([after(core, input_grad), finishing.astype(jnp.int32)])
+    scalars = jnp.concatenate([after(core, input_grad, up_pieces), finishing.astype(jnp.int32)])
     new_a, chosen = down_optimizer(
         scalars, adapter_params[0], adapter_second[0], down_sum, column_total[None, :]
     )

time: 169 us -> 136 us (0.80)
  waiting for transfers between devices: 35.8 us -> 15 us
  Pallas kernels: 54.6 us -> 45.6 us
  other arithmetic: 7.82 us -> 4.35 us
    ppermute x16 -> x17, waiting for transfers between devices: 21.8 us -> 7.13 us  [shifted(): return lax.ppermute(value, axis, pairs)]
    ppermute x6 -> x0, starting transfers between devices: 10.9 us -> none  [the longest x3 5.81 us: shifted_z(): return lax.ppermute(value, 'dp', pairs)]
    pallas_call x12 -> x13, Pallas kernels: 54.6 us -> 45.6 us  [call(): pl.pallas_call(body, out_shape=out_shape, grid_spec=pltpu.PrefetchScalarG...]
    all_gather x1, waiting for transfers between devices: 0.02 us -> 7.84 us  [local(): lax.all_gather(jnp.concatenate([factors, after(factors_next, *x_parts)],...]
    all_to_all x0 -> x1, starting transfers between devices: none -> 7.77 us  [local(): up = lax.all_to_all(jnp.tile(up, (n_data, 1, 1)), 'dp', 0, 0, tiled=True)]
    all_to_all x1, waiting for transfers between devices: 6.91 us -> 0.01 us  [local(): up_pieces = lax.all_to_all(up_pieces, 'dp', 0, 0, tiled=True)]
    all_to_all x1, waiting for transfers between devices: 4.37 us -> 0.01 us  [local(): down_pieces = lax.all_to_all(down_piece, 'dp', 0, 0, tiled=True)]
    ppermute x6 -> x0, waiting for transfers between devices: 2.67 us -> none  [the longest x3 2.66 us: shifted_z(): return lax.ppermute(value, 'dp', pairs)]
  transfers between devices with their start and end apart: 25 -> 21, of which waited for: 10 -> 4; matrix products, arithmetic and copies ran while one was open for 7% -> 7% of each run, Pallas kernels for 31% -> 32%
where the time goes in v1:
time: 136 us; the launch traced here: 135 us
  Pallas kernels  45.6 us (34%)
  starting transfers between devices  40.6 us (30%)
  between operations  15.2 us (11%)
  waiting for transfers between devices  15 us (11%)
  local copies, waits for them, and re-layouts  14.7 us (11%)
  other arithmetic  4.35 us (3%)
    pallas_call x13, Pallas kernels, call(): pl.pallas_call(body, out_shape=out_shape, grid_spec=pltpu.PrefetchScalarG...  45.6 us
    ppermute x17, starting transfers between devices, shifted(): return lax.ppermute(value, axis, pairs)  18 us
    all_to_all x1, starting transfers between devices, local(): up_pieces = lax.all_to_all(up_pieces, 'dp', 0, 0, tiled=True)  7.86 us
    all_gather x1, waiting for transfers between devices, local(): lax.all_gather(jnp.concatenate([factors, after(factors_next, *x_parts)],...  7.84 us
    all_to_all x1, starting transfers between devices, local(): up = lax.all_to_all(jnp.tile(up, (n_data, 1, 1)), 'dp', 0, 0, tiled=True)  7.77 us
    unnamed x52, local copies, waits for them, and re-layouts  7.51 us
    ppermute x17, waiting for transfers between devices, shifted(): return lax.ppermute(value, axis, pairs)  7.13 us
    all_to_all x1, starting transfers between devices, local(): down_pieces = lax.all_to_all(down_piece, 'dp', 0, 0, tiled=True)  6.93 us
  transfers between devices with their start and end apart: 21, of which 4 were waited for; matrix products, arithmetic and copies ran while one was open for 7% of the time, Pallas kernels for 32%

profile of v1, /device:TPU:1, one launch (start us, length us, event | category | flops | bytes accessed | tf_op | source)
XLA Modules:
  0.0 135.3 jit_solution(16003232821887349068)
XLA Ops:
  7.2 1.0 fusion
  8.2 1.0 convert_reduce_fusion.2
  9.2 3.4 %collective-permute-start.4 = (bf16[320,256]{1,0:T(8,128)(2,1)S(1)}, bf16[320,256]{1,0:T(8,128)(2,1)S(1)}, u32[]{:S(2)}, u32[]{:S(2)}) collective-permute-start(bf16[320,256]{1,0:T(8,128)(2,1)S(1)} %pad_maximum_fusion.1), channel_id=1, source_target_pairs={{0,96},{32,0},{64,32},{96,64},{1,97},{33,1},{65,33},{97,65},{2,98}... | collective-permute-start | bytes 491528 | tf_op jit(solution)/shard_map/ppermute | solution.py:34
  12.6 3.3 %fusion.5 = (bf16[256,2048]{1,0:T(8,128)(2,1)}, bf16[256,2048]{1,0:T(8,128)(2,1)}) fusion(bf16[256,4096]{1,0:T(8,128)(2,1)} %bitcast.37), kind=kLoop, calls=%fused_computation.44 | loop fusion | bytes 4194304 | tf_op jit(solution)/shard_map/slice | solution.py:661
  15.9 0.7 pad_maximum_fusion
  16.6 0.6 collective-permute-start.5
  17.3 0.7 tile.2
  18.0 7.8 %all-to-all-start = ((bf16[16,8,1024]{2,1,0:T(8,128)(2,1)}), bf16[16,8,1024]{2,1,0:T(8,128)(2,1)S(1)}, u32[]{:S(2)}, u32[]{:S(2)}) async-start(bf16[16,8,1024]{2,1,0:T(8,128)(2,1)} %tile.2), calls=%async_computation | async-start | bytes 524288 | tf_op jit(solution)/shard_map/all_to_all | solution.py:665
  25.8 0.5 multiply_reduce_fusion
  26.3 2.2 %collective-permute-start.3 = (f32[256,1]{0,1:T(1,128)S(1)}, f32[256,1]{0,1:T(1,128)S(1)}, u32[]{:S(2)}, u32[]{:S(2)}) collective-permute-start(f32[256,1]{0,1:T(1,128)S(1)} %bitcast.66), channel_id=1, source_target_pairs={{0,1},{1,0},{2,3},{3,2},{4,5},{5,4},{6,7},{7,6},{8,9},{9,8},{10,11... | collective-permute-start | bytes 3080 | tf_op jit(solution)/shard_map/ppermute | solution.py:34
  28.5 0.9 copy.27
  29.4 6.6 %shard_map.155 = (bf16[256,2048]{1,0:T(8,128)(2,1)}, bf16[256,2048]{1,0:T(8,128)(2,1)}) custom-call(s32[1]{0:T(128)} %bitcast.core_ref, bf16[256,1024]{1,0:T(8,128)(2,1)} %bitcast.40, bf16[8192,512]{1,0:T(8,128)(2,1)} %bitcast.52, bf16[8192,512]{1,0:T(8,128)(2,1)} %bitcast.56), custom_call_target="tpu_custom_call" | custom-call | flops 134217728 | bytes 1212416 | tf_op jit(solution)/shard_map/pallas_call | solution.py:82
  36.1 0.5 collective-permute-start.7
  37.2 1.5 %shard_map.157 = (bf16[256,2048]{1,0:T(8,128)(2,1)S(1)}, bf16[256,2048]{1,0:T(8,128)(2,1)S(1)}) custom-call(s32[1]{0:T(128)} %bitcast.core_ref, bf16[256,4096]{1,0:T(8,128)(2,1)S(1)} %bitcast.39, f32[256,1]{1,0:T(8,128)S(1)} %rsqrt.3.rstd_ref.rest_0_, f32[1,8192]{1,0:T(1,128)S(1)} %bitcast.48), custom_call_target="tpu_custom_call" | custom-call | flops 65536 | bytes 264256 | tf_op jit(solution)/shard_map/pallas_call | solution.py:82
  38.9 0.4 collective-permute-start.2
  39.3 2.8 %collective-permute-done.2 = f32[256,256]{1,0:T(8,128)S(1)} collective-permute-done((f32[256,256]{1,0:T(8,128)S(1)}, f32[256,256]{1,0:T(8,128)S(1)}, u32[]{:S(2)}, u32[]{:S(2)}) %collective-permute-start.2) | collective-permute-done | bytes 262176 | tf_op jit(solution)/shard_map/ppermute | solution.py:34
  42.1 1.2 collective-permute-start
  43.5 1.6 %collective-permute-start.9 = (bf16[256,256]{1,0:T(8,128)(2,1)S(1)}, bf16[256,256]{1,0:T(8,128)(2,1)S(1)}, u32[]{:S(2)}, u32[]{:S(2)}) collective-permute-start(bf16[256,256]{1,0:T(8,128)(2,1)S(1)} %select_convert_fusion.back_ref), channel_id=1, source_target_pairs={{0,96},{32,0},{64,32},{96,64},{1,97},{33,1},{65,33},{97,65},{2,98}... | collective-permute-start | bytes 393224 | tf_op jit(solution)/shard_map/ppermute | solution.py:34
  45.0 7.0 %shard_map.158 = bf16[256,4096]{1,0:T(8,128)(2,1)} custom-call(s32[1]{0:T(128)} %bitcast.core_ref, bf16[256,1024]{1,0:T(8,128)(2,1)} %bitcast.41, bf16[8192,512]{1,0:T(8,128)(2,1)} %bitcast.53, bf16[8192,512]{1,0:T(8,128)(2,1)} %bitcast.57, bf16[256,2048]{1,0:T(8,128)(2,1)} %collective-permute-done.6.rest_0_, ...), custom_call_target="tpu_custom_call" | custom-call | flops 134217728 | bytes 1345536 | tf_op jit(solution)/shard_map/pallas_call | solution.py:82
  52.1 1.7 %shard_map.159 = bf16[16,256,256]{2,1,0:T(8,128)(2,1)S(1)} custom-call(s32[1]{0:T(128)} %bitcast.core_ref, bf16[256,2048]{1,0:T(8,128)(2,1)S(1)} %get-tuple-element.32.kept_ref, bf16[256,2048]{1,0:T(8,128)(2,1)S(1)} %collective-permute-done.8.taken_ref, bf16[256,256]{1,0:T(8,128)(2,1)S(1)} %collective-permute-done.9.back_ref), custom_call_target="tpu_custom_call" | custom-call | flops 33554432 | bytes 270336 | tf_op jit(solution)/shard_map/pallas_call | solution.py:82
  53.7 1.4 %copy-done.2 = bf16[16,256,256]{2,1,0:T(8,128)(2,1)} copy-done((bf16[16,256,256]{2,1,0:T(8,128)(2,1)}, bf16[16,256,256]{2,1,0:T(8,128)(2,1)S(1)}, u32[]{:S(2)}) %copy-start.2) | copy-done | bytes 2097176
  55.1 6.9 %all-to-all-start.2 = ((bf16[16,256,256]{2,1,0:T(8,128)(2,1)}), bf16[16,256,256]{2,1,0:T(8,128)(2,1)S(1)}, u32[]{:S(2)}, u32[]{:S(2)}) async-start(bf16[16,256,256]{2,1,0:T(8,128)(2,1)} %copy-done.2), calls=%async_computation.2 | async-start | bytes 4194304 | tf_op jit(solution)/shard_map/all_to_all | solution.py:690
  62.1 1.2 collective-permute-start.13
  63.3 1.1 collective-permute-start.10
  64.4 3.9 %collective-permute-done.own_ref.rest_1_ = bf16[256,2048]{1,0:T(8,128)(2,1)} collective-permute-done((bf16[256,2048]{1,0:T(8,128)(2,1)}, bf16[256,2048]{1,0:T(8,128)(2,1)}, u32[]{:S(2)}, u32[]{:S(2)}) %collective-permute-start) | collective-permute-done | bytes 1048608 | tf_op jit(solution)/shard_map/ppermute | solution.py:34
  68.3 1.0 collective-permute-start.1
  69.2 1.0 copy-done.12
  70.2 6.6 %shard_map.160 = (f32[256,1024]{1,0:T(8,128)}, f32[256,128]{1,0:T(8,128)}) custom-call(s32[1]{0:T(128)} %bitcast.core_ref, bf16[256,2048]{1,0:T(8,128)(2,1)} %collective-permute-done.5.own_ref.rest_0_, bf16[256,2048]{1,0:T(8,128)(2,1)} %copy-done.12, f32[1,8192]{1,0:T(1,128)} %rest_2_.3, bf16[8192,512]{1,0:T(8,128)(2,1)} %bitcast.54, bf16[8192,512]{1,0:T(8,128)(2,1)} %bitcast.58), custom_call_target="tpu_custom_call" | custom-call | flops 134217728 | bytes 1255424 | tf_op jit(solution)/shard_map/pallas_call | solution.py:82
  76.8 1.0 copy-done.11
  77.8 7.3 %shard_map.161 = (f32[256,1024]{1,0:T(8,128)}, f32[256,128]{1,0:T(8,128)}) custom-call(s32[1]{0:T(128)} %bitcast.core_ref, bf16[256,2048]{1,0:T(8,128)(2,1)} %collective-permute-done.own_ref.rest_1_, bf16[256,2048]{1,0:T(8,128)(2,1)} %copy-done.11, f32[1,8192]{1,0:T(1,128)} %rest_2_.3, bf16[8192,512]{1,0:T(8,128)(2,1)} %bitcast.55, ...), custom_call_target="tpu_custom_call" | custom-call | flops 134217728 | bytes 1361920 | tf_op jit(solution)/shard_map/pallas_call | solution.py:82
  85.1 7.8 %all-gather.2.cloned.1.call-done.rest_3_.factors_ref = bf16[8192,512]{1,0:T(8,128)(2,1)} async-done(((bf16[256,512]{1,0:T(8,128)(2,1)}), bf16[8192,512]{1,0:T(8,128)(2,1)}) %all-gather.2.cloned.1.call-update) | async-done | bytes 8388624 | tf_op jit(solution)/shard_map/all_gather | solution.py:668
  93.0 4.2 %shard_map.162.mine_ref = f32[256,256]{1,0:T(8,128)} custom-call(s32[1]{0:T(128)} %bitcast.core_ref, bf16[256,2048]{1,0:T(8,128)(2,1)} %collective-permute-done.5.own_ref.rest_0_, bf16[256,2048]{1,0:T(8,128)(2,1)} %collective-permute-done.own_ref.rest_1_, f32[1,8192]{1,0:T(1,128)} %rest_2_.3, bf16[8192,512]{1,0:T(8,128)(2,1)} %all-gather.2.cloned.1.call-done.rest_3_.factors_ref), custom_call_target="tpu_custom_call" | custom-call | flops 33554432 | bytes 673792 | tf_op jit(solution)/shard_map/pallas_call | solution.py:82
  97.8 0.8 copy.26.jobs_ref
  99.0 0.6 copy-done.18
  99.6 0.7 copy-done.15
  100.3 2.5 %shard_map.163 = (bf16[256,256]{1,0:T(8,128)(2,1)}, bf16[128,1024]{1,0:T(8,128)(2,1)}, f32[256,1]{1,0:T(8,128)}, f32[256,1]{1,0:T(8,128)}) custom-call(s32[1]{0:T(128)} %bitcast.core_ref, f32[256,256]{1,0:T(8,128)} %shard_map.162.mine_ref, f32[256,256]{1,0:T(8,128)} %copy-done.15, s32[256,1]{1,0:T(8,128)} %copy.26.jobs_ref, bf16[256,1024]{1,0:T(8,128)(2,1)} %bitcast.43, ...), custom_call_target="tpu_custom_call" | custom-call | flops 4194304 | bytes 114880 | tf_op jit(solution)/shard_map/pallas_call | solution.py:82
  102.9 7.9 %all-to-all-start.1 = ((bf16[16,8,1024]{2,1,0:T(8,128)(2,1)}), bf16[16,8,1024]{2,1,0:T(8,128)(2,1)S(1)}, u32[]{:S(2)}, u32[]{:S(2)}) async-start(bf16[16,8,1024]{2,1,0:T(8,128)(2,1)} %bitcast.62), calls=%async_computation.1 | async-start | bytes 524288 | tf_op jit(solution)/shard_map/all_to_all | solution.py:701
  110.8 0.5 shard_map.166
  111.3 1.4 %collective-permute-start.15 = (bf16[256,256]{1,0:T(8,128)(2,1)S(1)}, bf16[256,256]{1,0:T(8,128)(2,1)S(1)}, u32[]{:S(2)}, u32[]{:S(2)}) collective-permute-start(bf16[256,256]{1,0:T(8,128)(2,1)S(1)} %shard_map.166), channel_id=1, source_target_pairs={{0,32},{32,64},{64,96},{96,0},{1,33},{33,65},{65,97},{97,1},{2,34}... | collective-permute-start | bytes 393224 | tf_op jit(solution)/shard_map/ppermute | solution.py:34
  112.9 1.4 %collective-permute-start.14 = (f32[256,1]{1,0:T(8,128)S(1)}, f32[256,1]{1,0:T(8,128)S(1)}, u32[]{:S(2)}, u32[]{:S(2)}) collective-permute-start(f32[256,1]{1,0:T(8,128)S(1)} %copy-done.22), channel_id=1, source_target_pairs={{0,96},{32,0},{64,32},{96,64},{1,97},{33,1},{65,33},{97,65},{2,98}... | collective-permute-start | bytes 3080 | tf_op jit(solution)/shard_map/ppermute | solution.py:34
  115.0 1.2 copy-done.4
  116.5 1.2 reshape.140
  117.7 0.6 copy-done.16
  118.4 5.4 %shard_map.165 = bf16[256,4096]{1,0:T(8,128)(2,1)} custom-call(s32[1]{0:T(128)} %bitcast.core_ref, bf16[256,4096]{1,0:T(8,128)(2,1)} %collective-permute-done.13.scaled_ref, bf16[256,256]{1,0:T(8,128)(2,1)} %copy-done.6, bf16[8192,512]{1,0:T(8,128)(2,1)} %all-gather.2.cloned.1.call-done.rest_3_.factors_ref, f32[1,8192]{1,0:T(1,128)} %bitcast.49, ...), custom_call_target="tpu_custom_call" | custom-call | flops 33554432 | bytes 927872 | tf_op jit(solution)/shard_map/pallas_call | solution.py:82
  123.9 1.7 %shard_map.167 = (f32[3,256,256]{2,1,0:T(8,128)}, f32[3,32,256]{2,1,0:T(8,128)S(1)}) custom-call(s32[2]{0:T(128)S(1)} %pad_add_fusion.scalars_ref, f32[2,256,256]{2,1,0:T(8,128)S(1)} %bitcast.47, f32[256,256]{1,0:T(8,128)S(1)} %bitcast.50, bf16[256,256]{1,0:T(8,128)(2,1)S(1)} %collective-permute-done.15.grad_ref, f32[1,256]{1,0:T(1,128)S(1)} %bitcast.51), custom_call_target="tpu_custom_call" | custom-call | flops 81920 | bytes 112704 | tf_op jit(solution)/shard_map/pallas_call | solution.py:82
  125.6 1.2 collective-permute-start.16
  127.1 0.7 maximum_bitcast_fusion.1
  127.8 0.7 maximum_bitcast_fusion
  (91 shorter events, 3.1 us)
Async XLA Ops:
  7.2 85.8 %all-gather.2.cloned.1.call-start = ((), (), s32[]{:S(2)}) async-start(), calls=%async_computation.3 | async-start | bytes 8650752 | tf_op jit(solution)/shard_map/all_gather | solution.py:668
  9.2 6.6 %collective-permute-start.4 = (bf16[320,256]{1,0:T(8,128)(2,1)S(1)}, bf16[320,256]{1,0:T(8,128)(2,1)S(1)}, u32[]{:S(2)}, u32[]{:S(2)}) collective-permute-start(bf16[320,256]{1,0:T(8,128)(2,1)S(1)} %pad_maximum_fusion.1), channel_id=1, source_target_pairs={{0,96},{32,0},{64,32},{96,64},{1,97},{33,1},{65,33},{97,65},{2,98}... | collective-permute-start | bytes 491528 | tf_op jit(solution)/shard_map/ppermute | solution.py:34
  12.6 4.6 %copy-start.19 = (f32[1,2,8,2,512]{4,3,2,1,0:T(2,128)S(1)}, f32[1,2,8,2,512]{4,3,2,1,0:T(2,128)}, u32[]{:S(2)}) copy-start(f32[1,2,8,2,512]{4,3,2,1,0:T(2,128)} %param.18) | copy-start | bytes 196612
  12.6 13.2 %copy-start = (bf16[1,256,4096]{2,1,0:T(8,128)(2,1)S(1)}, bf16[1,256,4096]{2,1,0:T(8,128)(2,1)}, u32[]{:S(2)}) copy-start(bf16[1,256,4096]{2,1,0:T(8,128)(2,1)} %param.12) | copy-start | bytes 6291460
  15.9 12.6 %copy-start.13 = (bf16[1,256,2,512]{3,2,1,0:T(2,128)(2,1)S(1)}, bf16[1,256,2,512]{3,2,1,0:T(2,128)(2,1)}, u32[]{:S(2)}) copy-start(bf16[1,256,2,512]{3,2,1,0:T(2,128)(2,1)} %param.23) | copy-start | bytes 1572868
  16.6 26.8 %collective-permute-start.5 = (bf16[256,2048]{1,0:T(8,128)(2,1)}, bf16[256,2048]{1,0:T(8,128)(2,1)}, u32[]{:S(2)}, u32[]{:S(2)}) collective-permute-start(bf16[256,2048]{1,0:T(8,128)(2,1)} %get-tuple-element.58), channel_id=1, source_target_pairs={{0,32},{32,64},{64,96},{96,0},{1,33},{33,65},{65,97},{97,1},{2,34}... | collective-permute-start | bytes 3145736 | tf_op jit(solution)/shard_map/ppermute | solution.py:34
  18.0 18.9 %all-to-all-start = ((bf16[16,8,1024]{2,1,0:T(8,128)(2,1)}), bf16[16,8,1024]{2,1,0:T(8,128)(2,1)S(1)}, u32[]{:S(2)}, u32[]{:S(2)}) async-start(bf16[16,8,1024]{2,1,0:T(8,128)(2,1)} %tile.2), calls=%async_computation | async-start | bytes 524288 | tf_op jit(solution)/shard_map/all_to_all | solution.py:665
  26.3 10.3 %collective-permute-start.3 = (f32[256,1]{0,1:T(1,128)S(1)}, f32[256,1]{0,1:T(1,128)S(1)}, u32[]{:S(2)}, u32[]{:S(2)}) collective-permute-start(f32[256,1]{0,1:T(1,128)S(1)} %bitcast.66), channel_id=1, source_target_pairs={{0,1},{1,0},{2,3},{3,2},{4,5},{5,4},{6,7},{7,6},{8,9},{9,8},{10,11... | collective-permute-start | bytes 3080 | tf_op jit(solution)/shard_map/ppermute | solution.py:34
  29.4 7.5 %copy-start.1 = (bf16[32,8,2,512]{3,1,2,0:T(8,128)(2,1)S(1)}, bf16[32,8,2,512]{3,1,2,0:T(8,128)(2,1)}, u32[]{:S(2)}) copy-start(bf16[32,8,2,512]{3,1,2,0:T(8,128)(2,1)} %copy.27) | copy-start | bytes 1572868
  36.0 7.3 %copy-start.21 = (s32[1,256]{1,0:T(1,128)S(1)}, s32[1,256]{1,0:T(1,128)}, u32[]{:S(2)}) copy-start(s32[1,256]{1,0:T(1,128)} %param.20) | copy-start | bytes 3076
  36.0 9.0 %collective-permute-start.6 = (bf16[256,2048]{1,0:T(8,128)(2,1)}, bf16[256,2048]{1,0:T(8,128)(2,1)}, u32[]{:S(2)}, u32[]{:S(2)}) collective-permute-start(bf16[256,2048]{1,0:T(8,128)(2,1)} %get-tuple-element.29), channel_id=1, source_target_pairs={{0,1},{1,0},{2,3},{3,2},{4,5},{5,4},{6,7},{7,6},{8,9},{9,8},{10,11... | collective-permute-start | bytes 3145736 | tf_op jit(solution)/shard_map/ppermute | solution.py:34
  36.1 8.9 %collective-permute-start.7 = (bf16[256,2048]{1,0:T(8,128)(2,1)}, bf16[256,2048]{1,0:T(8,128)(2,1)}, u32[]{:S(2)}, u32[]{:S(2)}) collective-permute-start(bf16[256,2048]{1,0:T(8,128)(2,1)} %get-tuple-element.34), channel_id=1, source_target_pairs={{0,1},{1,0},{2,3},{3,2},{4,5},{5,4},{6,7},{7,6},{8,9},{9,8},{10,11... | collective-permute-start | bytes 3145736 | tf_op jit(solution)/shard_map/ppermute | solution.py:34
  36.8 15.2 %copy-start.3 = (f32[256,1]{1,0:T(8,128)}, f32[256,1]{1,0:T(8,128)S(1)}, u32[]{:S(2)}) copy-start(f32[256,1]{1,0:T(8,128)S(1)} %rsqrt.3.rstd_ref.rest_0_) | copy-start | bytes 3076
  36.9 15.1 %copy-start.7 = (f32[1,1,32,256]{3,1,2,0:T(1,128)}, f32[1,1,32,256]{3,1,2,0:T(1,128)S(1)}, u32[]{:S(2)}) copy-start(f32[1,1,32,256]{3,1,2,0:T(1,128)S(1)} %copy.29) | copy-start | bytes 98308
  38.7 13.3 %collective-permute-start.8 = (bf16[256,2048]{1,0:T(8,128)(2,1)S(1)}, bf16[256,2048]{1,0:T(8,128)(2,1)S(1)}, u32[]{:S(2)}, u32[]{:S(2)}) collective-permute-start(bf16[256,2048]{1,0:T(8,128)(2,1)S(1)} %get-tuple-element.36), channel_id=1, source_target_pairs={{0,1},{1,0},{2,3},{3,2},{4,5},{5,4},{6,7},{7,6},{8,9},{9,8},{10,11... | collective-permute-start | bytes 3145736 | tf_op jit(solution)/shard_map/ppermute | solution.py:34
  38.9 3.2 %collective-permute-start.2 = (f32[256,256]{1,0:T(8,128)S(1)}, f32[256,256]{1,0:T(8,128)S(1)}, u32[]{:S(2)}, u32[]{:S(2)}) collective-permute-start(f32[256,256]{1,0:T(8,128)S(1)} %shard_map.156), channel_id=1, source_target_pairs={{0,1},{1,0},{2,3},{3,2},{4,5},{5,4},{6,7},{7,6},{8,9},{9,8},{10,11... | collective-permute-start | bytes 786440 | tf_op jit(solution)/shard_map/ppermute | solution.py:34
  42.1 26.1 %collective-permute-start = (bf16[256,2048]{1,0:T(8,128)(2,1)}, bf16[256,2048]{1,0:T(8,128)(2,1)}, u32[]{:S(2)}, u32[]{:S(2)}) collective-permute-start(bf16[256,2048]{1,0:T(8,128)(2,1)} %get-tuple-element.59), channel_id=1, source_target_pairs={{0,32},{32,64},{64,96},{96,0},{1,33},{33,65},{65,97},{97,1},{2,34}... | collective-permute-start | bytes 3145736 | tf_op jit(solution)/shard_map/ppermute | solution.py:34
  43.4 8.6 %copy-start.14 = (bf16[256,256]{1,0:T(8,128)(2,1)}, bf16[256,256]{1,0:T(8,128)(2,1)S(1)}, u32[]{:S(2)}) copy-start(bf16[256,256]{1,0:T(8,128)(2,1)S(1)} %select_convert_fusion.back_ref) | copy-start | bytes 393220
  43.5 8.6 %collective-permute-start.9 = (bf16[256,256]{1,0:T(8,128)(2,1)S(1)}, bf16[256,256]{1,0:T(8,128)(2,1)S(1)}, u32[]{:S(2)}, u32[]{:S(2)}) collective-permute-start(bf16[256,256]{1,0:T(8,128)(2,1)S(1)} %select_convert_fusion.back_ref), channel_id=1, source_target_pairs={{0,96},{32,0},{64,32},{96,64},{1,97},{33,1},{65,33},{97,65},{2,98}... | collective-permute-start | bytes 393224 | tf_op jit(solution)/shard_map/ppermute | solution.py:34
  52.0 1.7 %copy-start.6 = (bf16[256,256]{1,0:T(8,128)(2,1)}, bf16[256,256]{1,0:T(8,128)(2,1)S(1)}, u32[]{:S(2)}) copy-start(bf16[256,256]{1,0:T(8,128)(2,1)S(1)} %collective-permute-done.9.back_ref) | copy-start | bytes 393220
  53.7 1.4 %copy-start.2 = (bf16[16,256,256]{2,1,0:T(8,128)(2,1)}, bf16[16,256,256]{2,1,0:T(8,128)(2,1)S(1)}, u32[]{:S(2)}) copy-start(bf16[16,256,256]{2,1,0:T(8,128)(2,1)S(1)} %shard_map.159) | copy-start | bytes 6291460
  55.1 47.8 %all-to-all-start.2 = ((bf16[16,256,256]{2,1,0:T(8,128)(2,1)}), bf16[16,256,256]{2,1,0:T(8,128)(2,1)S(1)}, u32[]{:S(2)}, u32[]{:S(2)}) async-start(bf16[16,256,256]{2,1,0:T(8,128)(2,1)} %copy-done.2), calls=%async_computation.2 | async-start | bytes 4194304 | tf_op jit(solution)/shard_map/all_to_all | solution.py:690
  62.1 52.9 %collective-permute-start.13 = (bf16[256,4096]{1,0:T(8,128)(2,1)}, bf16[256,4096]{1,0:T(8,128)(2,1)}, u32[]{:S(2)}, u32[]{:S(2)}) collective-permute-start(bf16[256,4096]{1,0:T(8,128)(2,1)} %shard_map.158), channel_id=1, source_target_pairs={{0,96},{32,0},{64,32},{96,64},{1,97},{33,1},{65,33},{97,65},{2,98}... | collective-permute-start | bytes 6291464 | tf_op jit(solution)/shard_map/ppermute | solution.py:34
  63.3 5.9 %collective-permute-start.10 = (bf16[256,2048]{1,0:T(8,128)(2,1)}, bf16[256,2048]{1,0:T(8,128)(2,1)S(1)}, u32[]{:S(2)}, u32[]{:S(2)}) collective-permute-start(bf16[256,2048]{1,0:T(8,128)(2,1)} %collective-permute-done.5.own_ref.rest_0_), channel_id=1, source_target_pairs={{0,1},{1,0},{2,3},{3,2},{4,5},{5,4},{6,7},{7,6},{8,9},{9,8},{10,11... | collective-permute-start | bytes 3145736 | tf_op jit(solution)/shard_map/ppermute | solution.py:34
  68.3 8.5 %collective-permute-start.1 = (bf16[256,2048]{1,0:T(8,128)(2,1)}, bf16[256,2048]{1,0:T(8,128)(2,1)S(1)}, u32[]{:S(2)}, u32[]{:S(2)}) collective-permute-start(bf16[256,2048]{1,0:T(8,128)(2,1)} %collective-permute-done.own_ref.rest_1_), channel_id=1, source_target_pairs={{0,1},{1,0},{2,3},{3,2},{4,5},{5,4},{6,7},{7,6},{8,9},{9,8},{10,11... | collective-permute-start | bytes 3145736 | tf_op jit(solution)/shard_map/ppermute | solution.py:34
  69.2 1.0 copy-start.12
  76.8 1.0 copy-start.11
  85.1 12.4 %copy-start.17 = (f32[256,128]{1,0:T(8,128)S(1)}, f32[256,128]{1,0:T(8,128)}, u32[]{:S(2)}) copy-start(f32[256,128]{1,0:T(8,128)} %get-tuple-element.43.rest_0_) | copy-start | bytes 393220
  85.1 13.5 %copy-start.23 = (s32[8]{0:T(128)S(1)}, s32[8]{0:T(128)}, u32[]{:S(2)}) copy-start(s32[8]{0:T(128)} %param.21) | copy-start | bytes 100
  97.2 1.8 %collective-permute-start.11 = (f32[256,256]{1,0:T(8,128)}, f32[256,256]{1,0:T(8,128)S(1)}, u32[]{:S(2)}, u32[]{:S(2)}) collective-permute-start(f32[256,256]{1,0:T(8,128)} %shard_map.162.mine_ref), channel_id=1, source_target_pairs={{0,1},{1,0},{2,3},{3,2},{4,5},{5,4},{6,7},{7,6},{8,9},{9,8},{10,11... | collective-permute-start | bytes 786440 | tf_op jit(solution)/shard_map/ppermute | solution.py:34
  97.5 1.5 %collective-permute-start.12 = (f32[256,128]{1,0:T(8,128)S(1)}, f32[256,128]{1,0:T(8,128)S(1)}, u32[]{:S(2)}, u32[]{:S(2)}) collective-permute-start(f32[256,128]{1,0:T(8,128)S(1)} %copy-done.17), channel_id=1, source_target_pairs={{0,1},{1,0},{2,3},{3,2},{4,5},{5,4},{6,7},{7,6},{8,9},{9,8},{10,11... | collective-permute-start | bytes 393224 | tf_op jit(solution)/shard_map/ppermute | solution.py:34
  99.0 0.6 copy-start.18
  99.6 0.7 copy-start.15
  102.9 10.1 %copy-start.22 = (f32[256,1]{1,0:T(8,128)S(1)}, f32[256,1]{1,0:T(8,128)}, u32[]{:S(2)}) copy-start(f32[256,1]{1,0:T(8,128)} %get-tuple-element.49) | copy-start | bytes 3076
  102.9 12.1 %copy-start.9 = (bf16[256,256]{1,0:T(8,128)(2,1)S(1)}, bf16[256,256]{1,0:T(8,128)(2,1)}, u32[]{:S(2)}) copy-start(bf16[256,256]{1,0:T(8,128)(2,1)} %get-tuple-element.46.low_ref) | copy-start | bytes 393220
  102.9 12.1 %copy-start.10 = (f32[256,1]{1,0:T(8,128)S(1)}, f32[256,1]{1,0:T(8,128)}, u32[]{:S(2)}) copy-start(f32[256,1]{1,0:T(8,128)} %get-tuple-element.47.rstd_ref) | copy-start | bytes 3076
  102.9 20.9 %all-to-all-start.1 = ((bf16[16,8,1024]{2,1,0:T(8,128)(2,1)}), bf16[16,8,1024]{2,1,0:T(8,128)(2,1)S(1)}, u32[]{:S(2)}, u32[]{:S(2)}) async-start(bf16[16,8,1024]{2,1,0:T(8,128)(2,1)} %bitcast.62), calls=%async_computation.1 | async-start | bytes 524288 | tf_op jit(solution)/shard_map/all_to_all | solution.py:701
  111.3 12.5 %collective-permute-start.15 = (bf16[256,256]{1,0:T(8,128)(2,1)S(1)}, bf16[256,256]{1,0:T(8,128)(2,1)S(1)}, u32[]{:S(2)}, u32[]{:S(2)}) collective-permute-start(bf16[256,256]{1,0:T(8,128)(2,1)S(1)} %shard_map.166), channel_id=1, source_target_pairs={{0,32},{32,64},{64,96},{96,0},{1,33},{33,65},{65,97},{97,1},{2,34}... | collective-permute-start | bytes 393224 | tf_op jit(solution)/shard_map/ppermute | solution.py:34
  112.9 4.8 %collective-permute-start.14 = (f32[256,1]{1,0:T(8,128)S(1)}, f32[256,1]{1,0:T(8,128)S(1)}, u32[]{:S(2)}, u32[]{:S(2)}) collective-permute-start(f32[256,1]{1,0:T(8,128)S(1)} %copy-done.22), channel_id=1, source_target_pairs={{0,96},{32,0},{64,32},{96,64},{1,97},{33,1},{65,33},{97,65},{2,98}... | collective-permute-start | bytes 3080 | tf_op jit(solution)/shard_map/ppermute | solution.py:34
  115.0 1.2 copy-start.4
  117.7 6.1 %copy-start.5 = (f32[1,2,256,256]{3,2,1,0:T(8,128)S(1)}, f32[1,2,256,256]{3,2,1,0:T(8,128)}, u32[]{:S(2)}) copy-start(f32[1,2,256,256]{3,2,1,0:T(8,128)} %param.16) | copy-start | bytes 1572868
  117.7 6.2 %copy-start.8 = (f32[1,256,256]{2,1,0:T(8,128)S(1)}, f32[1,256,256]{2,1,0:T(8,128)}, u32[]{:S(2)}) copy-start(f32[1,256,256]{2,1,0:T(8,128)} %param.17) | copy-start | bytes 786436
  117.7 9.2 %copy-start.20 = (f32[1,8,2,512]{3,2,1,0:T(2,128)S(1)}, f32[1,8,2,512]{3,2,1,0:T(2,128)}, u32[]{:S(2)}) copy-start(f32[1,8,2,512]{3,2,1,0:T(2,128)} %param.19) | copy-start | bytes 98308
  117.7 0.7 copy-start.16
  125.6 2.1 %collective-permute-start.16 = (f32[3,32,256]{2,1,0:T(8,128)S(1)}, f32[3,32,256]{2,1,0:T(8,128)S(1)}, u32[]{:S(2)}, u32[]{:S(2)}) collective-permute-start(f32[3,32,256]{2,1,0:T(8,128)S(1)} %get-tuple-element.52), channel_id=1, source_target_pairs={{0,1},{1,0},{2,3},{3,2},{4,5},{5,4},{6,7},{7,6},{8,9},{9,8},{10,11... | collective-permute-start | bytes 294920 | tf_op jit(solution)/shard_map/ppermute | solution.py:34
Sparse Core Ops, SparseCore 0:
  16.8 76.1 all-gather.1

commit v2 on v1

--- a/solution.py
+++ b/solution.py
@@ -18,9 +18,11 @@
 COLUMNS = 2 * FEATURE_WIDTH
 STEP = 1024
 VMEM_LIMIT = 54 * 1024 * 1024
+LOW_LIMIT = 54 * 1024 * 1024
 FULL_LIMIT = 60 * 1024 * 1024
 SMALL_LIMIT = 24 * 1024 * 1024
 HINT = 16
+TURNS = 0
 CHUNKS = 2
 PARTS = 2
 
@@ -350,8 +352,8 @@
         sums_ref[...] = jnp.broadcast_to(squares, sums_ref.shape)
         if last:
             products = jnp.sum(out_ref[...] * cot_ref[...].astype(F32), axis=1, keepdims=True)
-            lane = lax.broadcasted_iota(jnp.int32, sums_ref.shape, 1)
-            sums_ref[...] = jnp.where(lane == 0, squares + sums_before_ref[...], products)
+            column = lax.broadcasted_iota(jnp.int32, sums_ref.shape, 1)
+            sums_ref[...] = jnp.where(column == 0, squares + sums_before_ref[...], products)
 
     sems = pltpu.SemaphoreType.DMA((steps,))
     total = jax.ShapeDtypeStruct((tokens, 2 * kv), F32)
@@ -360,7 +362,7 @@
         core,
         [own, other, gain, key_matrix, value_matrix] + ([cot, *before] if last else []),
         (0, 1, 3, 4),
-        [total, jax.ShapeDtypeStruct((tokens, 128), F32)],
+        [total, jax.ShapeDtypeStruct((tokens, 2), F32)],
         8 * tokens * part * kv,
         [
             pltpu.VMEM((tokens, 2 * part), BF16),
@@ -374,40 +376,27 @@
     )
 
 
-def low_rank_down(core, xs, gain, factors):
-    parts = len(xs)
-    tokens, part = xs[0].shape
-    half = parts * part
-    within = part // STEP
+def low_rank_down(core, x, rstd, gain, factors):
+    tokens, half = x.shape
     steps = half // STEP
 
-    def body(core_ref, *rest):
-        x_refs, rest = rest[:parts], rest[parts:]
-        gain_ref, factors_ref, out_ref, held, ours, x_sems, sems = rest
+    def body(core_ref, x_ref, rstd_ref, gain_ref, factors_ref, out_ref, held, ours, x_sems, sems):
         base = pl.multiple_of(core_ref[0] * half, half)
+        rows = [pl.ds(base + i * STEP, STEP) for i in range(steps)]
         copies = []
         for i in range(steps):
-            copies.append(
-                [
-                    pltpu.make_async_copy(
-                        x_refs[i // within].at[:, lanes_of(i % within)],
-                        held.at[:, lanes_of(i)],
-                        x_sems.at[i],
-                    ),
-                    pltpu.make_async_copy(
-                        factors_ref.at[pl.ds(base + i * STEP, STEP), :COLUMNS],
-                        ours.at[lanes_of(i)],
-                        sems.at[i],
-                    ),
-                ]
-            )
+            sources = [
+                (x_ref.at[:, lanes_of(i)], held.at[:, lanes_of(i)], x_sems),
+                (factors_ref.at[rows[i]], ours.at[lanes_of(i)], sems),
+            ]
+            copies.append([pltpu.make_async_copy(a, b, c.at[i]) for a, b, c in sources])
             for copy in copies[i]:
                 copy.start()
         for i in range(steps):
             for copy in copies[i]:
                 copy.wait()
-            scaled = held[:, lanes_of(i)].astype(F32) * gain_ref[:, pl.ds(base + i * STEP, STEP)]
-            product = dot(scaled.astype(BF16), ours[lanes_of(i)])
+            normed = held[:, lanes_of(i)].astype(F32) * rstd_ref[...] * gain_ref[:, rows[i]]
+            product = dot(normed.astype(BF16), ours[lanes_of(i)])
             if i == 0:
                 out_ref[...] = product
             else:
@@ -417,8 +406,8 @@
     return call(
         body,
         core,
-        [*xs, gain, factors],
-        tuple(range(parts)) + (parts + 1,),
+        [x, rstd, gain, factors],
+        (0, 3),
         jax.ShapeDtypeStruct((tokens, COLUMNS), F32),
         2 * tokens * half * COLUMNS,
         [
@@ -427,7 +416,7 @@
             sems,
             sems,
         ],
-        limit=VMEM_LIMIT,
+        limit=LOW_LIMIT,
     )
 
 
@@ -455,59 +444,38 @@
     )
 
 
-def up_gradient(core, mine, other, jobs, cot, back, sums, other_sums, width):
-    tokens, kv = cot.shape[0], cot.shape[1] // 2
-
-    def body(core_ref, mine_ref, other_ref, jobs_ref, cot_ref, back_ref, *rest):
-        sums_ref, other_sums_ref, low_ref, out_ref, rstd_ref, mean_ref = rest
+def with_low_rank(core, frozen, low, jobs, up, cot, back, sums, other_sums, width):
+    tokens, kv = frozen.shape[0], frozen.shape[1] // 2
+
+    def body(core_ref, frozen_ref, low_ref, jobs_ref, up_ref, cot_ref, back_ref, *rest):
+        sums_ref, other_sums_ref, out_ref, mean_ref, grad_ref = rest
         sums = sums_ref[...] + other_sums_ref[...]
         rstd = lax.rsqrt(sums[:, :1] / width + 1e-05)
-        rstd_ref[...] = rstd
-        total = masked((mine_ref[...] + other_ref[...]) * rstd, jobs_ref[...])
-        low_products = jnp.sum(total * back_ref[...].astype(F32), axis=1, keepdims=True)
+        low = masked(low_ref[...].astype(F32), jobs_ref[...])
+        low_products = jnp.sum(low * back_ref[...].astype(F32), axis=1, keepdims=True)
+        low = low.astype(BF16)
         mean_ref[...] = (sums[:, 1:2] * rstd + ADAPTER_SCALING * low_products) / width
-        low = total.astype(BF16)
-        low_ref[...] = low
         for side in range(2):
             lanes = lanes_of(side, kv)
             picked = low[:, side * FEATURE_WIDTH : (side + 1) * FEATURE_WIDTH]
-            out_ref[:, lanes] = (ADAPTER_SCALING * rows_dot(picked, cot_ref[:, lanes])).astype(BF16)
-
-    column = jax.ShapeDtypeStruct((tokens, 1), F32)
-    return call(
-        body,
-        core,
-        [mine, other, jobs, cot, back, sums, other_sums],
+            total = frozen_ref[:, lanes] * rstd
+            total += ADAPTER_SCALING * dot(picked, up_ref[:, lanes])
+            out_ref[:, lanes] = total.astype(BF16)
+            grad = ADAPTER_SCALING * rows_dot(picked, cot_ref[:, lanes])
+            grad_ref[:, lanes] = grad.astype(BF16)
+
+    return call(
+        body,
+        core,
+        [frozen, low, jobs, up, cot, back, sums, other_sums],
         (),
         [
-            jax.ShapeDtypeStruct((tokens, COLUMNS), BF16),
+            jax.ShapeDtypeStruct(frozen.shape, BF16),
+            jax.ShapeDtypeStruct((tokens, 1), F32),
             jax.ShapeDtypeStruct((FEATURE_WIDTH, 2 * kv), BF16),
-            column,
-            column,
         ],
         4 * tokens * kv * FEATURE_WIDTH,
         limit=FULL_LIMIT,
-    )
-
-
-def with_low_rank(core, frozen, low, up, rstd):
-    tokens, kv = frozen.shape[0], frozen.shape[1] // 2
-
-    def body(core_ref, frozen_ref, low_ref, up_ref, rstd_ref, out_ref):
-        for side in range(2):
-            lanes = lanes_of(side, kv)
-            picked = low_ref[:, side * FEATURE_WIDTH : (side + 1) * FEATURE_WIDTH]
-            total = frozen_ref[:, lanes] * rstd_ref[...]
-            total += ADAPTER_SCALING * dot(picked, up_ref[:, lanes])
-            out_ref[:, lanes] = total.astype(BF16)
-
-    return call(
-        body,
-        core,
-        [frozen, low, up, rstd],
-        (),
-        jax.ShapeDtypeStruct(frozen.shape, BF16),
-        4 * tokens * kv * FEATURE_WIDTH,
     )
 
 
@@ -523,7 +491,7 @@
         for i in range(steps):
             lanes = lanes_of(i)
             sources = [
-                (factors_ref.at[rows[i], COLUMNS:], ours.at[lanes], sems),
+                (factors_ref.at[rows[i]], ours.at[lanes], sems),
                 (x_ref.at[:, lanes], xs.at[:, lanes], x_sems),
                 (scaled_ref.at[:, lanes], ins.at[:, lanes], in_sems),
             ]
@@ -665,8 +633,8 @@
     up = lax.all_to_all(jnp.tile(up, (n_data, 1, 1)), "dp", 0, 0, tiled=True)
     up = up.reshape(FEATURE_WIDTH, 2 * kv)
 
-    both = lax.all_gather(
-        jnp.concatenate([factors, after(factors_next, *x_parts)], axis=1), ("dp", "tensor"), axis=0, tiled=True
+    all_next = lax.all_gather(
+        after(factors_next, *x_parts), ("dp", "tensor"), axis=0, tiled=True
     )
 
     leaving = frozen_back(core, cot, key_matrix, value_matrix, half)
@@ -689,27 +657,23 @@
     down_piece = down_gradient(after(core, scaled), kept, taken, back_next, block)
     down_pieces = lax.all_to_all(down_piece, "dp", 0, 0, tiled=True)
 
-    x_other = [swapped(value) for value in x_in]
     sources = (gain, key_matrix, value_matrix)
-    frozen = projected(after(core, down_piece), x_in[0], x_other[0], 0, half, *sources, cot)
-    frozen, sums = projected(core, x_in[1], x_other[1], part, half, *sources, cot, frozen)
-    low_part = low_rank_down(after(core, frozen), x_in, gain, both)
-    low, up_piece, rstd_in, mean = up_gradient(
-        core, low_part, swapped(low_part), jobs, cot, back, sums, swapped(sums), width
-    )
+    frozen = projected(
+        after(core, down_piece), x_in[0], swapped(x_in[0]), 0, half, *sources, cot
+    )
+    x_other = swapped(after(x_in[1], frozen[0]))
+    low_part = low_rank_down(after(core, frozen), x_here, rstd, gain_next, all_next)
+    frozen, sums = projected(after(core, low_part), x_in[1], x_other, part, half, *sources, cot, frozen)
+
+    low = shifted((low_part + swapped(low_part)).astype(BF16), "section", 1)
+    kv_out, mean, up_piece = with_low_rank(
+        core, frozen, low, jobs, up, cot, back, sums, swapped(sums), width
+    )
+    mean = shifted(mean, "section", -1)
     up_pieces = up_piece.reshape(n_data, rows_local, 2 * kv)
     up_pieces = lax.all_to_all(up_pieces, "dp", 0, 0, tiled=True)
-    mean = shifted(mean, "section", -1)
-    kv_out = with_low_rank(after(core, up_piece, scaled_next), frozen, low, up, rstd_in)
-    turn = swapped(kv_out[:16, :128])
-    down_sum = summed(after(core, turn), down_pieces)
+    down_sum = summed(after(core, up_piece), down_pieces)
     down_sum = shifted(down_sum, "section", 1)
-
-    input_grad = norm_backward(
-        after(core, kv_out), scaled_next, back_next, both, gain_next, x_here, rstd, mean
-    )
-    kv_out = kv_out.reshape(1, tokens, 2, kv)
-    up_sum = jnp.sum(up_pieces.astype(F32), axis=0).reshape(rows_local, 2, kv)
 
     job_ids = jnp.arange(JOBS, dtype=jnp.int32)
     counts = job_tokens.astype(F32)
@@ -721,10 +685,16 @@
     row_count = jnp.sum(
         jnp.where(row_job[:, None] == job_ids[None, :], counts[None, :], 0.0), axis=1
     )
-    scalars = jnp.concatenate([after(core, input_grad, up_pieces), finishing.astype(jnp.int32)])
+    scalars = jnp.concatenate([after(core, down_sum, up_pieces), finishing.astype(jnp.int32)])
     new_a, chosen = down_optimizer(
         scalars, adapter_params[0], adapter_second[0], down_sum, column_total[None, :]
     )
+    input_grad = norm_backward(
+        after(core, chosen), scaled_next, back_next, all_next, gain_next, x_here, rstd, mean
+    )
+    kv_out = kv_out.reshape(1, tokens, 2, kv)
+    up_sum = jnp.sum(up_pieces.astype(F32), axis=0).reshape(rows_local, 2, kv)
+
     new_b = jnp.stack(
         adam_update(
             right_params[0, 0],

time: 136 us -> 129 us (0.949)
  waiting for transfers between devices: 15 us -> 8.99 us
    all_gather x1, waiting for transfers between devices: 7.84 us -> 0.01 us  [local(): lax.all_gather(after(factors_next, *x_parts), ('dp', 'tensor'), axis=0, t...]
    unnamed x52 -> x42, local copies, waits for them, and re-layouts: 7.51 us -> 4.72 us
    all_to_all x1, starting transfers between devices: 7.86 us -> 5.28 us  [local(): up_pieces = lax.all_to_all(up_pieces, 'dp', 0, 0, tiled=True)]
    all_to_all x1, waiting for transfers between devices: 0.01 us -> 2.23 us  [local(): down_pieces = lax.all_to_all(down_piece, 'dp', 0, 0, tiled=True)]
    ppermute x17 -> x18, waiting for transfers between devices: 7.13 us -> 5.41 us  [shifted(): return lax.ppermute(value, axis, pairs)]
    ppermute x17 -> x18, starting transfers between devices: 18 us -> 18.7 us  [shifted(): return lax.ppermute(value, axis, pairs)]
    pallas_call x13 -> x12, Pallas kernels: 45.6 us -> 46.1 us  [call(): pl.pallas_call(body, out_shape=out_shape, grid_spec=pltpu.PrefetchScalarG...]
  transfers between devices with their start and end apart: 21 -> 22, of which waited for: 4 -> 7; matrix products, arithmetic and copies ran while one was open for 7% -> 9% of each run, Pallas kernels for 32% -> 36%
where the time goes in v2:
time: 129 us; the launch traced here: 128 us
  Pallas kernels  46.1 us (36%)
  starting transfers between devices  39.8 us (31%)
  between operations  15.1 us (12%)
  local copies, waits for them, and re-layouts  13.6 us (11%)
  waiting for transfers between devices  8.99 us (7%)
  other arithmetic  4.62 us (4%)
    pallas_call x12, Pallas kernels, call(): pl.pallas_call(body, out_shape=out_shape, grid_spec=pltpu.PrefetchScalarG...  46.1 us
    ppermute x18, starting transfers between devices, shifted(): return lax.ppermute(value, axis, pairs)  18.7 us
    all_to_all x1, starting transfers between devices, local(): down_pieces = lax.all_to_all(down_piece, 'dp', 0, 0, tiled=True)  7.92 us
    all_to_all x1, starting transfers between devices, local(): up = lax.all_to_all(jnp.tile(up, (n_data, 1, 1)), 'dp', 0, 0, tiled=True)  7.77 us
    ppermute x18, waiting for transfers between devices, shifted(): return lax.ppermute(value, axis, pairs)  5.41 us
    all_to_all x1, starting transfers between devices, local(): up_pieces = lax.all_to_all(up_pieces, 'dp', 0, 0, tiled=True)  5.28 us
    unnamed x42, local copies, waits for them, and re-layouts  4.72 us
    slice x1, local copies, waits for them, and re-layouts, local(): x_here[:, index * part:(index + 1) * part]  3.25 us
  transfers between devices with their start and end apart: 22, of which 7 were waited for; matrix products, arithmetic and copies ran while one was open for 9% of the time, Pallas kernels for 36%

profile of v2, /device:TPU:1, one launch (start us, length us, event | category | flops | bytes accessed | tf_op | source)
XLA Modules:
  0.0 128.2 jit_solution(5437943444417731583)
XLA Ops:
  7.2 1.0 convert_reduce_fusion.2
  8.3 1.0 fusion
  9.2 3.4 %collective-permute-start.2 = (bf16[320,256]{1,0:T(8,128)(2,1)S(1)}, bf16[320,256]{1,0:T(8,128)(2,1)S(1)}, u32[]{:S(2)}, u32[]{:S(2)}) collective-permute-start(bf16[320,256]{1,0:T(8,128)(2,1)S(1)} %pad_maximum_fusion), channel_id=1, source_target_pairs={{0,96},{32,0},{64,32},{96,64},{1,97},{33,1},{65,33},{97,65},{2,98}... | collective-permute-start | bytes 491528 | tf_op jit(solution)/shard_map/ppermute | solution.py:36
  12.6 3.3 %fusion.5 = (bf16[256,2048]{1,0:T(8,128)(2,1)}, bf16[256,2048]{1,0:T(8,128)(2,1)}) fusion(bf16[256,4096]{1,0:T(8,128)(2,1)} %bitcast.37), kind=kLoop, calls=%fused_computation.44 | loop fusion | bytes 4194304 | tf_op jit(solution)/shard_map/slice | solution.py:629
  15.9 0.7 slice.38
  16.6 0.6 collective-permute-start.3
  17.2 0.7 tile.2
  17.9 7.8 %all-to-all-start = ((bf16[16,8,1024]{2,1,0:T(8,128)(2,1)}), bf16[16,8,1024]{2,1,0:T(8,128)(2,1)S(1)}, u32[]{:S(2)}, u32[]{:S(2)}) async-start(bf16[16,8,1024]{2,1,0:T(8,128)(2,1)} %tile.2), calls=%async_computation | async-start | bytes 524288 | tf_op jit(solution)/shard_map/all_to_all | solution.py:633
  25.7 0.5 multiply_reduce_fusion
  26.2 2.2 %collective-permute-start.1 = (f32[256,1]{0,1:T(1,128)S(1)}, f32[256,1]{0,1:T(1,128)S(1)}, u32[]{:S(2)}, u32[]{:S(2)}) collective-permute-start(f32[256,1]{0,1:T(1,128)S(1)} %bitcast.68), channel_id=1, source_target_pairs={{0,1},{1,0},{2,3},{3,2},{4,5},{5,4},{6,7},{7,6},{8,9},{9,8},{10,11... | collective-permute-start | bytes 3080 | tf_op jit(solution)/shard_map/ppermute | solution.py:36
  28.4 0.9 copy.27
  29.3 6.6 %shard_map.155 = (bf16[256,2048]{1,0:T(8,128)(2,1)}, bf16[256,2048]{1,0:T(8,128)(2,1)}) custom-call(s32[1]{0:T(128)} %bitcast.core_ref, bf16[256,1024]{1,0:T(8,128)(2,1)} %bitcast.41, bf16[8192,512]{1,0:T(8,128)(2,1)} %bitcast.54, bf16[8192,512]{1,0:T(8,128)(2,1)} %bitcast.58), custom_call_target="tpu_custom_call" | custom-call | flops 134217728 | bytes 1212416 | tf_op jit(solution)/shard_map/pallas_call | solution.py:84
  36.0 0.5 collective-permute-start.5
  37.1 1.5 %shard_map.157 = (bf16[256,2048]{1,0:T(8,128)(2,1)S(1)}, bf16[256,2048]{1,0:T(8,128)(2,1)S(1)}) custom-call(s32[1]{0:T(128)} %bitcast.core_ref, bf16[256,4096]{1,0:T(8,128)(2,1)S(1)} %bitcast.40, f32[256,1]{1,0:T(8,128)S(1)} %rsqrt.3.rstd_ref.rest_0_, f32[1,8192]{1,0:T(1,128)S(1)} %bitcast.49), custom_call_target="tpu_custom_call" | custom-call | flops 65536 | bytes 264256 | tf_op jit(solution)/shard_map/pallas_call | solution.py:84
  38.8 0.4 collective-permute-start
  39.2 2.8 %collective-permute-done = f32[256,256]{1,0:T(8,128)S(1)} collective-permute-done((f32[256,256]{1,0:T(8,128)S(1)}, f32[256,256]{1,0:T(8,128)S(1)}, u32[]{:S(2)}, u32[]{:S(2)}) %collective-permute-start) | collective-permute-done | bytes 262176 | tf_op jit(solution)/shard_map/ppermute | solution.py:36
  42.0 1.2 collective-permute-start.9
  43.2 0.9 collective-permute-start.8
  44.2 1.5 %collective-permute-start.7 = (bf16[256,256]{1,0:T(8,128)(2,1)S(1)}, bf16[256,256]{1,0:T(8,128)(2,1)S(1)}, u32[]{:S(2)}, u32[]{:S(2)}) collective-permute-start(bf16[256,256]{1,0:T(8,128)(2,1)S(1)} %select_convert_fusion.back_ref), channel_id=1, source_target_pairs={{0,96},{32,0},{64,32},{96,64},{1,97},{33,1},{65,33},{97,65},{2,98}... | collective-permute-start | bytes 393224 | tf_op jit(solution)/shard_map/ppermute | solution.py:36
  45.8 7.1 %shard_map.158 = bf16[256,4096]{1,0:T(8,128)(2,1)} custom-call(s32[1]{0:T(128)} %bitcast.core_ref, bf16[256,1024]{1,0:T(8,128)(2,1)} %bitcast.42, bf16[8192,512]{1,0:T(8,128)(2,1)} %bitcast.55, bf16[8192,512]{1,0:T(8,128)(2,1)} %bitcast.59, bf16[256,2048]{1,0:T(8,128)(2,1)} %collective-permute-done.4.rest_0_, ...), custom_call_target="tpu_custom_call" | custom-call | flops 134217728 | bytes 1345536 | tf_op jit(solution)/shard_map/pallas_call | solution.py:84
  53.0 1.7 %shard_map.159 = bf16[16,256,256]{2,1,0:T(8,128)(2,1)S(1)} custom-call(s32[1]{0:T(128)} %bitcast.core_ref, bf16[256,2048]{1,0:T(8,128)(2,1)S(1)} %get-tuple-element.33.kept_ref, bf16[256,2048]{1,0:T(8,128)(2,1)S(1)} %collective-permute-done.6.taken_ref, bf16[256,256]{1,0:T(8,128)(2,1)S(1)} %collective-permute-done.7.back_ref), custom_call_target="tpu_custom_call" | custom-call | flops 33554432 | bytes 270336 | tf_op jit(solution)/shard_map/pallas_call | solution.py:84
  54.6 1.4 %copy-done.2 = bf16[16,256,256]{2,1,0:T(8,128)(2,1)} copy-done((bf16[16,256,256]{2,1,0:T(8,128)(2,1)}, bf16[16,256,256]{2,1,0:T(8,128)(2,1)S(1)}, u32[]{:S(2)}) %copy-start.2) | copy-done | bytes 2097176
  56.0 7.9 %all-to-all-start.1 = ((bf16[16,256,256]{2,1,0:T(8,128)(2,1)}), bf16[16,256,256]{2,1,0:T(8,128)(2,1)S(1)}, u32[]{:S(2)}, u32[]{:S(2)}) async-start(bf16[16,256,256]{2,1,0:T(8,128)(2,1)} %copy-done.2), calls=%async_computation.1 | async-start | bytes 4194304 | tf_op jit(solution)/shard_map/all_to_all | solution.py:658
  64.2 6.5 %shard_map.160 = (f32[256,1024]{1,0:T(8,128)}, f32[256,2]{1,0:T(8,128)}) custom-call(s32[1]{0:T(128)} %bitcast.core_ref, bf16[256,2048]{1,0:T(8,128)(2,1)} %collective-permute-done.3.own_ref, bf16[256,2048]{1,0:T(8,128)(2,1)} %collective-permute-done.8.other_ref, f32[1,8192]{1,0:T(1,128)} %gain_ref.3, bf16[8192,512]{1,0:T(8,128)(2,1)} %bitcast.56, ...), custom_call_target="tpu_custom_call" | custom-call | flops 134217728 | bytes 1247360 | tf_op jit(solution)/shard_map/pallas_call | solution.py:84
  70.8 0.7 collective-permute-start.10
  71.5 4.5 %shard_map.161 = f32[256,256]{1,0:T(8,128)} custom-call(s32[1]{0:T(128)} %bitcast.core_ref, bf16[256,4096]{1,0:T(8,128)(2,1)} %bitcast.38, f32[256,1]{1,0:T(8,128)} %copy-done.4, f32[1,8192]{1,0:T(1,128)} %bitcast.50, bf16[8192,256]{1,0:T(8,128)(2,1)} %all-gather.2.cloned.1.call-done.factors_ref), custom_call_target="tpu_custom_call" | custom-call | flops 33554432 | bytes 411712 | tf_op jit(solution)/shard_map/pallas_call | solution.py:84
  76.1 1.7 %collective-permute-done.11 = f32[256,256]{1,0:T(8,128)S(1)} collective-permute-done((f32[256,256]{1,0:T(8,128)}, f32[256,256]{1,0:T(8,128)S(1)}, u32[]{:S(2)}, u32[]{:S(2)}) %collective-permute-start.11) | collective-permute-done | bytes 262176 | tf_op jit(solution)/shard_map/ppermute | solution.py:36
  77.8 1.0 add_convert_fusion
  78.8 1.8 %collective-permute-start.12 = (bf16[256,256]{1,0:T(8,128)(2,1)S(1)}, bf16[256,256]{1,0:T(8,128)(2,1)S(1)}, u32[]{:S(2)}, u32[]{:S(2)}) collective-permute-start(bf16[256,256]{1,0:T(8,128)(2,1)S(1)} %add_convert_fusion), channel_id=1, source_target_pairs={{0,32},{32,64},{64,96},{96,0},{1,33},{33,65},{65,97},{97,1},{2,34}... | collective-permute-start | bytes 393224 | tf_op jit(solution)/shard_map/ppermute | solution.py:36
  80.6 1.0 copy-done.9
  81.6 7.3 %shard_map.162 = (f32[256,1024]{1,0:T(8,128)}, f32[256,2]{1,0:T(8,128)}) custom-call(s32[1]{0:T(128)} %bitcast.core_ref, bf16[256,2048]{1,0:T(8,128)(2,1)} %collective-permute-done.9.own_ref, bf16[256,2048]{1,0:T(8,128)(2,1)} %copy-done.9, f32[1,8192]{1,0:T(1,128)} %gain_ref.3, bf16[8192,512]{1,0:T(8,128)(2,1)} %bitcast.57, bf16[8192,512]{1,0:T(8,128)(2,1)} %bitcast.61, ...), custom_call_target="tpu_custom_call" | custom-call | flops 134217728 | bytes 1345792 | tf_op jit(solution)/shard_map/pallas_call | solution.py:84
  88.9 0.5 collective-permute-start.13
  89.4 0.8 copy.26.jobs_ref
  90.6 0.6 copy-done.14
  91.3 3.0 %shard_map.163 = (bf16[256,1024]{1,0:T(8,128)(2,1)}, f32[256,1]{1,0:T(8,128)}, bf16[128,1024]{1,0:T(8,128)(2,1)}) custom-call(s32[1]{0:T(128)} %bitcast.core_ref, f32[256,1024]{1,0:T(8,128)} %get-tuple-element.45.frozen_ref, bf16[256,256]{1,0:T(8,128)(2,1)} %copy-done.13, s32[256,1]{1,0:T(8,128)} %copy.26.jobs_ref, bf16[128,1024]{1,0:T(8,128)(2,1)} %bitcast.47, ...), custom_call_target="tpu_custom_call" | custom-call | flops 4194304 | bytes 180608 | tf_op jit(solution)/shard_map/pallas_call | solution.py:84
  94.3 2.2 %all-to-all-done.1.pieces_ref = bf16[16,256,256]{2,1,0:T(8,128)(2,1)S(1)} async-done(((bf16[16,256,256]{2,1,0:T(8,128)(2,1)}), bf16[16,256,256]{2,1,0:T(8,128)(2,1)S(1)}, u32[]{:S(2)}, u32[]{:S(2)}) %all-to-all-start.1) | async-done | bytes 2097184 | tf_op jit(solution)/shard_map/all_to_all | solution.py:658
  96.5 5.3 %all-to-all-start.2 = ((bf16[16,8,1024]{2,1,0:T(8,128)(2,1)}), bf16[16,8,1024]{2,1,0:T(8,128)(2,1)S(1)}, u32[]{:S(2)}, u32[]{:S(2)}) async-start(bf16[16,8,1024]{2,1,0:T(8,128)(2,1)} %bitcast.64), calls=%async_computation.2 | async-start | bytes 524288 | tf_op jit(solution)/shard_map/all_to_all | solution.py:674
  102.0 0.5 shard_map.164
  102.5 2.1 %collective-permute-start.14 = (bf16[256,256]{1,0:T(8,128)(2,1)S(1)}, bf16[256,256]{1,0:T(8,128)(2,1)S(1)}, u32[]{:S(2)}, u32[]{:S(2)}) collective-permute-start(bf16[256,256]{1,0:T(8,128)(2,1)S(1)} %shard_map.164), channel_id=1, source_target_pairs={{0,32},{32,64},{64,96},{96,0},{1,33},{33,65},{65,97},{97,1},{2,34}... | collective-permute-start | bytes 393224 | tf_op jit(solution)/shard_map/ppermute | solution.py:36
  105.4 0.9 collective-permute-start.16
  106.2 2.2 %reshape.140 = bf16[1,256,2,512]{3,2,1,0:T(2,128)(2,1)} reshape(bf16[256,1024]{1,0:T(8,128)(2,1)} %get-tuple-element.47) | data formatting | bytes 1048576 | tf_op jit(solution)/shard_map/reshape | solution.py:695
  108.6 1.3 %all-to-all-done.2 = bf16[16,8,1024]{2,1,0:T(8,128)(2,1)S(1)} async-done(((bf16[16,8,1024]{2,1,0:T(8,128)(2,1)}), bf16[16,8,1024]{2,1,0:T(8,128)(2,1)S(1)}, u32[]{:S(2)}, u32[]{:S(2)}) %all-to-all-start.2) | async-done | bytes 262176 | tf_op jit(solution)/shard_map/all_to_all | solution.py:674
  110.0 1.7 %shard_map.165 = (f32[3,256,256]{2,1,0:T(8,128)}, f32[3,32,256]{2,1,0:T(8,128)S(1)}) custom-call(s32[2]{0:T(128)S(1)} %pad_add_fusion.scalars_ref, f32[2,256,256]{2,1,0:T(8,128)S(1)} %bitcast.48, f32[256,256]{1,0:T(8,128)S(1)} %bitcast.52, bf16[256,256]{1,0:T(8,128)(2,1)S(1)} %collective-permute-done.14.grad_ref, f32[1,256]{1,0:T(1,128)S(1)} %bitcast.53), custom_call_target="tpu_custom_call" | custom-call | flops 81920 | bytes 112704 | tf_op jit(solution)/shard_map/pallas_call | solution.py:84
  111.8 1.5 %collective-permute-start.17 = (f32[3,32,256]{2,1,0:T(8,128)S(1)}, f32[3,32,256]{2,1,0:T(8,128)S(1)}, u32[]{:S(2)}, u32[]{:S(2)}) collective-permute-start(f32[3,32,256]{2,1,0:T(8,128)S(1)} %get-tuple-element.51), channel_id=1, source_target_pairs={{0,1},{1,0},{2,3},{3,2},{4,5},{5,4},{6,7},{7,6},{8,9},{9,8},{10,11... | collective-permute-start | bytes 294920 | tf_op jit(solution)/shard_map/ppermute | solution.py:36
  113.9 0.7 copy-done.12
  114.5 5.4 %shard_map.166 = bf16[256,4096]{1,0:T(8,128)(2,1)} custom-call(s32[1]{0:T(128)} %bitcast.core_ref, bf16[256,4096]{1,0:T(8,128)(2,1)} %collective-permute-done.15.scaled_ref, bf16[256,256]{1,0:T(8,128)(2,1)} %copy-done.7, bf16[8192,256]{1,0:T(8,128)(2,1)} %all-gather.2.cloned.1.call-done.factors_ref, f32[1,8192]{1,0:T(1,128)} %bitcast.51, ...), custom_call_target="tpu_custom_call" | custom-call | flops 33554432 | bytes 665728 | tf_op jit(solution)/shard_map/pallas_call | solution.py:84
  119.9 0.7 maximum_bitcast_fusion.1
  120.6 0.7 maximum_bitcast_fusion
  (82 shorter events, 3.0 us)
Async XLA Ops:
  7.2 64.3 %all-gather.2.cloned.1.call-start = ((), (), s32[]{:S(2)}) async-start(), calls=%async_computation.3 | async-start | bytes 4325376 | tf_op jit(solution)/shard_map/all_gather | solution.py:636
  9.2 6.6 %collective-permute-start.2 = (bf16[320,256]{1,0:T(8,128)(2,1)S(1)}, bf16[320,256]{1,0:T(8,128)(2,1)S(1)}, u32[]{:S(2)}, u32[]{:S(2)}) collective-permute-start(bf16[320,256]{1,0:T(8,128)(2,1)S(1)} %pad_maximum_fusion), channel_id=1, source_target_pairs={{0,96},{32,0},{64,32},{96,64},{1,97},{33,1},{65,33},{97,65},{2,98}... | collective-permute-start | bytes 491528 | tf_op jit(solution)/shard_map/ppermute | solution.py:36
  12.6 4.6 %copy-start.15 = (f32[1,2,8,2,512]{4,3,2,1,0:T(2,128)S(1)}, f32[1,2,8,2,512]{4,3,2,1,0:T(2,128)}, u32[]{:S(2)}) copy-start(f32[1,2,8,2,512]{4,3,2,1,0:T(2,128)} %param.18) | copy-start | bytes 196612
  12.6 13.1 %copy-start = (bf16[1,256,4096]{2,1,0:T(8,128)(2,1)S(1)}, bf16[1,256,4096]{2,1,0:T(8,128)(2,1)}, u32[]{:S(2)}) copy-start(bf16[1,256,4096]{2,1,0:T(8,128)(2,1)} %param.12) | copy-start | bytes 6291460
  15.9 12.5 %copy-start.10 = (bf16[1,256,2,512]{3,2,1,0:T(2,128)(2,1)S(1)}, bf16[1,256,2,512]{3,2,1,0:T(2,128)(2,1)}, u32[]{:S(2)}) copy-start(bf16[1,256,2,512]{3,2,1,0:T(2,128)(2,1)} %param.23) | copy-start | bytes 1572868
  16.6 26.6 %collective-permute-start.3 = (bf16[256,2048]{1,0:T(8,128)(2,1)}, bf16[256,2048]{1,0:T(8,128)(2,1)}, u32[]{:S(2)}, u32[]{:S(2)}) collective-permute-start(bf16[256,2048]{1,0:T(8,128)(2,1)} %get-tuple-element.61), channel_id=1, source_target_pairs={{0,32},{32,64},{64,96},{96,0},{1,33},{33,65},{65,97},{97,1},{2,34}... | collective-permute-start | bytes 3145736 | tf_op jit(solution)/shard_map/ppermute | solution.py:36
  17.9 18.8 %all-to-all-start = ((bf16[16,8,1024]{2,1,0:T(8,128)(2,1)}), bf16[16,8,1024]{2,1,0:T(8,128)(2,1)S(1)}, u32[]{:S(2)}, u32[]{:S(2)}) async-start(bf16[16,8,1024]{2,1,0:T(8,128)(2,1)} %tile.2), calls=%async_computation | async-start | bytes 524288 | tf_op jit(solution)/shard_map/all_to_all | solution.py:633
  26.2 10.3 %collective-permute-start.1 = (f32[256,1]{0,1:T(1,128)S(1)}, f32[256,1]{0,1:T(1,128)S(1)}, u32[]{:S(2)}, u32[]{:S(2)}) collective-permute-start(f32[256,1]{0,1:T(1,128)S(1)} %bitcast.68), channel_id=1, source_target_pairs={{0,1},{1,0},{2,3},{3,2},{4,5},{5,4},{6,7},{7,6},{8,9},{9,8},{10,11... | collective-permute-start | bytes 3080 | tf_op jit(solution)/shard_map/ppermute | solution.py:36
  29.3 7.5 %copy-start.1 = (bf16[32,8,2,512]{3,1,2,0:T(8,128)(2,1)S(1)}, bf16[32,8,2,512]{3,1,2,0:T(8,128)(2,1)}, u32[]{:S(2)}) copy-start(bf16[32,8,2,512]{3,1,2,0:T(8,128)(2,1)} %copy.27) | copy-start | bytes 1572868
  35.9 8.2 %copy-start.17 = (s32[1,256]{1,0:T(1,128)S(1)}, s32[1,256]{1,0:T(1,128)}, u32[]{:S(2)}) copy-start(s32[1,256]{1,0:T(1,128)} %param.20) | copy-start | bytes 3076
  35.9 8.3 %collective-permute-start.4 = (bf16[256,2048]{1,0:T(8,128)(2,1)}, bf16[256,2048]{1,0:T(8,128)(2,1)}, u32[]{:S(2)}, u32[]{:S(2)}) collective-permute-start(bf16[256,2048]{1,0:T(8,128)(2,1)} %get-tuple-element.30), channel_id=1, source_target_pairs={{0,1},{1,0},{2,3},{3,2},{4,5},{5,4},{6,7},{7,6},{8,9},{9,8},{10,11... | collective-permute-start | bytes 3145736 | tf_op jit(solution)/shard_map/ppermute | solution.py:36
  36.0 9.8 %collective-permute-start.5 = (bf16[256,2048]{1,0:T(8,128)(2,1)}, bf16[256,2048]{1,0:T(8,128)(2,1)}, u32[]{:S(2)}, u32[]{:S(2)}) collective-permute-start(bf16[256,2048]{1,0:T(8,128)(2,1)} %get-tuple-element.35), channel_id=1, source_target_pairs={{0,1},{1,0},{2,3},{3,2},{4,5},{5,4},{6,7},{7,6},{8,9},{9,8},{10,11... | collective-permute-start | bytes 3145736 | tf_op jit(solution)/shard_map/ppermute | solution.py:36
  36.7 16.2 %copy-start.4 = (f32[256,1]{1,0:T(8,128)}, f32[256,1]{1,0:T(8,128)S(1)}, u32[]{:S(2)}) copy-start(f32[256,1]{1,0:T(8,128)S(1)} %rsqrt.3.rstd_ref.rest_0_) | copy-start | bytes 3076
  36.7 16.2 %copy-start.6 = (f32[1,1,32,256]{3,1,2,0:T(1,128)}, f32[1,1,32,256]{3,1,2,0:T(1,128)S(1)}, u32[]{:S(2)}) copy-start(f32[1,1,32,256]{3,1,2,0:T(1,128)S(1)} %copy.29) | copy-start | bytes 98308
  36.8 16.1 %copy-start.3 = (bf16[16,8,1024]{2,1,0:T(8,128)(2,1)}, bf16[16,8,1024]{2,1,0:T(8,128)(2,1)S(1)}, u32[]{:S(2)}) copy-start(bf16[16,8,1024]{2,1,0:T(8,128)(2,1)S(1)} %all-to-all-done) | copy-start | bytes 786436
  38.6 14.3 %collective-permute-start.6 = (bf16[256,2048]{1,0:T(8,128)(2,1)S(1)}, bf16[256,2048]{1,0:T(8,128)(2,1)S(1)}, u32[]{:S(2)}, u32[]{:S(2)}) collective-permute-start(bf16[256,2048]{1,0:T(8,128)(2,1)S(1)} %get-tuple-element.37), channel_id=1, source_target_pairs={{0,1},{1,0},{2,3},{3,2},{4,5},{5,4},{6,7},{7,6},{8,9},{9,8},{10,11... | collective-permute-start | bytes 3145736 | tf_op jit(solution)/shard_map/ppermute | solution.py:36
  38.8 3.2 %collective-permute-start = (f32[256,256]{1,0:T(8,128)S(1)}, f32[256,256]{1,0:T(8,128)S(1)}, u32[]{:S(2)}, u32[]{:S(2)}) collective-permute-start(f32[256,256]{1,0:T(8,128)S(1)} %shard_map.156), channel_id=1, source_target_pairs={{0,1},{1,0},{2,3},{3,2},{4,5},{5,4},{6,7},{7,6},{8,9},{9,8},{10,11... | collective-permute-start | bytes 786440 | tf_op jit(solution)/shard_map/ppermute | solution.py:36
  42.0 28.8 %collective-permute-start.9 = (bf16[256,2048]{1,0:T(8,128)(2,1)}, bf16[256,2048]{1,0:T(8,128)(2,1)}, u32[]{:S(2)}, u32[]{:S(2)}) collective-permute-start(bf16[256,2048]{1,0:T(8,128)(2,1)} %get-tuple-element.60), channel_id=1, source_target_pairs={{0,32},{32,64},{64,96},{96,0},{1,33},{33,65},{65,97},{97,1},{2,34}... | collective-permute-start | bytes 3145736 | tf_op jit(solution)/shard_map/ppermute | solution.py:36
  43.2 21.0 %collective-permute-start.8 = (bf16[256,2048]{1,0:T(8,128)(2,1)}, bf16[256,2048]{1,0:T(8,128)(2,1)}, u32[]{:S(2)}, u32[]{:S(2)}) collective-permute-start(bf16[256,2048]{1,0:T(8,128)(2,1)} %collective-permute-done.3.own_ref), channel_id=1, source_target_pairs={{0,1},{1,0},{2,3},{3,2},{4,5},{5,4},{6,7},{7,6},{8,9},{9,8},{10,11... | collective-permute-start | bytes 3145736 | tf_op jit(solution)/shard_map/ppermute | solution.py:36
  44.2 8.7 %copy-start.11 = (bf16[256,256]{1,0:T(8,128)(2,1)}, bf16[256,256]{1,0:T(8,128)(2,1)S(1)}, u32[]{:S(2)}) copy-start(bf16[256,256]{1,0:T(8,128)(2,1)S(1)} %select_convert_fusion.back_ref) | copy-start | bytes 393220
  44.2 8.7 %collective-permute-start.7 = (bf16[256,256]{1,0:T(8,128)(2,1)S(1)}, bf16[256,256]{1,0:T(8,128)(2,1)S(1)}, u32[]{:S(2)}, u32[]{:S(2)}) collective-permute-start(bf16[256,256]{1,0:T(8,128)(2,1)S(1)} %select_convert_fusion.back_ref), channel_id=1, source_target_pairs={{0,96},{32,0},{64,32},{96,64},{1,97},{33,1},{65,33},{97,65},{2,98}... | collective-permute-start | bytes 393224 | tf_op jit(solution)/shard_map/ppermute | solution.py:36
  52.9 1.7 %copy-start.7 = (bf16[256,256]{1,0:T(8,128)(2,1)}, bf16[256,256]{1,0:T(8,128)(2,1)S(1)}, u32[]{:S(2)}) copy-start(bf16[256,256]{1,0:T(8,128)(2,1)S(1)} %collective-permute-done.7.back_ref) | copy-start | bytes 393220
  54.6 1.4 %copy-start.2 = (bf16[16,256,256]{2,1,0:T(8,128)(2,1)}, bf16[16,256,256]{2,1,0:T(8,128)(2,1)S(1)}, u32[]{:S(2)}) copy-start(bf16[16,256,256]{2,1,0:T(8,128)(2,1)S(1)} %shard_map.159) | copy-start | bytes 6291460
  56.0 40.5 %all-to-all-start.1 = ((bf16[16,256,256]{2,1,0:T(8,128)(2,1)}), bf16[16,256,256]{2,1,0:T(8,128)(2,1)S(1)}, u32[]{:S(2)}, u32[]{:S(2)}) async-start(bf16[16,256,256]{2,1,0:T(8,128)(2,1)} %copy-done.2), calls=%async_computation.1 | async-start | bytes 4194304 | tf_op jit(solution)/shard_map/all_to_all | solution.py:658
  64.0 49.6 %collective-permute-start.15 = (bf16[256,4096]{1,0:T(8,128)(2,1)}, bf16[256,4096]{1,0:T(8,128)(2,1)}, u32[]{:S(2)}, u32[]{:S(2)}) collective-permute-start(bf16[256,4096]{1,0:T(8,128)(2,1)} %shard_map.158), channel_id=1, source_target_pairs={{0,96},{32,0},{64,32},{96,64},{1,97},{33,1},{65,33},{97,65},{2,98}... | collective-permute-start | bytes 6291464 | tf_op jit(solution)/shard_map/ppermute | solution.py:36
  70.8 9.8 %collective-permute-start.10 = (bf16[256,2048]{1,0:T(8,128)(2,1)}, bf16[256,2048]{1,0:T(8,128)(2,1)S(1)}, u32[]{:S(2)}, u32[]{:S(2)}) collective-permute-start(bf16[256,2048]{1,0:T(8,128)(2,1)} %collective-permute-done.9.own_ref), channel_id=1, source_target_pairs={{0,1},{1,0},{2,3},{3,2},{4,5},{5,4},{6,7},{7,6},{8,9},{9,8},{10,11... | collective-permute-start | bytes 3145736 | tf_op jit(solution)/shard_map/ppermute | solution.py:36
  76.0 1.8 %collective-permute-start.11 = (f32[256,256]{1,0:T(8,128)}, f32[256,256]{1,0:T(8,128)S(1)}, u32[]{:S(2)}, u32[]{:S(2)}) collective-permute-start(f32[256,256]{1,0:T(8,128)} %shard_map.161), channel_id=1, source_target_pairs={{0,1},{1,0},{2,3},{3,2},{4,5},{5,4},{6,7},{7,6},{8,9},{9,8},{10,11... | collective-permute-start | bytes 786440 | tf_op jit(solution)/shard_map/ppermute | solution.py:36
  78.8 11.8 %collective-permute-start.12 = (bf16[256,256]{1,0:T(8,128)(2,1)S(1)}, bf16[256,256]{1,0:T(8,128)(2,1)S(1)}, u32[]{:S(2)}, u32[]{:S(2)}) collective-permute-start(bf16[256,256]{1,0:T(8,128)(2,1)S(1)} %add_convert_fusion), channel_id=1, source_target_pairs={{0,32},{32,64},{64,96},{96,0},{1,33},{33,65},{65,97},{97,1},{2,34}... | collective-permute-start | bytes 393224 | tf_op jit(solution)/shard_map/ppermute | solution.py:36
  80.6 9.6 %copy-start.18 = (s32[8]{0:T(128)S(1)}, s32[8]{0:T(128)}, u32[]{:S(2)}) copy-start(s32[8]{0:T(128)} %param.21) | copy-start | bytes 100
  80.6 1.0 copy-start.9
  88.9 1.7 %collective-permute-start.13 = (f32[256,2]{1,0:T(8,128)}, f32[256,2]{1,0:T(8,128)S(1)}, u32[]{:S(2)}, u32[]{:S(2)}) collective-permute-start(f32[256,2]{1,0:T(8,128)} %get-tuple-element.46.rest_0_), channel_id=1, source_target_pairs={{0,1},{1,0},{2,3},{3,2},{4,5},{5,4},{6,7},{7,6},{8,9},{9,8},{10,11... | collective-permute-start | bytes 6152 | tf_op jit(solution)/shard_map/ppermute | solution.py:36
  90.6 0.7 copy-start.14
  90.6 0.7 copy-start.13
  94.3 15.7 %copy-start.5 = (f32[1,2,256,256]{3,2,1,0:T(8,128)S(1)}, f32[1,2,256,256]{3,2,1,0:T(8,128)}, u32[]{:S(2)}) copy-start(f32[1,2,256,256]{3,2,1,0:T(8,128)} %param.16) | copy-start | bytes 1572868
  94.3 15.7 %copy-start.8 = (f32[1,256,256]{2,1,0:T(8,128)S(1)}, f32[1,256,256]{2,1,0:T(8,128)}, u32[]{:S(2)}) copy-start(f32[1,256,256]{2,1,0:T(8,128)} %param.17) | copy-start | bytes 786436
  96.5 13.4 %all-to-all-start.2 = ((bf16[16,8,1024]{2,1,0:T(8,128)(2,1)}), bf16[16,8,1024]{2,1,0:T(8,128)(2,1)S(1)}, u32[]{:S(2)}, u32[]{:S(2)}) async-start(bf16[16,8,1024]{2,1,0:T(8,128)(2,1)} %bitcast.64), calls=%async_computation.2 | async-start | bytes 524288 | tf_op jit(solution)/shard_map/all_to_all | solution.py:674
  102.0 11.4 %copy-start.16 = (f32[1,8,2,512]{3,2,1,0:T(2,128)S(1)}, f32[1,8,2,512]{3,2,1,0:T(2,128)}, u32[]{:S(2)}) copy-start(f32[1,8,2,512]{3,2,1,0:T(2,128)} %param.19) | copy-start | bytes 98308
  102.5 6.1 %collective-permute-start.14 = (bf16[256,256]{1,0:T(8,128)(2,1)S(1)}, bf16[256,256]{1,0:T(8,128)(2,1)S(1)}, u32[]{:S(2)}, u32[]{:S(2)}) collective-permute-start(bf16[256,256]{1,0:T(8,128)(2,1)S(1)} %shard_map.164), channel_id=1, source_target_pairs={{0,32},{32,64},{64,96},{96,0},{1,33},{33,65},{65,97},{97,1},{2,34}... | collective-permute-start | bytes 393224 | tf_op jit(solution)/shard_map/ppermute | solution.py:36
  105.4 8.5 %collective-permute-start.16 = (f32[256,1]{1,0:T(8,128)}, f32[256,1]{1,0:T(8,128)S(1)}, u32[]{:S(2)}, u32[]{:S(2)}) collective-permute-start(f32[256,1]{1,0:T(8,128)} %get-tuple-element.53), channel_id=1, source_target_pairs={{0,96},{32,0},{64,32},{96,64},{1,97},{33,1},{65,33},{97,65},{2,98}... | collective-permute-start | bytes 3080 | tf_op jit(solution)/shard_map/ppermute | solution.py:36
  111.8 8.8 %collective-permute-start.17 = (f32[3,32,256]{2,1,0:T(8,128)S(1)}, f32[3,32,256]{2,1,0:T(8,128)S(1)}, u32[]{:S(2)}, u32[]{:S(2)}) collective-permute-start(f32[3,32,256]{2,1,0:T(8,128)S(1)} %get-tuple-element.51), channel_id=1, source_target_pairs={{0,1},{1,0},{2,3},{3,2},{4,5},{5,4},{6,7},{7,6},{8,9},{9,8},{10,11... | collective-permute-start | bytes 294920 | tf_op jit(solution)/shard_map/ppermute | solution.py:36
  113.9 0.7 copy-start.12
Sparse Core Ops, SparseCore 0:
  16.7 50.5 all-gather.1

commit v3 on v2

--- a/solution.py
+++ b/solution.py
@@ -650,7 +650,7 @@
     back_next = shifted(back, "section", -1)
 
     scaled = frozen_back(
-        after(core, back, kept, x_in[0]), cot, key_matrix, value_matrix, half, received, gain
+        after(core, back, kept, x_in[0], jobs), cot, key_matrix, value_matrix, half, received, gain
     )
     scaled_next = shifted(scaled, "section", -1)
 
@@ -688,9 +688,6 @@
     scalars = jnp.concatenate([after(core, down_sum, up_pieces), finishing.astype(jnp.int32)])
     new_a, chosen = down_optimizer(
         scalars, adapter_params[0], adapter_second[0], down_sum, column_total[None, :]
-    )
-    input_grad = norm_backward(
-        after(core, chosen), scaled_next, back_next, all_next, gain_next, x_here, rstd, mean
     )
     kv_out = kv_out.reshape(1, tokens, 2, kv)
     up_sum = jnp.sum(up_pieces.astype(F32), axis=0).reshape(rows_local, 2, kv)
@@ -703,6 +700,18 @@
             up_sum / row_count[:, None, None],
         )
     )
+
+    input_grad = norm_backward(
+        after(core, chosen, new_b),
+        scaled_next,
+        back_next,
+        all_next,
+        gain_next,
+        x_here,
+        rstd,
+        mean,
+    )
+
     other = swapped(chosen)
     own = core_index == 0
     checkpoint = jnp.concatenate(

time: 129 us -> 129 us (level)
  no operation moved by 1% of the time
where the time goes in v3:
time: 129 us; the launch traced here: 128 us
  Pallas kernels  46.1 us (36%)
  starting transfers between devices  39.8 us (31%)
  between operations  15.1 us (12%)
  local copies, waits for them, and re-layouts  13.6 us (11%)
  waiting for transfers between devices  8.99 us (7%)
  other arithmetic  4.62 us (4%)
    pallas_call x12, Pallas kernels, call(): pl.pallas_call(body, out_shape=out_shape, grid_spec=pltpu.PrefetchScalarG...  46.1 us
    ppermute x18, starting transfers between devices, shifted(): return lax.ppermute(value, axis, pairs)  18.7 us
    all_to_all x1, starting transfers between devices, local(): down_pieces = lax.all_to_all(down_piece, 'dp', 0, 0, tiled=True)  7.92 us
    all_to_all x1, starting transfers between devices, local(): up = lax.all_to_all(jnp.tile(up, (n_data, 1, 1)), 'dp', 0, 0, tiled=True)  7.77 us
    ppermute x18, waiting for transfers between devices, shifted(): return lax.ppermute(value, axis, pairs)  5.41 us
    all_to_all x1, starting transfers between devices, local(): up_pieces = lax.all_to_all(up_pieces, 'dp', 0, 0, tiled=True)  5.28 us
    unnamed x42, local copies, waits for them, and re-layouts  4.72 us
    slice x1, local copies, waits for them, and re-layouts, local(): x_here[:, index * part:(index + 1) * part]  3.25 us
  transfers between devices with their start and end apart: 22, of which 7 were waited for; matrix products, arithmetic and copies ran while one was open for 9% of the time, Pallas kernels for 36%

profile of v3, /device:TPU:1, one launch (start us, length us, event | category | flops | bytes accessed | tf_op | source)
XLA Modules:
  0.0 128.2 jit_solution(5437943444417731583)
XLA Ops:
  7.2 1.0 convert_reduce_fusion.2
  8.3 1.0 fusion
  9.2 3.4 %collective-permute-start.2 = (bf16[320,256]{1,0:T(8,128)(2,1)S(1)}, bf16[320,256]{1,0:T(8,128)(2,1)S(1)}, u32[]{:S(2)}, u32[]{:S(2)}) collective-permute-start(bf16[320,256]{1,0:T(8,128)(2,1)S(1)} %pad_maximum_fusion), channel_id=1, source_target_pairs={{0,96},{32,0},{64,32},{96,64},{1,97},{33,1},{65,33},{97,65},{2,98}... | collective-permute-start | bytes 491528 | tf_op jit(solution)/shard_map/ppermute | solution.py:36
  12.6 3.3 %fusion.5 = (bf16[256,2048]{1,0:T(8,128)(2,1)}, bf16[256,2048]{1,0:T(8,128)(2,1)}) fusion(bf16[256,4096]{1,0:T(8,128)(2,1)} %bitcast.37), kind=kLoop, calls=%fused_computation.44 | loop fusion | bytes 4194304 | tf_op jit(solution)/shard_map/slice | solution.py:629
  15.9 0.7 slice.38
  16.6 0.6 collective-permute-start.3
  17.2 0.7 tile.2
  17.9 7.8 %all-to-all-start = ((bf16[16,8,1024]{2,1,0:T(8,128)(2,1)}), bf16[16,8,1024]{2,1,0:T(8,128)(2,1)S(1)}, u32[]{:S(2)}, u32[]{:S(2)}) async-start(bf16[16,8,1024]{2,1,0:T(8,128)(2,1)} %tile.2), calls=%async_computation | async-start | bytes 524288 | tf_op jit(solution)/shard_map/all_to_all | solution.py:633
  25.7 0.5 multiply_reduce_fusion
  26.2 2.2 %collective-permute-start.1 = (f32[256,1]{0,1:T(1,128)S(1)}, f32[256,1]{0,1:T(1,128)S(1)}, u32[]{:S(2)}, u32[]{:S(2)}) collective-permute-start(f32[256,1]{0,1:T(1,128)S(1)} %bitcast.68), channel_id=1, source_target_pairs={{0,1},{1,0},{2,3},{3,2},{4,5},{5,4},{6,7},{7,6},{8,9},{9,8},{10,11... | collective-permute-start | bytes 3080 | tf_op jit(solution)/shard_map/ppermute | solution.py:36
  28.4 0.9 copy.27
  29.3 6.6 %shard_map.155 = (bf16[256,2048]{1,0:T(8,128)(2,1)}, bf16[256,2048]{1,0:T(8,128)(2,1)}) custom-call(s32[1]{0:T(128)} %bitcast.core_ref, bf16[256,1024]{1,0:T(8,128)(2,1)} %bitcast.41, bf16[8192,512]{1,0:T(8,128)(2,1)} %bitcast.54, bf16[8192,512]{1,0:T(8,128)(2,1)} %bitcast.58), custom_call_target="tpu_custom_call" | custom-call | flops 134217728 | bytes 1212416 | tf_op jit(solution)/shard_map/pallas_call | solution.py:84
  36.0 0.5 collective-permute-start.5
  37.1 1.5 %shard_map.157 = (bf16[256,2048]{1,0:T(8,128)(2,1)S(1)}, bf16[256,2048]{1,0:T(8,128)(2,1)S(1)}) custom-call(s32[1]{0:T(128)} %bitcast.core_ref, bf16[256,4096]{1,0:T(8,128)(2,1)S(1)} %bitcast.40, f32[256,1]{1,0:T(8,128)S(1)} %rsqrt.3.rstd_ref.rest_0_, f32[1,8192]{1,0:T(1,128)S(1)} %bitcast.49), custom_call_target="tpu_custom_call" | custom-call | flops 65536 | bytes 264256 | tf_op jit(solution)/shard_map/pallas_call | solution.py:84
  38.8 0.4 collective-permute-start
  39.2 2.8 %collective-permute-done = f32[256,256]{1,0:T(8,128)S(1)} collective-permute-done((f32[256,256]{1,0:T(8,128)S(1)}, f32[256,256]{1,0:T(8,128)S(1)}, u32[]{:S(2)}, u32[]{:S(2)}) %collective-permute-start) | collective-permute-done | bytes 262176 | tf_op jit(solution)/shard_map/ppermute | solution.py:36
  42.0 1.2 collective-permute-start.9
  43.2 0.9 collective-permute-start.8
  44.2 1.5 %collective-permute-start.7 = (bf16[256,256]{1,0:T(8,128)(2,1)S(1)}, bf16[256,256]{1,0:T(8,128)(2,1)S(1)}, u32[]{:S(2)}, u32[]{:S(2)}) collective-permute-start(bf16[256,256]{1,0:T(8,128)(2,1)S(1)} %select_convert_fusion.back_ref), channel_id=1, source_target_pairs={{0,96},{32,0},{64,32},{96,64},{1,97},{33,1},{65,33},{97,65},{2,98}... | collective-permute-start | bytes 393224 | tf_op jit(solution)/shard_map/ppermute | solution.py:36
  45.8 7.1 %shard_map.158 = bf16[256,4096]{1,0:T(8,128)(2,1)} custom-call(s32[1]{0:T(128)} %bitcast.core_ref, bf16[256,1024]{1,0:T(8,128)(2,1)} %bitcast.42, bf16[8192,512]{1,0:T(8,128)(2,1)} %bitcast.55, bf16[8192,512]{1,0:T(8,128)(2,1)} %bitcast.59, bf16[256,2048]{1,0:T(8,128)(2,1)} %collective-permute-done.4.rest_0_, ...), custom_call_target="tpu_custom_call" | custom-call | flops 134217728 | bytes 1345536 | tf_op jit(solution)/shard_map/pallas_call | solution.py:84
  53.0 1.7 %shard_map.159 = bf16[16,256,256]{2,1,0:T(8,128)(2,1)S(1)} custom-call(s32[1]{0:T(128)} %bitcast.core_ref, bf16[256,2048]{1,0:T(8,128)(2,1)S(1)} %get-tuple-element.33.kept_ref, bf16[256,2048]{1,0:T(8,128)(2,1)S(1)} %collective-permute-done.6.taken_ref, bf16[256,256]{1,0:T(8,128)(2,1)S(1)} %collective-permute-done.7.back_ref), custom_call_target="tpu_custom_call" | custom-call | flops 33554432 | bytes 270336 | tf_op jit(solution)/shard_map/pallas_call | solution.py:84
  54.6 1.4 %copy-done.2 = bf16[16,256,256]{2,1,0:T(8,128)(2,1)} copy-done((bf16[16,256,256]{2,1,0:T(8,128)(2,1)}, bf16[16,256,256]{2,1,0:T(8,128)(2,1)S(1)}, u32[]{:S(2)}) %copy-start.2) | copy-done | bytes 2097176
  56.0 7.9 %all-to-all-start.1 = ((bf16[16,256,256]{2,1,0:T(8,128)(2,1)}), bf16[16,256,256]{2,1,0:T(8,128)(2,1)S(1)}, u32[]{:S(2)}, u32[]{:S(2)}) async-start(bf16[16,256,256]{2,1,0:T(8,128)(2,1)} %copy-done.2), calls=%async_computation.1 | async-start | bytes 4194304 | tf_op jit(solution)/shard_map/all_to_all | solution.py:658
  64.2 6.5 %shard_map.160 = (f32[256,1024]{1,0:T(8,128)}, f32[256,2]{1,0:T(8,128)}) custom-call(s32[1]{0:T(128)} %bitcast.core_ref, bf16[256,2048]{1,0:T(8,128)(2,1)} %collective-permute-done.3.own_ref, bf16[256,2048]{1,0:T(8,128)(2,1)} %collective-permute-done.8.other_ref, f32[1,8192]{1,0:T(1,128)} %gain_ref.3, bf16[8192,512]{1,0:T(8,128)(2,1)} %bitcast.56, ...), custom_call_target="tpu_custom_call" | custom-call | flops 134217728 | bytes 1247360 | tf_op jit(solution)/shard_map/pallas_call | solution.py:84
  70.8 0.7 collective-permute-start.10
  71.5 4.5 %shard_map.161 = f32[256,256]{1,0:T(8,128)} custom-call(s32[1]{0:T(128)} %bitcast.core_ref, bf16[256,4096]{1,0:T(8,128)(2,1)} %bitcast.38, f32[256,1]{1,0:T(8,128)} %copy-done.4, f32[1,8192]{1,0:T(1,128)} %bitcast.50, bf16[8192,256]{1,0:T(8,128)(2,1)} %all-gather.2.cloned.1.call-done.factors_ref), custom_call_target="tpu_custom_call" | custom-call | flops 33554432 | bytes 411712 | tf_op jit(solution)/shard_map/pallas_call | solution.py:84
  76.1 1.7 %collective-permute-done.11 = f32[256,256]{1,0:T(8,128)S(1)} collective-permute-done((f32[256,256]{1,0:T(8,128)}, f32[256,256]{1,0:T(8,128)S(1)}, u32[]{:S(2)}, u32[]{:S(2)}) %collective-permute-start.11) | collective-permute-done | bytes 262176 | tf_op jit(solution)/shard_map/ppermute | solution.py:36
  77.8 1.0 add_convert_fusion
  78.8 1.8 %collective-permute-start.12 = (bf16[256,256]{1,0:T(8,128)(2,1)S(1)}, bf16[256,256]{1,0:T(8,128)(2,1)S(1)}, u32[]{:S(2)}, u32[]{:S(2)}) collective-permute-start(bf16[256,256]{1,0:T(8,128)(2,1)S(1)} %add_convert_fusion), channel_id=1, source_target_pairs={{0,32},{32,64},{64,96},{96,0},{1,33},{33,65},{65,97},{97,1},{2,34}... | collective-permute-start | bytes 393224 | tf_op jit(solution)/shard_map/ppermute | solution.py:36
  80.6 1.0 copy-done.9
  81.6 7.3 %shard_map.162 = (f32[256,1024]{1,0:T(8,128)}, f32[256,2]{1,0:T(8,128)}) custom-call(s32[1]{0:T(128)} %bitcast.core_ref, bf16[256,2048]{1,0:T(8,128)(2,1)} %collective-permute-done.9.own_ref, bf16[256,2048]{1,0:T(8,128)(2,1)} %copy-done.9, f32[1,8192]{1,0:T(1,128)} %gain_ref.3, bf16[8192,512]{1,0:T(8,128)(2,1)} %bitcast.57, bf16[8192,512]{1,0:T(8,128)(2,1)} %bitcast.61, ...), custom_call_target="tpu_custom_call" | custom-call | flops 134217728 | bytes 1345792 | tf_op jit(solution)/shard_map/pallas_call | solution.py:84
  88.9 0.5 collective-permute-start.13
  89.4 0.8 copy.26.jobs_ref
  90.6 0.6 copy-done.14
  91.3 3.0 %shard_map.163 = (bf16[256,1024]{1,0:T(8,128)(2,1)}, f32[256,1]{1,0:T(8,128)}, bf16[128,1024]{1,0:T(8,128)(2,1)}) custom-call(s32[1]{0:T(128)} %bitcast.core_ref, f32[256,1024]{1,0:T(8,128)} %get-tuple-element.45.frozen_ref, bf16[256,256]{1,0:T(8,128)(2,1)} %copy-done.13, s32[256,1]{1,0:T(8,128)} %copy.26.jobs_ref, bf16[128,1024]{1,0:T(8,128)(2,1)} %bitcast.47, ...), custom_call_target="tpu_custom_call" | custom-call | flops 4194304 | bytes 180608 | tf_op jit(solution)/shard_map/pallas_call | solution.py:84
  94.3 2.2 %all-to-all-done.1.pieces_ref = bf16[16,256,256]{2,1,0:T(8,128)(2,1)S(1)} async-done(((bf16[16,256,256]{2,1,0:T(8,128)(2,1)}), bf16[16,256,256]{2,1,0:T(8,128)(2,1)S(1)}, u32[]{:S(2)}, u32[]{:S(2)}) %all-to-all-start.1) | async-done | bytes 2097184 | tf_op jit(solution)/shard_map/all_to_all | solution.py:658
  96.5 5.3 %all-to-all-start.2 = ((bf16[16,8,1024]{2,1,0:T(8,128)(2,1)}), bf16[16,8,1024]{2,1,0:T(8,128)(2,1)S(1)}, u32[]{:S(2)}, u32[]{:S(2)}) async-start(bf16[16,8,1024]{2,1,0:T(8,128)(2,1)} %bitcast.64), calls=%async_computation.2 | async-start | bytes 524288 | tf_op jit(solution)/shard_map/all_to_all | solution.py:674
  102.0 0.5 shard_map.164
  102.5 2.1 %collective-permute-start.14 = (bf16[256,256]{1,0:T(8,128)(2,1)S(1)}, bf16[256,256]{1,0:T(8,128)(2,1)S(1)}, u32[]{:S(2)}, u32[]{:S(2)}) collective-permute-start(bf16[256,256]{1,0:T(8,128)(2,1)S(1)} %shard_map.164), channel_id=1, source_target_pairs={{0,32},{32,64},{64,96},{96,0},{1,33},{33,65},{65,97},{97,1},{2,34}... | collective-permute-start | bytes 393224 | tf_op jit(solution)/shard_map/ppermute | solution.py:36
  105.4 0.9 collective-permute-start.16
  106.2 2.2 %reshape.140 = bf16[1,256,2,512]{3,2,1,0:T(2,128)(2,1)} reshape(bf16[256,1024]{1,0:T(8,128)(2,1)} %get-tuple-element.47) | data formatting | bytes 1048576 | tf_op jit(solution)/shard_map/reshape | solution.py:692
  108.6 1.3 %all-to-all-done.2 = bf16[16,8,1024]{2,1,0:T(8,128)(2,1)S(1)} async-done(((bf16[16,8,1024]{2,1,0:T(8,128)(2,1)}), bf16[16,8,1024]{2,1,0:T(8,128)(2,1)S(1)}, u32[]{:S(2)}, u32[]{:S(2)}) %all-to-all-start.2) | async-done | bytes 262176 | tf_op jit(solution)/shard_map/all_to_all | solution.py:674
  110.0 1.7 %shard_map.165 = (f32[3,256,256]{2,1,0:T(8,128)}, f32[3,32,256]{2,1,0:T(8,128)S(1)}) custom-call(s32[2]{0:T(128)S(1)} %pad_add_fusion.scalars_ref, f32[2,256,256]{2,1,0:T(8,128)S(1)} %bitcast.48, f32[256,256]{1,0:T(8,128)S(1)} %bitcast.52, bf16[256,256]{1,0:T(8,128)(2,1)S(1)} %collective-permute-done.14.grad_ref, f32[1,256]{1,0:T(1,128)S(1)} %bitcast.53), custom_call_target="tpu_custom_call" | custom-call | flops 81920 | bytes 112704 | tf_op jit(solution)/shard_map/pallas_call | solution.py:84
  111.8 1.5 %collective-permute-start.17 = (f32[3,32,256]{2,1,0:T(8,128)S(1)}, f32[3,32,256]{2,1,0:T(8,128)S(1)}, u32[]{:S(2)}, u32[]{:S(2)}) collective-permute-start(f32[3,32,256]{2,1,0:T(8,128)S(1)} %get-tuple-element.51), channel_id=1, source_target_pairs={{0,1},{1,0},{2,3},{3,2},{4,5},{5,4},{6,7},{7,6},{8,9},{9,8},{10,11... | collective-permute-start | bytes 294920 | tf_op jit(solution)/shard_map/ppermute | solution.py:36
  113.9 0.7 copy-done.12
  114.5 5.4 %shard_map.166 = bf16[256,4096]{1,0:T(8,128)(2,1)} custom-call(s32[1]{0:T(128)} %bitcast.core_ref, bf16[256,4096]{1,0:T(8,128)(2,1)} %collective-permute-done.15.scaled_ref, bf16[256,256]{1,0:T(8,128)(2,1)} %copy-done.7, bf16[8192,256]{1,0:T(8,128)(2,1)} %all-gather.2.cloned.1.call-done.factors_ref, f32[1,8192]{1,0:T(1,128)} %bitcast.51, ...), custom_call_target="tpu_custom_call" | custom-call | flops 33554432 | bytes 665728 | tf_op jit(solution)/shard_map/pallas_call | solution.py:84
  119.9 0.7 fusion.6
  120.6 0.7 maximum_bitcast_fusion
  (82 shorter events, 3.0 us)
Async XLA Ops:
  7.2 64.3 %all-gather.2.cloned.1.call-start = ((), (), s32[]{:S(2)}) async-start(), calls=%async_computation.3 | async-start | bytes 4325376 | tf_op jit(solution)/shard_map/all_gather | solution.py:636
  9.2 6.6 %collective-permute-start.2 = (bf16[320,256]{1,0:T(8,128)(2,1)S(1)}, bf16[320,256]{1,0:T(8,128)(2,1)S(1)}, u32[]{:S(2)}, u32[]{:S(2)}) collective-permute-start(bf16[320,256]{1,0:T(8,128)(2,1)S(1)} %pad_maximum_fusion), channel_id=1, source_target_pairs={{0,96},{32,0},{64,32},{96,64},{1,97},{33,1},{65,33},{97,65},{2,98}... | collective-permute-start | bytes 491528 | tf_op jit(solution)/shard_map/ppermute | solution.py:36
  12.6 4.6 %copy-start.15 = (f32[1,2,8,2,512]{4,3,2,1,0:T(2,128)S(1)}, f32[1,2,8,2,512]{4,3,2,1,0:T(2,128)}, u32[]{:S(2)}) copy-start(f32[1,2,8,2,512]{4,3,2,1,0:T(2,128)} %param.18) | copy-start | bytes 196612
  12.6 13.1 %copy-start = (bf16[1,256,4096]{2,1,0:T(8,128)(2,1)S(1)}, bf16[1,256,4096]{2,1,0:T(8,128)(2,1)}, u32[]{:S(2)}) copy-start(bf16[1,256,4096]{2,1,0:T(8,128)(2,1)} %param.12) | copy-start | bytes 6291460
  15.9 12.5 %copy-start.10 = (bf16[1,256,2,512]{3,2,1,0:T(2,128)(2,1)S(1)}, bf16[1,256,2,512]{3,2,1,0:T(2,128)(2,1)}, u32[]{:S(2)}) copy-start(bf16[1,256,2,512]{3,2,1,0:T(2,128)(2,1)} %param.23) | copy-start | bytes 1572868
  16.6 26.6 %collective-permute-start.3 = (bf16[256,2048]{1,0:T(8,128)(2,1)}, bf16[256,2048]{1,0:T(8,128)(2,1)}, u32[]{:S(2)}, u32[]{:S(2)}) collective-permute-start(bf16[256,2048]{1,0:T(8,128)(2,1)} %get-tuple-element.61), channel_id=1, source_target_pairs={{0,32},{32,64},{64,96},{96,0},{1,33},{33,65},{65,97},{97,1},{2,34}... | collective-permute-start | bytes 3145736 | tf_op jit(solution)/shard_map/ppermute | solution.py:36
  17.9 18.8 %all-to-all-start = ((bf16[16,8,1024]{2,1,0:T(8,128)(2,1)}), bf16[16,8,1024]{2,1,0:T(8,128)(2,1)S(1)}, u32[]{:S(2)}, u32[]{:S(2)}) async-start(bf16[16,8,1024]{2,1,0:T(8,128)(2,1)} %tile.2), calls=%async_computation | async-start | bytes 524288 | tf_op jit(solution)/shard_map/all_to_all | solution.py:633
  26.2 10.3 %collective-permute-start.1 = (f32[256,1]{0,1:T(1,128)S(1)}, f32[256,1]{0,1:T(1,128)S(1)}, u32[]{:S(2)}, u32[]{:S(2)}) collective-permute-start(f32[256,1]{0,1:T(1,128)S(1)} %bitcast.68), channel_id=1, source_target_pairs={{0,1},{1,0},{2,3},{3,2},{4,5},{5,4},{6,7},{7,6},{8,9},{9,8},{10,11... | collective-permute-start | bytes 3080 | tf_op jit(solution)/shard_map/ppermute | solution.py:36
  29.3 7.5 %copy-start.1 = (bf16[32,8,2,512]{3,1,2,0:T(8,128)(2,1)S(1)}, bf16[32,8,2,512]{3,1,2,0:T(8,128)(2,1)}, u32[]{:S(2)}) copy-start(bf16[32,8,2,512]{3,1,2,0:T(8,128)(2,1)} %copy.27) | copy-start | bytes 1572868
  35.9 8.2 %copy-start.17 = (s32[1,256]{1,0:T(1,128)S(1)}, s32[1,256]{1,0:T(1,128)}, u32[]{:S(2)}) copy-start(s32[1,256]{1,0:T(1,128)} %param.20) | copy-start | bytes 3076
  35.9 8.3 %collective-permute-start.4 = (bf16[256,2048]{1,0:T(8,128)(2,1)}, bf16[256,2048]{1,0:T(8,128)(2,1)}, u32[]{:S(2)}, u32[]{:S(2)}) collective-permute-start(bf16[256,2048]{1,0:T(8,128)(2,1)} %get-tuple-element.30), channel_id=1, source_target_pairs={{0,1},{1,0},{2,3},{3,2},{4,5},{5,4},{6,7},{7,6},{8,9},{9,8},{10,11... | collective-permute-start | bytes 3145736 | tf_op jit(solution)/shard_map/ppermute | solution.py:36
  36.0 9.8 %collective-permute-start.5 = (bf16[256,2048]{1,0:T(8,128)(2,1)}, bf16[256,2048]{1,0:T(8,128)(2,1)}, u32[]{:S(2)}, u32[]{:S(2)}) collective-permute-start(bf16[256,2048]{1,0:T(8,128)(2,1)} %get-tuple-element.35), channel_id=1, source_target_pairs={{0,1},{1,0},{2,3},{3,2},{4,5},{5,4},{6,7},{7,6},{8,9},{9,8},{10,11... | collective-permute-start | bytes 3145736 | tf_op jit(solution)/shard_map/ppermute | solution.py:36
  36.7 16.2 %copy-start.4 = (f32[256,1]{1,0:T(8,128)}, f32[256,1]{1,0:T(8,128)S(1)}, u32[]{:S(2)}) copy-start(f32[256,1]{1,0:T(8,128)S(1)} %rsqrt.3.rstd_ref.rest_0_) | copy-start | bytes 3076
  36.7 16.2 %copy-start.6 = (f32[1,1,32,256]{3,1,2,0:T(1,128)}, f32[1,1,32,256]{3,1,2,0:T(1,128)S(1)}, u32[]{:S(2)}) copy-start(f32[1,1,32,256]{3,1,2,0:T(1,128)S(1)} %copy.29) | copy-start | bytes 98308
  36.8 16.1 %copy-start.3 = (bf16[16,8,1024]{2,1,0:T(8,128)(2,1)}, bf16[16,8,1024]{2,1,0:T(8,128)(2,1)S(1)}, u32[]{:S(2)}) copy-start(bf16[16,8,1024]{2,1,0:T(8,128)(2,1)S(1)} %all-to-all-done) | copy-start | bytes 786436
  38.6 14.3 %collective-permute-start.6 = (bf16[256,2048]{1,0:T(8,128)(2,1)S(1)}, bf16[256,2048]{1,0:T(8,128)(2,1)S(1)}, u32[]{:S(2)}, u32[]{:S(2)}) collective-permute-start(bf16[256,2048]{1,0:T(8,128)(2,1)S(1)} %get-tuple-element.37), channel_id=1, source_target_pairs={{0,1},{1,0},{2,3},{3,2},{4,5},{5,4},{6,7},{7,6},{8,9},{9,8},{10,11... | collective-permute-start | bytes 3145736 | tf_op jit(solution)/shard_map/ppermute | solution.py:36
  38.8 3.2 %collective-permute-start = (f32[256,256]{1,0:T(8,128)S(1)}, f32[256,256]{1,0:T(8,128)S(1)}, u32[]{:S(2)}, u32[]{:S(2)}) collective-permute-start(f32[256,256]{1,0:T(8,128)S(1)} %shard_map.156), channel_id=1, source_target_pairs={{0,1},{1,0},{2,3},{3,2},{4,5},{5,4},{6,7},{7,6},{8,9},{9,8},{10,11... | collective-permute-start | bytes 786440 | tf_op jit(solution)/shard_map/ppermute | solution.py:36
  42.0 28.8 %collective-permute-start.9 = (bf16[256,2048]{1,0:T(8,128)(2,1)}, bf16[256,2048]{1,0:T(8,128)(2,1)}, u32[]{:S(2)}, u32[]{:S(2)}) collective-permute-start(bf16[256,2048]{1,0:T(8,128)(2,1)} %get-tuple-element.60), channel_id=1, source_target_pairs={{0,32},{32,64},{64,96},{96,0},{1,33},{33,65},{65,97},{97,1},{2,34}... | collective-permute-start | bytes 3145736 | tf_op jit(solution)/shard_map/ppermute | solution.py:36
  43.2 21.0 %collective-permute-start.8 = (bf16[256,2048]{1,0:T(8,128)(2,1)}, bf16[256,2048]{1,0:T(8,128)(2,1)}, u32[]{:S(2)}, u32[]{:S(2)}) collective-permute-start(bf16[256,2048]{1,0:T(8,128)(2,1)} %collective-permute-done.3.own_ref), channel_id=1, source_target_pairs={{0,1},{1,0},{2,3},{3,2},{4,5},{5,4},{6,7},{7,6},{8,9},{9,8},{10,11... | collective-permute-start | bytes 3145736 | tf_op jit(solution)/shard_map/ppermute | solution.py:36
  44.2 8.7 %copy-start.11 = (bf16[256,256]{1,0:T(8,128)(2,1)}, bf16[256,256]{1,0:T(8,128)(2,1)S(1)}, u32[]{:S(2)}) copy-start(bf16[256,256]{1,0:T(8,128)(2,1)S(1)} %select_convert_fusion.back_ref) | copy-start | bytes 393220
  44.2 8.7 %collective-permute-start.7 = (bf16[256,256]{1,0:T(8,128)(2,1)S(1)}, bf16[256,256]{1,0:T(8,128)(2,1)S(1)}, u32[]{:S(2)}, u32[]{:S(2)}) collective-permute-start(bf16[256,256]{1,0:T(8,128)(2,1)S(1)} %select_convert_fusion.back_ref), channel_id=1, source_target_pairs={{0,96},{32,0},{64,32},{96,64},{1,97},{33,1},{65,33},{97,65},{2,98}... | collective-permute-start | bytes 393224 | tf_op jit(solution)/shard_map/ppermute | solution.py:36
  52.9 1.7 %copy-start.7 = (bf16[256,256]{1,0:T(8,128)(2,1)}, bf16[256,256]{1,0:T(8,128)(2,1)S(1)}, u32[]{:S(2)}) copy-start(bf16[256,256]{1,0:T(8,128)(2,1)S(1)} %collective-permute-done.7.back_ref) | copy-start | bytes 393220
  54.6 1.4 %copy-start.2 = (bf16[16,256,256]{2,1,0:T(8,128)(2,1)}, bf16[16,256,256]{2,1,0:T(8,128)(2,1)S(1)}, u32[]{:S(2)}) copy-start(bf16[16,256,256]{2,1,0:T(8,128)(2,1)S(1)} %shard_map.159) | copy-start | bytes 6291460
  56.0 40.5 %all-to-all-start.1 = ((bf16[16,256,256]{2,1,0:T(8,128)(2,1)}), bf16[16,256,256]{2,1,0:T(8,128)(2,1)S(1)}, u32[]{:S(2)}, u32[]{:S(2)}) async-start(bf16[16,256,256]{2,1,0:T(8,128)(2,1)} %copy-done.2), calls=%async_computation.1 | async-start | bytes 4194304 | tf_op jit(solution)/shard_map/all_to_all | solution.py:658
  64.0 49.6 %collective-permute-start.15 = (bf16[256,4096]{1,0:T(8,128)(2,1)}, bf16[256,4096]{1,0:T(8,128)(2,1)}, u32[]{:S(2)}, u32[]{:S(2)}) collective-permute-start(bf16[256,4096]{1,0:T(8,128)(2,1)} %shard_map.158), channel_id=1, source_target_pairs={{0,96},{32,0},{64,32},{96,64},{1,97},{33,1},{65,33},{97,65},{2,98}... | collective-permute-start | bytes 6291464 | tf_op jit(solution)/shard_map/ppermute | solution.py:36
  70.8 9.8 %collective-permute-start.10 = (bf16[256,2048]{1,0:T(8,128)(2,1)}, bf16[256,2048]{1,0:T(8,128)(2,1)S(1)}, u32[]{:S(2)}, u32[]{:S(2)}) collective-permute-start(bf16[256,2048]{1,0:T(8,128)(2,1)} %collective-permute-done.9.own_ref), channel_id=1, source_target_pairs={{0,1},{1,0},{2,3},{3,2},{4,5},{5,4},{6,7},{7,6},{8,9},{9,8},{10,11... | collective-permute-start | bytes 3145736 | tf_op jit(solution)/shard_map/ppermute | solution.py:36
  76.0 1.8 %collective-permute-start.11 = (f32[256,256]{1,0:T(8,128)}, f32[256,256]{1,0:T(8,128)S(1)}, u32[]{:S(2)}, u32[]{:S(2)}) collective-permute-start(f32[256,256]{1,0:T(8,128)} %shard_map.161), channel_id=1, source_target_pairs={{0,1},{1,0},{2,3},{3,2},{4,5},{5,4},{6,7},{7,6},{8,9},{9,8},{10,11... | collective-permute-start | bytes 786440 | tf_op jit(solution)/shard_map/ppermute | solution.py:36
  78.8 11.8 %collective-permute-start.12 = (bf16[256,256]{1,0:T(8,128)(2,1)S(1)}, bf16[256,256]{1,0:T(8,128)(2,1)S(1)}, u32[]{:S(2)}, u32[]{:S(2)}) collective-permute-start(bf16[256,256]{1,0:T(8,128)(2,1)S(1)} %add_convert_fusion), channel_id=1, source_target_pairs={{0,32},{32,64},{64,96},{96,0},{1,33},{33,65},{65,97},{97,1},{2,34}... | collective-permute-start | bytes 393224 | tf_op jit(solution)/shard_map/ppermute | solution.py:36
  80.6 9.6 %copy-start.18 = (s32[8]{0:T(128)S(1)}, s32[8]{0:T(128)}, u32[]{:S(2)}) copy-start(s32[8]{0:T(128)} %param.21) | copy-start | bytes 100
  80.6 1.0 copy-start.9
  88.9 1.7 %collective-permute-start.13 = (f32[256,2]{1,0:T(8,128)}, f32[256,2]{1,0:T(8,128)S(1)}, u32[]{:S(2)}, u32[]{:S(2)}) collective-permute-start(f32[256,2]{1,0:T(8,128)} %get-tuple-element.46.rest_0_), channel_id=1, source_target_pairs={{0,1},{1,0},{2,3},{3,2},{4,5},{5,4},{6,7},{7,6},{8,9},{9,8},{10,11... | collective-permute-start | bytes 6152 | tf_op jit(solution)/shard_map/ppermute | solution.py:36
  90.6 0.7 copy-start.14
  90.6 0.7 copy-start.13
  94.3 15.7 %copy-start.5 = (f32[1,2,256,256]{3,2,1,0:T(8,128)S(1)}, f32[1,2,256,256]{3,2,1,0:T(8,128)}, u32[]{:S(2)}) copy-start(f32[1,2,256,256]{3,2,1,0:T(8,128)} %param.16) | copy-start | bytes 1572868
  94.3 15.7 %copy-start.8 = (f32[1,256,256]{2,1,0:T(8,128)S(1)}, f32[1,256,256]{2,1,0:T(8,128)}, u32[]{:S(2)}) copy-start(f32[1,256,256]{2,1,0:T(8,128)} %param.17) | copy-start | bytes 786436
  96.5 13.4 %all-to-all-start.2 = ((bf16[16,8,1024]{2,1,0:T(8,128)(2,1)}), bf16[16,8,1024]{2,1,0:T(8,128)(2,1)S(1)}, u32[]{:S(2)}, u32[]{:S(2)}) async-start(bf16[16,8,1024]{2,1,0:T(8,128)(2,1)} %bitcast.64), calls=%async_computation.2 | async-start | bytes 524288 | tf_op jit(solution)/shard_map/all_to_all | solution.py:674
  102.0 11.4 %copy-start.16 = (f32[1,8,2,512]{3,2,1,0:T(2,128)S(1)}, f32[1,8,2,512]{3,2,1,0:T(2,128)}, u32[]{:S(2)}) copy-start(f32[1,8,2,512]{3,2,1,0:T(2,128)} %param.19) | copy-start | bytes 98308
  102.5 6.1 %collective-permute-start.14 = (bf16[256,256]{1,0:T(8,128)(2,1)S(1)}, bf16[256,256]{1,0:T(8,128)(2,1)S(1)}, u32[]{:S(2)}, u32[]{:S(2)}) collective-permute-start(bf16[256,256]{1,0:T(8,128)(2,1)S(1)} %shard_map.164), channel_id=1, source_target_pairs={{0,32},{32,64},{64,96},{96,0},{1,33},{33,65},{65,97},{97,1},{2,34}... | collective-permute-start | bytes 393224 | tf_op jit(solution)/shard_map/ppermute | solution.py:36
  105.4 8.5 %collective-permute-start.16 = (f32[256,1]{1,0:T(8,128)}, f32[256,1]{1,0:T(8,128)S(1)}, u32[]{:S(2)}, u32[]{:S(2)}) collective-permute-start(f32[256,1]{1,0:T(8,128)} %get-tuple-element.53), channel_id=1, source_target_pairs={{0,96},{32,0},{64,32},{96,64},{1,97},{33,1},{65,33},{97,65},{2,98}... | collective-permute-start | bytes 3080 | tf_op jit(solution)/shard_map/ppermute | solution.py:36
  111.8 8.8 %collective-permute-start.17 = (f32[3,32,256]{2,1,0:T(8,128)S(1)}, f32[3,32,256]{2,1,0:T(8,128)S(1)}, u32[]{:S(2)}, u32[]{:S(2)}) collective-permute-start(f32[3,32,256]{2,1,0:T(8,128)S(1)} %get-tuple-element.51), channel_id=1, source_target_pairs={{0,1},{1,0},{2,3},{3,2},{4,5},{5,4},{6,7},{7,6},{8,9},{9,8},{10,11... | collective-permute-start | bytes 294920 | tf_op jit(solution)/shard_map/ppermute | solution.py:36
  113.9 0.7 copy-start.12
Sparse Core Ops, SparseCore 0:
  16.7 50.5 all-gather.1
